TPU v7x, 32 devices: a whole 2x2x4 slice. The times are simulated.
32 devices in a mesh: seq: 8 (over y, x, core), mp: 4 (over z).
Axes of the slice: x: 2, y: 2, z: 4, core: 2. Of those that a mesh axis runs over, the one named last changes fastest.
Arguments:
- tokens: bfloat16 [2, 1024, 2048], P(None, 'seq', 'mp'), may hold values from -6 to 6
- norm_gain: float32 [2048], replicated, may hold values from 0.5 to 1.5
- in_weight: bfloat16 [2, 2048, 4096], P(None, 'seq', 'mp'), may hold values from -0.125 to 0.125
- conv_weight: float32 [4, 4096], P(None, 'mp'), may hold values from -3 to 3
- conv_bias: float32 [4096], P('mp'), may hold values from -3 to 3
- low_weight: bfloat16 [4096, 128], P('mp'), may hold values from -0.09375 to 0.09375
- state_weight: bfloat16 [4096, 32], P('mp'), may hold values from -0.09375 to 0.09375
- delta_weight: bfloat16 [128, 4096], P(None, 'mp'), may hold values from -0.5 to 0.5
- delta_bias: float32 [4096], P('mp'), may hold values from -7 to -2
- skip_gain: float32 [4096], P('mp'), may hold values from 0.5 to 1.5
- out_weight: bfloat16 [4096, 2048], P('mp', 'seq'), may hold values from -0.09375 to 0.09375
- cotangent: float32 [2, 1024, 2048], P(None, 'seq', 'mp'), may hold values from -6 to 6
- seq_group: int32 [2], replicated, may hold values from 0 to 3
- group_weight: float32 [4], replicated, may hold values from 0.25 to 4
Outputs:
- block_out: bfloat16 [2, 1024, 2048], P(None, 'seq', 'mp')
- d_tokens: float32 [2, 1024, 2048], P(None, 'seq', 'mp')
- d_norm_gain: float32 [2048], replicated
- d_in_weight: float32 [2, 2048, 4096], P(None, 'seq', 'mp')
- d_conv_weight: float32 [4, 4096], P(None, 'mp')
- d_conv_bias: float32 [4096], P('mp')
- d_low_weight: float32 [4096, 128], P('mp')
- d_state_weight: float32 [4096, 32], P('mp')
- d_delta_weight: float32 [128, 4096], P(None, 'mp')
- d_delta_bias: float32 [4096], P('mp')
- d_skip_gain: float32 [4096], P('mp')
- d_out_weight: float32 [4096, 2048], P('mp', 'seq')
All inputs are finite; a program needn't handle non-finite values.
Results may differ from a plain program's by a relative error of at most 0.012.
Values may be sent and summed in bfloat16 or wider, within the bound.
A program may use at most 256 MiB of HBM per device.

v0:
```python
import math

import jax
import jax.numpy as jnp
from jax import lax
from jax.sharding import PartitionSpec as P

SEQ_MB = 1
NMB = 2


EPSILON = 1e-05


def from_behind(value, axis, steps):
    count = lax.axis_size(axis)
    leading, last = (max(0, -steps), min(count, count - steps))
    return lax.ppermute(value, axis, [(source, source + steps) for source in range(leading, last)])


def prefix(value, axis, join, neutral, backward):
    count, mine = (lax.axis_size(axis), lax.axis_index(axis))
    pieces = jax.tree.map(lambda part: lax.all_gather(part, axis), value)
    if backward:
        pieces = jax.tree.map(lambda part: part[::-1], pieces)
        mine = count - 1 - mine
    subtotal = jax.tree.map(
        lambda part, zero: jnp.full_like(part, 0) + jnp.asarray(zero, part.dtype), value, neutral
    )

    def lap(position, subtotal):
        longer = join(subtotal, jax.tree.map(lambda part: part[position], pieces))
        return jax.tree.map(lambda new, old: jnp.where(position < mine, new, old), longer, subtotal)

    return lax.fori_loop(0, count - 1, lap, subtotal)


def combine(earlier, later):
    return (earlier[0] * later[0], later[0] * earlier[1] + later[1])


def make_gates(delta_raw, b_state, inputs):
    beta_gate = jax.nn.sigmoid(delta_raw)
    key_sq = jnp.sum(b_state * b_state, axis=-1, keepdims=True)
    step_size = beta_gate / (1.0 + beta_gate * key_sq)
    decays = 1.0 - step_size[:, :, None, :] * (b_state * b_state)[:, :, :, None]
    source = (step_size * inputs)[:, :, None, :] * b_state[:, :, :, None]
    return (decays, source)


def to_blocks(value, span_rows):
    old_shape = value.shape
    reshaped = value.reshape((old_shape[0], old_shape[1] // span_rows, span_rows) + old_shape[2:])
    return jnp.swapaxes(reshaped, 0, 1)


def from_blocks(value):
    joined = jnp.swapaxes(value, 0, 1)
    old_shape = joined.shape
    return joined.reshape((old_shape[0], old_shape[1] * old_shape[2]) + old_shape[3:])


def forward_block(carry_pair, block_items):
    delta_raw, b_state, inputs = block_items
    decays, source = make_gates(delta_raw, b_state, inputs)
    run_prod, run_state = carry_pair
    prod_list = []
    state_list = []
    for row_idx in range(decays.shape[1]):
        run_prod = run_prod * decays[:, row_idx]
        run_state = decays[:, row_idx] * run_state + source[:, row_idx]
        prod_list.append(run_prod)
        state_list.append(run_state)
    return ((run_prod, run_state), (jnp.stack(prod_list, axis=1), jnp.stack(state_list, axis=1)))


def backward_block(carry_trio, block_items):
    delta_raw, b_state, inputs, read_grad, c_state = block_items
    decays, _ = make_gates(delta_raw, b_state, inputs)
    grad_next, dec_next, tail_prod = carry_trio
    span_rows = decays.shape[1]
    grad_list = [None] * span_rows
    tail_list = [None] * span_rows
    for row_idx in reversed(range(span_rows)):
        drive_term = read_grad[:, row_idx][:, None, :] * c_state[:, row_idx][:, :, None]
        grad_next = drive_term + dec_next * grad_next
        tail_prod = dec_next * tail_prod
        grad_list[row_idx] = grad_next
        tail_list[row_idx] = tail_prod
        dec_next = decays[:, row_idx]
    return (
        (grad_next, dec_next, tail_prod),
        (jnp.stack(grad_list, axis=1), jnp.stack(tail_list, axis=1)),
    )


def silu_slope(value):
    sig_value = jax.nn.sigmoid(value)
    return sig_value * (1.0 + value * (1.0 - sig_value))


def local(
    tokens,
    norm_gain,
    in_weight,
    conv_weight,
    conv_bias,
    low_weight,
    state_weight,
    delta_weight,
    delta_bias,
    skip_gain,
    out_weight,
    cotangent,
    seq_group,
    group_weight,
):
    stretch = tokens.shape[1]
    feature_dev = tokens.shape[2]
    channels = in_weight.shape[2]
    model_width = norm_gain.shape[0]
    num_taps = conv_weight.shape[0]
    nstate = state_weight.shape[1] // 2
    span_rows = math.gcd(stretch, 8)
    picks = (
        seq_group[:, None] == jnp.arange(group_weight.shape[0], dtype=jnp.int32)[None, :]
    ).astype(jnp.float32)
    seq_weight = jnp.sum(picks * group_weight[None, :], axis=1)
    feature_start = lax.axis_index("mp") * feature_dev
    ones_state = jnp.ones((SEQ_MB, nstate, channels), jnp.float32)
    zero_state = jnp.zeros_like(ones_state)
    acc_in = jnp.zeros((2, model_width, channels), jnp.float32)
    acc_out = jnp.zeros((channels, model_width), jnp.float32)
    acc_gain = jnp.zeros_like(norm_gain)
    acc_conv = jnp.zeros_like(conv_weight)
    acc_cbias = jnp.zeros_like(conv_bias)
    acc_low = jnp.zeros(low_weight.shape, jnp.float32)
    acc_state = jnp.zeros(state_weight.shape, jnp.float32)
    acc_delta = jnp.zeros(delta_weight.shape, jnp.float32)
    acc_dbias = jnp.zeros_like(delta_bias)
    acc_skip = jnp.zeros_like(skip_gain)
    outputs = []
    input_grads = []
    for micro_idx in range(NMB):
        whole_in, whole_out = (
            lax.all_gather(in_weight, "seq", axis=1, tiled=True),
            lax.all_gather(out_weight, "seq", axis=1, tiled=True),
        )
        first_seq = micro_idx * SEQ_MB
        block_tokens = tokens[first_seq : first_seq + SEQ_MB]
        full_tokens = lax.all_gather(block_tokens, "mp", axis=2, tiled=True).astype(jnp.float32)
        inv_rms = lax.rsqrt(jnp.mean(full_tokens * full_tokens, axis=-1, keepdims=True) + EPSILON)
        normed = (full_tokens * inv_rms * norm_gain).astype(jnp.bfloat16)
        both_parts = jnp.einsum(
            "scd,kdi->ksci", normed, whole_in, preferred_element_type=jnp.float32
        )
        x_round = both_parts[0].astype(jnp.bfloat16)
        z_part = both_parts[1]
        rim_rows = from_behind(x_round[:, stretch - (num_taps - 1) :], "seq", 1)
        padded = jnp.concatenate([rim_rows, x_round], axis=1).astype(jnp.float32)
        conv_sum = conv_bias + jnp.zeros((SEQ_MB, stretch, channels), jnp.float32)
        for tap_index in range(num_taps):
            conv_sum = (
                conv_sum + conv_weight[tap_index] * padded[:, tap_index : tap_index + stretch]
            )
        inputs_round = jax.nn.silu(conv_sum).astype(jnp.bfloat16)
        inputs_f = inputs_round.astype(jnp.float32)
        low_part = jnp.einsum(
            "sci,ir->scr", inputs_round, low_weight, preferred_element_type=jnp.float32
        )
        state_part = jnp.einsum(
            "sci,ir->scr", inputs_round, state_weight, preferred_element_type=jnp.float32
        )
        delta_low, state_proj = lax.psum((low_part, state_part), "mp")
        delta_round = delta_low.astype(jnp.bfloat16)
        delta_raw = (
            jnp.einsum("scr,ri->sci", delta_round, delta_weight, preferred_element_type=jnp.float32)
            + delta_bias
        )
        b_state = state_proj[..., :nstate]
        c_state = state_proj[..., nstate:]
        delta_blocks = to_blocks(delta_raw, span_rows)
        b_blocks = to_blocks(b_state, span_rows)
        c_blocks = to_blocks(c_state, span_rows)
        in_blocks = to_blocks(inputs_f, span_rows)
        stretch_pair, (prod_blocks, local_blocks) = lax.scan(
            forward_block, (ones_state, zero_state), (delta_blocks, b_blocks, in_blocks)
        )
        carried = prefix(stretch_pair, "seq", combine, (ones_state, zero_state), False)
        states = from_blocks(local_blocks) + from_blocks(prod_blocks) * carried[1][:, None]
        before = jnp.concatenate([carried[1][:, None], states[:, :-1]], axis=1)
        read_rec = jnp.einsum("scni,scn->sci", states, c_state)
        read_out = read_rec + skip_gain * inputs_f
        z_gate = jax.nn.silu(z_part)
        gated_round = (read_out * z_gate).astype(jnp.bfloat16)
        out_part = jnp.einsum(
            "sci,id->scd", gated_round, whole_out, preferred_element_type=jnp.float32
        )
        branch = lax.psum_scatter(out_part, "mp", scatter_dimension=2, tiled=True)
        outputs.append((block_tokens.astype(jnp.float32) + branch).astype(jnp.bfloat16))
        d_out = (
            cotangent[first_seq : first_seq + SEQ_MB]
            * seq_weight[first_seq : first_seq + SEQ_MB][:, None, None]
        )
        d_branch = lax.all_gather(d_out.astype(jnp.bfloat16), "mp", axis=2, tiled=True)
        acc_out = acc_out + jnp.einsum(
            "sci,scd->id", gated_round, d_branch, preferred_element_type=jnp.float32
        )
        d_gated = jnp.einsum("scd,id->sci", d_branch, whole_out, preferred_element_type=jnp.float32)
        d_read = d_gated * z_gate
        d_zpart = d_gated * read_out * silu_slope(z_part)
        acc_skip = acc_skip + jnp.sum(d_read * inputs_f, axis=(0, 1))
        read_blocks_grad = to_blocks(d_read, span_rows)
        (last_grad, first_dec, _), (grad_blocks, tail_blocks) = lax.scan(
            backward_block,
            (zero_state, ones_state, ones_state),
            (delta_blocks, b_blocks, in_blocks, read_blocks_grad, c_blocks),
            reverse=True,
        )
        tail_grad = first_dec * last_grad
        crossing = prefix(
            (stretch_pair[0], tail_grad), "seq", combine, (ones_state, zero_state), True
        )
        state_grad = from_blocks(grad_blocks) + from_blocks(tail_blocks) * crossing[1][:, None]
        _, gate_pullback = jax.vjp(make_gates, delta_raw, b_state, inputs_f)
        d_delta, d_bstate, d_inputs_state = gate_pullback((state_grad * before, state_grad))
        d_cstate = jnp.einsum("scni,sci->scn", states, d_read)
        acc_dbias = acc_dbias + jnp.sum(d_delta, axis=(0, 1))
        d_delta_round = d_delta.astype(jnp.bfloat16)
        acc_delta = acc_delta + jnp.einsum(
            "scr,sci->ri", delta_round, d_delta_round, preferred_element_type=jnp.float32
        )
        low_grad_part = jnp.einsum(
            "sci,ri->scr", d_delta_round, delta_weight, preferred_element_type=jnp.float32
        )
        state_grad_part = jnp.concatenate([d_bstate, d_cstate], axis=-1)
        d_low, d_state = lax.psum((low_grad_part, state_grad_part), "mp")
        d_low_round = d_low.astype(jnp.bfloat16)
        d_state_round = d_state.astype(jnp.bfloat16)
        acc_low = acc_low + jnp.einsum(
            "sci,scr->ir", inputs_round, d_low_round, preferred_element_type=jnp.float32
        )
        acc_state = acc_state + jnp.einsum(
            "sci,scr->ir", inputs_round, d_state_round, preferred_element_type=jnp.float32
        )
        d_inputs = d_read * skip_gain + d_inputs_state
        d_inputs = d_inputs + jnp.einsum(
            "scr,ir->sci", d_low_round, low_weight, preferred_element_type=jnp.float32
        )
        d_inputs = d_inputs + jnp.einsum(
            "scr,ir->sci", d_state_round, state_weight, preferred_element_type=jnp.float32
        )
        d_conv = d_inputs * silu_slope(conv_sum)
        acc_cbias = acc_cbias + jnp.sum(d_conv, axis=(0, 1))
        tap_grads = []
        d_padded = jnp.zeros((SEQ_MB, stretch + num_taps - 1, channels), jnp.float32)
        for tap_index in range(num_taps):
            tap_grads.append(
                jnp.sum(d_conv * padded[:, tap_index : tap_index + stretch], axis=(0, 1))
            )
            d_padded = d_padded + jnp.pad(
                conv_weight[tap_index] * d_conv,
                ((0, 0), (tap_index, num_taps - 1 - tap_index), (0, 0)),
            )
        acc_conv = acc_conv + jnp.stack(tap_grads)
        back_rim = from_behind(d_padded[:, : num_taps - 1], "seq", -1)
        d_xpart = d_padded[:, num_taps - 1 :] + jnp.pad(
            back_rim, ((0, 0), (stretch - (num_taps - 1), 0), (0, 0))
        )
        d_parts_round = jnp.stack([d_xpart, d_zpart]).astype(jnp.bfloat16)
        acc_in = acc_in + jnp.einsum(
            "scd,ksci->kdi", normed, d_parts_round, preferred_element_type=jnp.float32
        )
        norm_part = jnp.einsum(
            "ksci,kdi->scd", d_parts_round, whole_in, preferred_element_type=jnp.float32
        )
        d_normed = lax.psum(norm_part, "mp")
        acc_gain = acc_gain + jnp.sum(d_normed * full_tokens * inv_rms, axis=(0, 1))
        scaled = d_normed * norm_gain
        d_full = inv_rms * scaled - full_tokens * (inv_rms * inv_rms * inv_rms) * jnp.mean(
            scaled * full_tokens, axis=-1, keepdims=True
        )
        d_mine = lax.dynamic_slice_in_dim(d_full, feature_start, feature_dev, 2)
        input_grads.append(d_out + d_mine)
    d_in_weight, d_out_weight = (
        lax.psum_scatter(acc_in, "seq", scatter_dimension=1, tiled=True),
        lax.psum_scatter(acc_out, "seq", scatter_dimension=1, tiled=True),
    )
    summed = lax.psum(
        (acc_gain, acc_conv, acc_cbias, acc_low, acc_state, acc_delta, acc_dbias, acc_skip), "seq"
    )
    return (
        jnp.concatenate(outputs, axis=0),
        jnp.concatenate(input_grads, axis=0),
        summed[0],
        d_in_weight,
        summed[1],
        summed[2],
        summed[3],
        summed[4],
        summed[5],
        summed[6],
        summed[7],
        d_out_weight,
    )


def solution(mesh):
    placed = (
        P(None, "seq", "mp"),
        P(),
        P(None, "seq", "mp"),
        P(None, "mp"),
        P("mp"),
        P("mp", None),
        P("mp", None),
        P(None, "mp"),
        P("mp"),
        P("mp"),
        P("mp", "seq"),
        P(None, "seq", "mp"),
        P(),
        P(),
    )
    return jax.shard_map(
        local,
        mesh=mesh,
        in_specs=placed,
        out_specs=(
            P(None, "seq", "mp"),
            P(None, "seq", "mp"),
            P(),
            P(None, "seq", "mp"),
            P(None, "mp"),
            P("mp"),
            P("mp", None),
            P("mp", None),
            P(None, "mp"),
            P("mp"),
            P("mp"),
            P("mp", "seq"),
        ),
        check_vma=False,
    )
```

profile of v0, /device:TPU:0, one launch (start us, length us, event | category | flops | bytes accessed | tf_op | source)
XLA Modules:
  0.0 990.6 jit_solution(17291108296898301011)
XLA Ops:
  11.3 17.4 %all_gather.60 = bf16[1,128,2048]{2,1,0:T(8,128)(2,1)S(1)} all-gather(bf16[1,128,512]{2,1,0:T(8,128)(2,1)S(1)} %get-tuple-element.1679), channel_id=1, replica_groups=mesh['seq'=8,'mp'=4] {'mp'}, dimensions={2}, use_global_device_ids=true | all-gather | bytes 655360 | tf_op jit(solution)/shard_map/all_gather | solution.py:151
  28.8 16.3 %all_gather.67 = bf16[1,128,2048]{2,1,0:T(8,128)(2,1)S(1)} all-gather(bf16[1,128,512]{2,1,0:T(8,128)(2,1)S(1)} %get-tuple-element.1680), channel_id=1, replica_groups=mesh['seq'=8,'mp'=4] {'mp'}, dimensions={2}, use_global_device_ids=true | all-gather | bytes 655360 | tf_op jit(solution)/shard_map/all_gather | solution.py:151
  47.7 16.3 %all_gather.75 = bf16[1,128,2048]{2,1,0:T(8,128)(2,1)S(1)} all-gather(bf16[1,128,512]{2,1,0:T(8,128)(2,1)S(1)} %get-tuple-element.1673), channel_id=1, replica_groups=mesh['seq'=8,'mp'=4] {'mp'}, dimensions={2}, use_global_device_ids=true | all-gather | bytes 655360 | tf_op jit(solution)/shard_map/all_gather | solution.py:205
  63.9 15.6 %all_gather.72 = bf16[1,128,2048]{2,1,0:T(8,128)(2,1)} all-gather(bf16[1,128,512]{2,1,0:T(8,128)(2,1)S(1)} %get-tuple-element.1672), channel_id=1, replica_groups=mesh['seq'=8,'mp'=4] {'mp'}, dimensions={2}, use_global_device_ids=true | all-gather | bytes 655360 | tf_op jit(solution)/shard_map/all_gather | solution.py:205
  81.7 4.8 fusion.168
  94.7 11.7 %all-gather.11.cloned.1.call-done = bf16[1024,2048]{1,0:T(8,128)(2,1)} async-done(((bf16[1024,256]{1,0:T(8,128)(2,1)}), bf16[1024,2048]{1,0:T(8,128)(2,1)}) %all-gather.11.cloned.1.call-update) | async-done | bytes 4194320 | tf_op jit(solution)/shard_map/all_gather | solution.py:147
  106.4 4.9 fusion.97
  111.3 4.7 fusion.110
  118.8 22.0 %all-reduce.23 = (bf16[1,128,128]{2,1,0:T(8,128)(2,1)S(1)}, f32[1,128,32]{1,2,0:T(8,128)S(1)}, bf16[1,128,128]{2,1,0:T(8,128)(2,1)S(1)}, f32[1,128,32]{1,2,0:T(8,128)S(1)}) all-reduce(f32[1,128,128]{2,1,0:T(8,128)S(1)} %convolution_bitcast_fusion.7, ...), channel_id=1, replica_groups=mesh['seq'=8,'mp'=4] {'mp'}, use_global_device_ids=true, to_apply=%region_10.11 | all-reduce | flops 40960 | bytes 262144 | tf_op jit(solution)/shard_map/psum | solution.py:174
  145.6 4.4 broadcast.1522.clone
  149.9 4.3 broadcast.1522.clone.1
  154.3 40.9 %while.138 = (s32[]{:T(128)}, f32[1,16,1024]{2,1,0:T(8,128)S(1)}, f32[1,16,1024]{2,1,0:T(8,128)S(1)}, f32[16,1,8,16,1024]{4,3,2,1,0:T(8,128)}, f32[16,1,8,16,102...) while((s32[]{:T(128)}, f32[1,16,1024]{2,1,0:T(8,128)S(1)}, ...), condition=%wide.region_14.15_spmd.clone, body=%wide.region_12.14_spmd.clone.sunk | while | flops 1065337 | bytes 7736520 | solution.py:186
  195.2 9.8 all-gather.2
  205.0 10.3 %all-gather.3 = f32[8,16,1024]{2,1,0:T(8,128)} all-gather(f32[1,16,1024]{2,1,0:T(8,128)S(1)} %get-tuple-element.888), channel_id=5, replica_groups=mesh['seq'=8,'mp'=4] {'seq'}, dimensions={0}, use_global_device_ids=true | all-gather | bytes 589824 | tf_op jit(solution)/shard_map/all_gather | solution.py:23
  216.1 6.3 while.139
  223.9 4.4 broadcast.1522.clone.2
  232.6 66.5 %while.142 = (s32[]{:T(128)}, f32[1,16,1024]{2,1,0:T(8,128)S(1)}, f32[1,16,1024]{2,1,0:T(8,128)S(1)}, f32[1,16,1024]{2,1,0:T(8,128)S(1)}, f32[16,1,8,16,1024]{4,...) while((s32[]{:T(128)}, f32[1,16,1024]{2,1,0:T(8,128)S(1)}, ...), condition=%wide.region_37.38_spmd.clone, body=%wide.region_35.37_spmd.clone.sunk | while | flops 1106170 | bytes 7096048 | solution.py:214
  299.1 9.8 all-gather.5
  309.0 6.3 while.143
  317.3 4.4 broadcast.1522.clone.4
  321.6 4.3 broadcast.1522.clone.5
  326.0 41.0 %while.136 = (s32[]{:T(128)}, f32[1,16,1024]{2,1,0:T(8,128)S(1)}, f32[1,16,1024]{2,1,0:T(8,128)S(1)}, f32[16,1,8,16,1024]{4,3,2,1,0:T(8,128)}, f32[16,1,8,16,102...) while((s32[]{:T(128)}, f32[1,16,1024]{2,1,0:T(8,128)S(1)}, ...), condition=%wide.region_5.6_spmd.clone, body=%wide.region_3.0_spmd.clone.sunk | while | flops 1065337 | bytes 7736520 | solution.py:186
  367.0 9.0 all-gather
  376.0 10.7 %all-gather.1 = f32[8,16,1024]{2,1,0:T(8,128)} all-gather(f32[1,16,1024]{2,1,0:T(8,128)S(1)} %get-tuple-element.883), channel_id=3, replica_groups=mesh['seq'=8,'mp'=4] {'seq'}, dimensions={0}, use_global_device_ids=true | all-gather | bytes 589824 | tf_op jit(solution)/shard_map/all_gather | solution.py:23
  387.5 6.3 while.137
  396.1 8.1 fusion.66
  404.2 13.5 %slice_add_fusion = f32[1,127,16,1024]{3,2,1,0:T(8,128)} fusion(f32[1,128,16,1024]{3,2,1,0:T(8,128)} %bitcast.1458, f32[1,128,16,1024]{3,2,1,0:T(8,128)} %bitcast.1457, f32[16,1024]{1,0:T(8,128)S(1)} %bitcast.1473), kind=kLoop, calls=%fused_computation.277 | loop fusion | flops 4161536 | bytes 25034752 | tf_op jit(solution)/shard_map/add | solution.py:190
  417.7 8.3 pad_maximum_fusion.1
  427.6 8.1 fusion.67
  436.6 13.1 %multiply_reduce_fusion.2 = (f32[16,8,16]{2,1,0:T(8,128)S(1)}, f32[16,8,1024]{2,1,0:T(8,128)S(1)}, f32[16,8,16]{2,1,0:T(8,128)}, f32[16,8,1024]{2,1,0:T(8,128)S(1)}) fusion(f32[16,8,1024]{2,1,0:T(8,128)} %fusion.204, f32[16,1,8,16,1024]{4,3,2,1,0:T(8,128)} %bitcast.1461, f32[16,8,16]{2,1,0:T(8,128)S(1)} %bitcast.1515, f32[16,8,1024]{2,1,0:T(8,128)} %fusion.84, ...), kind=kLoop, calls=%fused_computation.265 | loop fusion | flops 24899584 | bytes 27361280 | tf_op jit(solution)/shard_map/transpose(jvp())/reduce_sum | solution.py:46
  449.8 4.3 fusion.85
  461.7 4.4 broadcast.1522.clone.6
  466.1 4.4 broadcast.1522.clone.7
  470.5 57.1 %while.140 = (s32[]{:T(128)}, f32[1,16,1024]{2,1,0:T(8,128)S(1)}, f32[1,16,1024]{2,1,0:T(8,128)S(1)}, f32[1,16,1024]{2,1,0:T(8,128)S(1)}, f32[16,1,8,16,1024]{4,...) while((s32[]{:T(128)}, f32[1,16,1024]{2,1,0:T(8,128)S(1)}, ...), condition=%wide.region_22.23_spmd.clone, body=%wide.region_20.22_spmd.clone.sunk | while | flops 1106170 | bytes 7096048 | solution.py:214
  527.6 9.0 all-gather.4
  536.6 6.5 while.141
  543.1 12.0 %slice_add_fusion.1 = f32[1,127,16,1024]{3,2,1,0:T(8,128)} fusion(f32[1,128,16,1024]{3,2,1,0:T(8,128)} %bitcast.1460, f32[1,128,16,1024]{3,2,1,0:T(8,128)} %bitcast.1459, f32[16,1024]{1,0:T(8,128)S(1)} %bitcast.1470), kind=kLoop, calls=%fused_computation.279 | loop fusion | flops 4161536 | bytes 25034752 | tf_op jit(solution)/shard_map/add | solution.py:190
  559.4 10.7 %multiply_reduce_fusion.6 = (f32[16,8,16]{2,1,0:T(8,128)}, f32[16,8,1024]{2,1,0:T(8,128)}, f32[16,8,16]{2,1,0:T(8,128)}, f32[16,8,1024]{2,1,0:T(8,128)}) fusion(f32[16,8,1024]{2,1,0:T(8,128)} %fusion.203, f32[16,1,8,16,1024]{4,3,2,1,0:T(8,128)S(1)} %bitcast.1462, f32[16,8,16]{2,1,0:T(8,128)} %bitcast.1516, f32[16,8,1024]{2,1,0:T(8,128)} %get-tuple-element.1699, ...), kind=kLoop, calls=%fused_computation.271 | loop fusion | flops 24899584 | bytes 27361280 | tf_op jit(solution)/shard_map/transpose(jvp())/reduce_sum | solution.py:46
  579.6 19.7 %all-reduce.24 = (bf16[1,128,128]{2,1,0:T(8,128)(2,1)S(1)}, bf16[1,128,32]{1,2,0:T(8,128)(2,1)S(1)}, bf16[1,128,128]{2,1,0:T(8,128)(2,1)S(1)}, bf16[1,128,32]{1,2,0:T(8,128)(2,1)S(1)}) all-reduce(f32[1,128,128]{2,1,0:T(8,128)} %convolution_bitcast_fusion.5, ...), channel_id=1, replica_groups=mesh['seq'=8,'mp'=4] {'mp'}, use_global_device_ids=true, to_apply=%region_42.43 | all-reduce | flops 40960 | bytes 245760 | tf_op jit(solution)/shard_map/psum | solution.py:237
  614.6 7.5 convolution_bitcast_fusion
  628.6 8.3 add_bitcast_fusion
  640.6 5.6 fusion.111
  646.6 8.2 convolution_add_fusion
  659.1 63.0 %all-reduce.22.cloned.1.call-done = (f32[1,128,2048]{2,1,0:T(8,128)}, f32[1,128,2048]{2,1,0:T(8,128)}) async-done(((f32[1,128,2048]{2,1,0:T(8,128)}, f32[1,128,2048]{2,1,0:T(8,128)}), (f32[1,128,2048]{2,1,0:T(8,128)}, f32[1,128,2048]{2,1,0:T(8,128)})) %all-reduce.22.cloned.1.call-update) | async-done | bytes 2097168 | tf_op jit(solution)/shard_map/psum | solution.py:277
  725.0 24.9 %all-reduce.10 = (f32[2048]{0:T(1024)}, f32[4,1024]{1,0:T(4,128)}, f32[1024]{0:T(1024)}, f32[1024]{0:T(1024)}, f32[1024]{0:T(1024)}) all-reduce(f32[2048]{0:T(1024)S(1)} %add.917, f32[4,1024]{1,0:T(4,128)S(1)} %maximum_add_fusion, f32[1024]{0:T(1024)S(1)} %add.921, f32[1024]{0:T(1024)S(1)} %add.925, ...), channel_id=1, replica_groups=mesh['seq'=8,'mp'=4] {'seq'}, use_global_device_ids=true, to_apply=%region_51.52 | all-reduce | flops 9216 | bytes 73728 | tf_op jit(solution)/shard_map/psum | solution.py:289
  753.4 87.5 %reduce-scatter.9.cloned.1.call-done = f32[2,256,1024]{1,2,0:T(8,128)} async-done(((f32[2,2048,1024]{1,2,0:T(8,128)}), f32[2,256,1024]{1,2,0:T(8,128)}) %reduce-scatter.9.cloned.1.call-update) | async-done | bytes 2097168 | tf_op jit(solution)/shard_map/reduce_scatter | solution.py:286
  843.8 59.5 %all-reduce.20.cloned.1.call-done = (f32[1024,128]{1,0:T(8,128)}, f32[1024,32]{0,1:T(8,128)}, f32[128,1024]{1,0:T(8,128)}) async-done(((f32[1024,128]{1,0:T(8,128)}, f32[1024,32]{0,1:T(8,128)}, f32[128,1024]{1,0:T(8,128)}), (f32[1024,128]{1,0:T(8,128)}, f32[1024,32]{0,1:T(8,128)}, f32[128,1024]{1,0:T(8,128)})) %all-reduce.20.cloned.1.call-update) | async-done | bytes 1179664 | tf_op jit(solution)/shard_map/psum | solution.py:289
  903.3 74.7 %reduce-scatter.11.cloned.1.call-done = f32[1024,256]{1,0:T(8,128)} async-done(((f32[1024,2048]{1,0:T(8,128)}), f32[1024,256]{1,0:T(8,128)}) %reduce-scatter.11.cloned.1.call-update) | async-done | bytes 1048592 | tf_op jit(solution)/shard_map/reduce_scatter | solution.py:287
  (1484 shorter events, 329.0 us)
Async XLA Ops:
  7.2 133.6 %copy-start = (bf16[128,1024]{1,0:T(8,128)(2,1)S(1)}, bf16[128,1024]{1,0:T(8,128)(2,1)}, u32[]{:S(2)}) copy-start(bf16[128,1024]{1,0:T(8,128)(2,1)} %param.37) | copy-start | bytes 786436
  7.2 74.5 %all-gather.9.cloned.1.call-start = ((), (), s32[]{:S(2)}) async-start(), calls=%async_computation.4 | async-start | bytes 9437184 | tf_op jit(solution)/shard_map/all_gather | solution.py:146
  7.9 98.5 %all-gather.11.cloned.1.call-start = ((), (), s32[]{:S(2)}) async-start(), calls=%async_computation.5 | async-start | bytes 4718592 | tf_op jit(solution)/shard_map/all_gather | solution.py:147
  8.7 648.5 %reduce-scatter.5.cloned.1.call-start = ((), (), s32[]{:S(2)}) async-start(), calls=%async_computation.6 | async-start | bytes 1310720 | tf_op jit(solution)/shard_map/reduce_scatter | solution.py:199
  28.7 57.9 %copy-start.2 = (bf16[1,128,2048]{2,1,0:T(8,128)(2,1)}, bf16[1,128,2048]{2,1,0:T(8,128)(2,1)S(1)}, u32[]{:S(2)}) copy-start(bf16[1,128,2048]{2,1,0:T(8,128)(2,1)S(1)} %all_gather.60) | copy-start | bytes 1572868
  45.1 42.8 %copy-start.4 = (bf16[1,128,2048]{2,1,0:T(8,128)(2,1)}, bf16[1,128,2048]{2,1,0:T(8,128)(2,1)S(1)}, u32[]{:S(2)}) copy-start(bf16[1,128,2048]{2,1,0:T(8,128)(2,1)S(1)} %all_gather.67) | copy-start | bytes 1572868
  63.9 42.5 %copy-start.35 = (bf16[1,128,2048]{2,1,0:T(8,128)(2,1)}, bf16[1,128,2048]{2,1,0:T(8,128)(2,1)S(1)}, u32[]{:S(2)}) copy-start(bf16[1,128,2048]{2,1,0:T(8,128)(2,1)S(1)} %all_gather.75) | copy-start | bytes 1572868
  81.6 34.7 %copy-start.72 = (f32[1,1024]{1,0:T(1,128)}, f32[1,1024]{1,0:T(1,128)S(1)}, u32[]{:S(2)}) copy-start(f32[1,1024]{1,0:T(1,128)S(1)} %get-tuple-element.1692) | copy-start | bytes 12292
  81.6 34.7 %copy-start.74 = (f32[1,1024]{1,0:T(1,128)}, f32[1,1024]{1,0:T(1,128)S(1)}, u32[]{:S(2)}) copy-start(f32[1,1024]{1,0:T(1,128)S(1)} %get-tuple-element.1693) | copy-start | bytes 12292
  81.6 34.7 %copy-start.76 = (f32[1,1024]{1,0:T(1,128)}, f32[1,1024]{1,0:T(1,128)S(1)}, u32[]{:S(2)}) copy-start(f32[1,1024]{1,0:T(1,128)S(1)} %get-tuple-element.1694) | copy-start | bytes 12292
  81.6 34.7 %copy-start.78 = (f32[1,1024]{1,0:T(1,128)}, f32[1,1024]{1,0:T(1,128)S(1)}, u32[]{:S(2)}) copy-start(f32[1,1024]{1,0:T(1,128)S(1)} %get-tuple-element.1695) | copy-start | bytes 12292
  86.5 24.8 %copy-start.13 = (f32[128,2,1024]{2,0,1:T(8,128)}, f32[128,2,1024]{2,0,1:T(8,128)S(1)}, u32[]{:S(2)}) copy-start(f32[128,2,1024]{2,0,1:T(8,128)S(1)} %fusion.168) | copy-start | bytes 3145732
  86.6 29.4 %collective-permute-start = (bf16[1,3,1024]{2,1,0:T(4,128)(2,1)S(1)}, bf16[1,3,1024]{2,1,0:T(4,128)(2,1)S(1)}, u32[]{:S(2)}, u32[]{:S(2)}) collective-permute-start(bf16[1,3,1024]{2,1,0:T(4,128)(2,1)S(1)} %slice.845), channel_id=1, source_target_pairs={{0,4},{4,8},{8,12},{12,16},{16,20},{20,24},{24,28},{1,5},{5,9},{9,... | collective-permute-start | bytes 18440 | tf_op jit(solution)/shard_map/ppermute | solution.py:18
  88.0 23.3 %copy-start.36 = (bf16[1,128,2048]{2,1,0:T(8,128)(2,1)S(1)}, bf16[1,128,2048]{2,1,0:T(8,128)(2,1)}, u32[]{:S(2)}) copy-start(bf16[1,128,2048]{2,1,0:T(8,128)(2,1)} %all_gather.72) | copy-start | bytes 1572868
  90.3 26.0 %copy-start.92 = (f32[1024]{0:T(1024)S(1)}, f32[1024]{0:T(1024)}, u32[]{:S(2)}) copy-start(f32[1024]{0:T(1024)} %param.34) | copy-start | bytes 12292
  90.4 25.7 %copy-start.43 = (bf16[1,128,1024]{2,1,0:T(8,128)(2,1)S(1)}, bf16[1,128,1024]{2,1,0:T(8,128)(2,1)}, u32[]{:S(2)}) copy-start(bf16[1,128,1024]{2,1,0:T(8,128)(2,1)} %copy-done.42) | copy-start | bytes 786436
  90.4 25.7 %collective-permute-start.1 = (bf16[1,3,1024]{2,1,0:T(4,128)(2,1)S(1)}, bf16[1,3,1024]{2,1,0:T(4,128)(2,1)S(1)}, u32[]{:S(2)}, u32[]{:S(2)}) collective-permute-start(bf16[1,3,1024]{2,1,0:T(4,128)(2,1)S(1)} %slice.854), channel_id=1, source_target_pairs={{0,4},{4,8},{8,12},{12,16},{16,20},{20,24},{24,28},{1,5},{5,9},{9,... | collective-permute-start | bytes 18440 | tf_op jit(solution)/shard_map/ppermute | solution.py:18
  116.1 24.8 %copy-start.68 = (f32[1024]{0:T(1024)S(1)}, f32[1024]{0:T(1024)}, u32[]{:S(2)}) copy-start(f32[1024]{0:T(1024)} %param.38) | copy-start | bytes 12292
  140.8 13.5 %copy-start.61 = (bf16[1,128,128]{2,1,0:T(8,128)(2,1)}, bf16[1,128,128]{2,1,0:T(8,128)(2,1)S(1)}, u32[]{:S(2)}) copy-start(bf16[1,128,128]{2,1,0:T(8,128)(2,1)S(1)} %get-tuple-element.1494) | copy-start | bytes 98308
  140.8 13.5 %copy-start.63 = (f32[1,128,32]{1,2,0:T(8,128)}, f32[1,128,32]{1,2,0:T(8,128)S(1)}, u32[]{:S(2)}) copy-start(f32[1,128,32]{1,2,0:T(8,128)S(1)} %get-tuple-element.1497) | copy-start | bytes 49156
  140.8 13.5 %copy-start.86 = (f32[128]{0:T(128)}, f32[128]{0:T(128)S(1)}, u32[]{:S(2)}) copy-start(f32[128]{0:T(128)S(1)} %get-tuple-element.1689) | copy-start | bytes 1540
  154.3 61.8 %copy-start.16 = (f32[1,16,1024]{2,1,0:T(8,128)S(1)}, f32[1,16,1024]{2,1,0:T(8,128)}, u32[]{:S(2)}) copy-start(f32[1,16,1024]{2,1,0:T(8,128)} %custom-call.5) | copy-start | bytes 196612
  195.2 37.4 %copy-start.51 = (f32[16,1,8,16]{3,2,1,0:T(8,128)}, f32[16,1,8,16]{3,2,1,0:T(8,128)S(1)}, u32[]{:S(2)}) copy-start(f32[16,1,8,16]{3,2,1,0:T(8,128)S(1)} %get-tuple-element.2623) | copy-start | bytes 24580
  232.6 76.4 %copy-start.25 = (f32[1,16,1024]{2,1,0:T(8,128)S(1)}, f32[1,16,1024]{2,1,0:T(8,128)}, u32[]{:S(2)}) copy-start(f32[1,16,1024]{2,1,0:T(8,128)} %custom-call.11) | copy-start | bytes 196612
  232.6 82.7 %copy-start.81 = (bf16[128,16,1]{0,1,2:T(8,128)(2,1)S(1)}, bf16[128,16,1]{0,1,2:T(8,128)(2,1)}, u32[]{:S(2)}) copy-start(bf16[128,16,1]{0,1,2:T(8,128)(2,1)} %slice_bitcast_fusion.64) | copy-start | bytes 12292
  232.6 82.9 %copy-start.69 = (f32[1024]{0:T(1024)S(1)}, f32[1024]{0:T(1024)}, u32[]{:S(2)}) copy-start(f32[1024]{0:T(1024)} %param.38) | copy-start | bytes 12292
  299.1 26.8 %copy-start.11 = (f32[16,1,8,1024]{3,2,1,0:T(8,128)}, f32[16,1,8,1024]{3,2,1,0:T(8,128)S(1)}, u32[]{:S(2)}) copy-start(f32[16,1,8,1024]{3,2,1,0:T(8,128)S(1)} %get-tuple-element.2604) | copy-start | bytes 1572868
  326.0 61.6 %copy-start.15 = (f32[1,16,1024]{2,1,0:T(8,128)S(1)}, f32[1,16,1024]{2,1,0:T(8,128)}, u32[]{:S(2)}) copy-start(f32[1,16,1024]{2,1,0:T(8,128)} %custom-call.2) | copy-start | bytes 196612
  326.0 67.9 %copy-start.80 = (bf16[128,16,1]{0,1,2:T(8,128)(2,1)S(1)}, bf16[128,16,1]{0,1,2:T(8,128)(2,1)}, u32[]{:S(2)}) copy-start(bf16[128,16,1]{0,1,2:T(8,128)(2,1)} %slice_bitcast_fusion.65) | copy-start | bytes 12292
  326.0 68.0 %copy-start.84 = (f32[128]{0:T(128)S(1)}, f32[128]{0:T(128)}, u32[]{:S(2)}) copy-start(f32[128]{0:T(128)} %get-tuple-element.1685) | copy-start | bytes 1540
  404.2 21.8 %copy-start.8 = (bf16[128,16,1024]{2,1,0:T(8,128)(2,1)}, bf16[128,16,1024]{2,1,0:T(8,128)(2,1)S(1)}, u32[]{:S(2)}) copy-start(bf16[128,16,1024]{2,1,0:T(8,128)(2,1)S(1)} %fusion.66) | copy-start | bytes 12582916
  435.7 14.0 %copy-start.6 = (bf16[128,16,1024]{2,1,0:T(8,128)(2,1)}, bf16[128,16,1024]{2,1,0:T(8,128)(2,1)S(1)}, u32[]{:S(2)}) copy-start(bf16[128,16,1024]{2,1,0:T(8,128)(2,1)S(1)} %fusion.67) | copy-start | bytes 12582916
  436.5 13.2 %copy-start.12 = (f32[16,1,8,1024]{3,2,1,0:T(8,128)S(1)}, f32[16,1,8,1024]{3,2,1,0:T(8,128)}, u32[]{:S(2)}) copy-start(f32[16,1,8,1024]{3,2,1,0:T(8,128)} %copy-done.11) | copy-start | bytes 1572868
  455.9 201.3 %reduce-scatter.7.cloned.1.call-start = ((), (), s32[]{:S(2)}) async-start(), calls=%async_computation.7 | async-start | bytes 1310720 | tf_op jit(solution)/shard_map/reduce_scatter | solution.py:199
  470.5 66.1 %copy-start.24 = (f32[1,16,1024]{2,1,0:T(8,128)S(1)}, f32[1,16,1024]{2,1,0:T(8,128)}, u32[]{:S(2)}) copy-start(f32[1,16,1024]{2,1,0:T(8,128)} %custom-call.8) | copy-start | bytes 196612
  559.4 15.2 %copy-start.7 = (bf16[128,16,1024]{2,1,0:T(8,128)(2,1)S(1)}, bf16[128,16,1024]{2,1,0:T(8,128)(2,1)}, u32[]{:S(2)}) copy-start(bf16[128,16,1024]{2,1,0:T(8,128)(2,1)} %copy-done.6) | copy-start | bytes 12582916
  577.8 27.0 %copy-start.45 = (bf16[1024,128]{1,0:T(8,128)(2,1)S(1)}, bf16[1024,128]{1,0:T(8,128)(2,1)}, u32[]{:S(2)}) copy-start(bf16[1024,128]{1,0:T(8,128)(2,1)} %param.35) | copy-start | bytes 786436
  577.8 27.0 %copy-start.85 = (f32[128]{0:T(128)S(1)}, f32[128]{0:T(128)}, u32[]{:S(2)}) copy-start(f32[128]{0:T(128)} %get-tuple-element.1685) | copy-start | bytes 1540
  577.8 27.0 %copy-start.91 = (f32[1024]{0:T(1024)S(1)}, f32[1024]{0:T(1024)}, u32[]{:S(2)}) copy-start(f32[1024]{0:T(1024)} %param.39) | copy-start | bytes 12292
  603.2 9.0 collective-permute-start.3
  608.2 113.9 %all-reduce.22.cloned.1.call-start = ((), (), s32[]{:S(2)}) async-start(), calls=%async_computation.11 | async-start | bytes 4194304 | tf_op jit(solution)/shard_map/psum | solution.py:277
  610.6 4.0 collective-permute-start.2
  626.1 214.8 %reduce-scatter.9.cloned.1.call-start = ((), (), s32[]{:S(2)}) async-start(), calls=%async_computation.8 | async-start | bytes 18874368 | tf_op jit(solution)/shard_map/reduce_scatter | solution.py:286
  637.0 266.3 %all-reduce.20.cloned.1.call-start = ((), (), s32[]{:S(2)}) async-start(), calls=%async_computation.10 | async-start | bytes 2359296 | tf_op jit(solution)/shard_map/psum | solution.py:289
  646.3 331.7 %reduce-scatter.11.cloned.1.call-start = ((), (), s32[]{:S(2)}) async-start(), calls=%async_computation.9 | async-start | bytes 9437184 | tf_op jit(solution)/shard_map/reduce_scatter | solution.py:287
  654.9 95.1 %copy-start.38 = (f32[2,128,512]{2,1,0:T(8,128)S(1)}, f32[2,128,512]{2,1,0:T(8,128)}, u32[]{:S(2)}) copy-start(f32[2,128,512]{2,1,0:T(8,128)} %param.41) | copy-start | bytes 1572868
  654.9 95.1 %copy-start.93 = (f32[128]{0:T(128)S(1)}, f32[128]{0:T(128)}, u32[]{:S(2)}) copy-start(f32[128]{0:T(128)} %get-tuple-element.1702) | copy-start | bytes 1540
  654.9 95.1 %copy-start.94 = (f32[128]{0:T(128)S(1)}, f32[128]{0:T(128)}, u32[]{:S(2)}) copy-start(f32[128]{0:T(128)} %get-tuple-element.1704) | copy-start | bytes 1540
  (61 other events, 423.6 us)
Sparse Core Ops, SparseCore 0:
  9.9 57.0 all-gather.8
  68.9 37.4 all-gather.10
  456.1 24.6 reduce-scatter.4
  608.3 25.6 reduce-scatter.6
  636.3 85.6 all-reduce.21
  725.9 114.9 reduce-scatter.8
  845.9 57.3 all-reduce.19
  907.3 70.5 reduce-scatter.10
where the time goes:
time: 1010 us; the launch traced here: 991 us
  waiting for transfers between devices  300 us (30%)
  other arithmetic  226 us (22%)
  blocking collectives  191 us (19%)
  local copies, waits for them, and re-layouts  164 us (16%)
  matrix products  79.1 us (8%)
  between operations  16.1 us (2%)
    reduce_scatter x1, waiting for transfers between devices, local(): lax.psum_scatter(acc_in, 'seq', scatter_dimension=1, tiled=True)  87.5 us
    reduce_scatter x1, waiting for transfers between devices, local(): lax.psum_scatter(acc_out, 'seq', scatter_dimension=1, tiled=True)  74.7 us
    dynamic_update_slice x64, local copies, waits for them, and re-layouts, local(): lax.scan(forward_block, (ones_state, zero_state), (delta_blocks, b_blocks...  70.1 us
    psum x1, waiting for transfers between devices, local(): d_normed = lax.psum(norm_part, 'mp')  63 us
    psum x1, waiting for transfers between devices, local(): lax.psum((acc_gain, acc_conv, acc_cbias, acc_low, acc_state, acc_delta, a...  59.5 us
    all_gather x6, blocking collectives, prefix(): pieces = jax.tree.map(lambda part: lax.all_gather(part, axis), value)  58.5 us
    add x4, other arithmetic, local(): from_blocks(local_blocks) + from_blocks(prod_blocks) * carried[1][:, None]  41.7 us
    another operation x12, local copies, waits for them, and re-layouts  36.2 us
  transfers between devices with their start and end apart: 12, of which 6 were waited for; matrix products, arithmetic and copies ran while one was open for 20% of the time, Pallas kernels for 0%

commit v1 on v0

--- a/solution.py
+++ b/solution.py
@@ -1,15 +1,17 @@
+import functools
 import math
 
 import jax
 import jax.numpy as jnp
 from jax import lax
+from jax.experimental import pallas as pl
+from jax.experimental.pallas import tpu as pltpu
 from jax.sharding import PartitionSpec as P
 
 SEQ_MB = 1
 NMB = 2
-
-
 EPSILON = 1e-05
+VMEM_BYTES = 64 * 1024 * 1024 - 512 * 1024
 
 
 def from_behind(value, axis, steps):
@@ -99,7 +101,7 @@
     return sig_value * (1.0 + value * (1.0 - sig_value))
 
 
-def local(
+def plain(
     tokens,
     norm_gain,
     in_weight,
@@ -305,6 +307,1199 @@
     )
 
 
+MESH = pl.DeviceIdType.MESH
+F32 = jnp.float32
+BF16 = jnp.bfloat16
+LANE = 128
+GRP = 16
+PADV = 8
+SGVEC = 16
+
+
+def nn(a, b):
+    return lax.dot_general(a, b, (((1,), (0,)), ((), ())), preferred_element_type=F32)
+
+
+def nt(a, b):
+    return lax.dot_general(a, b, (((1,), (1,)), ((), ())), preferred_element_type=F32)
+
+
+def tn(a, b):
+    return lax.dot_general(a, b, (((0,), (0,)), ((), ())), preferred_element_type=F32)
+
+
+def cut(start, size):
+    return pl.ds(pl.multiple_of(start, size), size)
+
+
+def each(count, step):
+    lax.fori_loop(0, count, lambda index, unused: (step(index), unused)[1], 0)
+
+
+def wide(value, times):
+    return jnp.concatenate([value] * times, axis=1) if times > 1 else value
+
+
+class Sizes:
+    def __init__(self, mesh_shape, nseq, stretch, feature_dev, model, channels, nstate, rank):
+        self.S, self.M = mesh_shape["seq"], mesh_shape["mp"]
+        self.Q, self.T, self.Df, self.D, self.C = nseq, stretch, feature_dev, model, channels
+        self.N, self.RK = nstate, rank
+        self.R = nseq * stretch
+        self.Ds = model // self.S
+        self.B = max(1, feature_dev // self.Ds)
+        self.levels = self.S.bit_length() - 1
+        self.dims = [1 << bit for bit in range(1, self.levels)]
+        self.masks = [2 * value for value in range(self.S // 2)]
+        self.rows_sg = -(-(2 * rank + 2 * nstate + SGVEC) // (self.S * 32)) * 32
+        self.E = max(self.R, self.Ds)
+
+    def order(self, half):
+        turn = half * (len(self.dims) // 2)
+        return self.dims[turn:] + self.dims[:turn]
+
+    def fits(self, taps):
+        return (
+            self.S >= 4
+            and self.S & (self.S - 1) == 0
+            and self.M > 1
+            and self.Q == 2
+            and self.T == LANE
+            and self.Ds % 256 == 0
+            and self.Df % self.Ds == 0
+            and self.C % 256 == 0
+            and self.N == GRP
+            and self.RK == LANE
+            and taps == 4
+            and self.C * self.D <= (1 << 21)
+        )
+
+
+class Rows:
+    def __init__(self, ref, base, rows, count):
+        self.ref, self.base, self.rows, self.end = ref, base, rows, base + rows * count
+
+    def block(self, index, start=0, size=None):
+        first = pl.multiple_of(self.base + index * self.rows + start, 16)
+        return self.ref.at[pl.ds(first, self.rows if size is None else size), :]
+
+
+class Links:
+    def __init__(self, sems, seq, mp):
+        self.sems, self.used, self.seq, self.mp = sems, 0, seq, mp
+
+    def sem(self, count=1):
+        first = self.used
+        self.used += count
+        return first
+
+    def copy(self, src, dst, send, recv, seq=None, mp=None):
+        target = (self.seq if seq is None else seq, self.mp if mp is None else mp)
+        return pltpu.make_async_remote_copy(
+            src_ref=src,
+            dst_ref=dst,
+            send_sem=self.sems.at[send],
+            recv_sem=self.sems.at[recv],
+            device_id=target,
+            device_id_type=MESH,
+        )
+
+    def arrived(self, dst, recv):
+        self.copy(dst, dst, recv, recv).wait_recv()
+
+
+class TreeGather:
+    def __init__(self, z, links, half_view, whole_view):
+        self.z, self.links, self.half, self.whole = z, links, half_view, whole_view
+        self.recv = {(mask, h): links.sem() for mask in z.masks[1:] for h in range(2)}
+        self.near = {mask: links.sem() for mask in z.masks}
+        self.sent = []
+
+    def level(self, depth):
+        z, links = self.z, self.links
+        for mask in z.masks:
+            if bin(mask).count("1") != depth:
+                continue
+            owner = links.seq ^ mask
+            for h in range(2):
+                order = z.order(h)
+                last = max([i for i, dim in enumerate(order) if dim & mask], default=-1)
+                view = self.half(owner, h)
+                if mask:
+                    links.arrived(view, self.recv[mask, h])
+                for dim in order[last + 1 :]:
+                    copy = links.copy(view, view, links.sem(), self.recv[mask | dim, h], seq=links.seq ^ dim)
+                    copy.start()
+                    self.sent.append(copy)
+            view = self.whole(owner)
+            copy = links.copy(view, view, links.sem(), self.near[mask], seq=links.seq ^ 1)
+            copy.start()
+            self.sent.append(copy)
+
+    def finish(self):
+        for mask in self.z.masks:
+            self.links.arrived(self.whole(self.links.seq ^ 1 ^ mask), self.near[mask])
+
+    def drain(self):
+        for copy in self.sent:
+            copy.wait_send()
+
+
+class LineGather:
+    def __init__(self, z, links, view):
+        self.z, self.links, self.view = z, links, view
+        self.recv = links.sem(z.M)
+        self.send = links.sem(2 * z.M)
+
+    def parts(self, depth):
+        for side, way in enumerate((1, -1)):
+            owner, target = self.links.mp - way * depth, self.links.mp + way
+            held = (owner >= 0) & (owner < self.z.M)
+            more = held & (target >= 0) & (target < self.z.M)
+            yield side, owner, target, held, more
+
+    def copy(self, side, depth, owner, target):
+        view = self.view(owner)
+        return self.links.copy(view, view, self.send + 2 * depth + side, self.recv + owner, mp=target)
+
+    def step(self, depth):
+        for side, owner, target, held, more in self.parts(depth):
+            if depth:
+
+                @pl.when(held)
+                def _():
+                    self.links.arrived(self.view(owner), self.recv + owner)
+
+            @pl.when(more)
+            def _():
+                self.copy(side, depth, owner, target).start()
+
+    def drain(self):
+        for depth in range(self.z.M):
+            for side, owner, target, held, more in self.parts(depth):
+
+                @pl.when(more)
+                def _():
+                    self.copy(side, depth, owner, target).wait_send()
+
+
+class Swap:
+    def __init__(self, z, links, slot):
+        self.z, self.links, self.slot = z, links, slot
+        self.recv = links.sem(z.M)
+        self.send = links.sem(z.M)
+
+    def one(self, src, away):
+        target = lax.rem(self.links.mp + away, self.z.M)
+        return self.links.copy(src, self.slot(away - 1), self.send + away, self.recv + away, mp=target)
+
+    def start(self, src):
+        for away in range(1, self.z.M):
+            self.one(src, away).start()
+
+    def wait(self):
+        for away in range(1, self.z.M):
+            self.links.arrived(self.slot(away - 1), self.recv + away)
+
+    def drain(self, src):
+        for away in range(1, self.z.M):
+            self.one(src, away).wait_send()
+
+
+class Scatter:
+    def __init__(self, z, links, out, sums, far, rows):
+        self.z, self.links, self.out, self.sums, self.far, self.rows = z, links, out, sums, far, rows
+        self.near = {mask: links.sem() for mask in z.masks}
+        self.near_send = {mask: links.sem() for mask in z.masks}
+        self.sent = []
+        self.hops = {}
+        place = 0
+        for h in range(2):
+            order = z.order(h)
+            for step, dim in enumerate(order):
+                for mask in z.masks:
+                    if mask & dim and not any(mask & other for other in order[:step]):
+                        self.hops[h, step, mask] = (dim, links.sem(), links.sem(), place)
+                        place += 1
+        self.slots = place
+
+    def half(self, mask, h):
+        return self.sums.block(mask // 2, h * (self.rows // 2), self.rows // 2)
+
+    def first(self, make, ready=None):
+        z, links = self.z, self.links
+        for mask in z.masks:
+            src = make(links.seq ^ 1 ^ mask, mask)
+            if ready is not None and mask == 0:
+                ready()
+            copy = links.copy(src, self.sums.block(mask // 2), self.near_send[mask], self.near[mask], seq=links.seq ^ 1)
+            copy.start()
+            self.sent.append(copy)
+
+    def second(self, add):
+        z, links = self.z, self.links
+        by_need = sorted(z.masks, key=lambda mask: -bin(mask).count("1"))
+        for mask in by_need:
+            links.arrived(self.sums.block(mask // 2), self.near[mask])
+            add(links.seq ^ mask, mask)
+        self.send(0)
+
+    def send(self, step):
+        links = self.links
+        for (h, at, mask), (dim, send, recv, place) in self.hops.items():
+            if at == step:
+                copy = links.copy(self.half(mask, h), self.far.block(place), send, recv, seq=links.seq ^ dim)
+                copy.start()
+                self.sent.append(copy)
+
+    def fold(self, step):
+        links = self.links
+        for (h, at, mask), (dim, send, recv, place) in self.hops.items():
+            if at != step:
+                continue
+            links.arrived(self.far.block(place), recv)
+            into = mask ^ dim
+            if step < len(self.z.dims) - 1:
+                half = self.half(into, h)
+                half[...] = (half[...].astype(F32) + self.far.block(place)[...].astype(F32)).astype(BF16)
+        if step < len(self.z.dims) - 1:
+            self.send(step + 1)
+
+    def total(self, write):
+        last = len(self.z.dims) - 1
+        for (h, at, mask), (dim, send, recv, place) in self.hops.items():
+            if at == last:
+                rows = (h * (self.rows // 2), self.rows // 2)
+                write(rows, self.half(0, h)[...].astype(F32) + self.far.block(place)[...].astype(F32))
+
+    def drain(self):
+        for copy in self.sent:
+            copy.wait_send()
+
+
+def slots_of(z):
+    return Scatter(z, Links(None, 0, 0), None, None, None, 0).slots
+
+
+NAMES_IN = [
+    "tok",
+    "cot",
+    "gain",
+    "win",
+    "wout",
+    "convw",
+    "convb",
+    "dbias",
+    "skip",
+    "loww",
+    "statewt",
+    "deltaw",
+    "seqg",
+    "groupw",
+]
+NAMES_OUT = ["blk", "dtok", "dgain", "din", "dout", "sg"]
+
+
+def scratch_of(z):
+    V = pltpu.VMEM
+    half = z.S // 2
+    slots = slots_of(z)
+    return dict(
+        tokg=V((z.S, z.R, z.Ds), BF16),
+        halg=V((z.S, 16, z.Ds), BF16),
+        hals=V((z.B, 16, z.Ds), BF16),
+        db=V((z.S, z.R, z.Ds), BF16),
+        inv=V((z.R, LANE), F32),
+        normed=V((z.R + 16, z.D), BF16),
+        normt=V((z.D, z.R), BF16),
+        wx=V((2, z.D, z.C), BF16),
+        wo=V((z.S, z.C, z.Ds), BF16),
+        xpad=V((z.Q, 8 + z.T, z.C), F32),
+        dcp=V((z.Q, z.T + 8, z.C), F32),
+        conv=V((z.E, z.C), F32),
+        s=V((z.E, z.C), F32),
+        su=V((z.R, z.C), F32),
+        fac=V((z.E, z.C), F32),
+        zp=V((z.R, z.C), F32),
+        rd=V((z.R, z.C), F32),
+        dr=V((z.R, z.C), F32),
+        u=V((z.R, z.C), BF16),
+        gat=V((z.R, z.C), BF16),
+        gatt=V((z.C, z.R), BF16),
+        ddr=V((z.R, z.C), BF16),
+        dzr=V((z.R, z.C), BF16),
+        dxr=V((z.R, z.C), BF16),
+        lowp=V((z.M, z.R, z.RK), BF16),
+        stp=V((z.M, 2 * z.N, z.R), F32),
+        low=V((z.R, z.RK), BF16),
+        st=V((2 * z.N, z.R), F32),
+        blkb=V((z.R, GRP * z.N), BF16),
+        blkk=V((z.R, GRP * z.N), BF16),
+        blkc=V((z.R, GRP * z.N), BF16),
+        bc=V((z.Q, z.T, 2 * z.N, LANE), F32),
+        hist=V((z.Q * (z.T + 1) * z.N, z.C), BF16),
+        gbuf=V((GRP * z.N, z.C), BF16),
+        ghbuf=V((GRP * z.N, z.C), BF16),
+        ptot=V((z.Q, z.N, z.C), F32),
+        stot=V((z.Q, z.N, z.C), F32),
+        ppre=V((z.Q, z.N, z.C), F32),
+        spre=V((z.Q, z.N, z.C), F32),
+        csend=V((z.levels, z.Q, 2, z.N, z.C), BF16),
+        crecv=V((z.levels, z.Q, 2, z.N, z.C), BF16),
+        bsend=V((z.levels, z.Q, z.N, z.C), BF16),
+        brecv=V((z.levels, z.Q, z.N, z.C), BF16),
+        est=V((3, z.N, z.R), F32),
+        dlowp=V((z.M, z.R, z.RK), BF16),
+        dstp=V((z.M, 2 * z.N, z.R), BF16),
+        orecv=V((z.M - 1, z.R, z.Df), BF16),
+        nrecv=V((z.M - 1, z.R, z.Df), BF16),
+        near_o=V((half * z.C, z.Ds), BF16),
+        sum_o=V((half * z.C, z.Ds), BF16),
+        far_o=V((slots * (z.C // 2), z.Ds), BF16),
+        near_i=V((half * z.Ds, z.C), BF16),
+        sum_1=V((half * z.Ds, z.C), BF16),
+        far_1=V((slots * (z.Ds // 2), z.C), BF16),
+        vec=V((SGVEC, z.C), F32),
+        gv=V((z.levels + 1, 8, z.D), F32),
+        gvr=V((z.levels, 8, z.D), F32),
+        gvm=V((z.M - 1, 8, z.D), F32),
+        mrow=V((z.M, 8, z.R), F32),
+        sems=pltpu.SemaphoreType.DMA((420,)),
+        local=pltpu.SemaphoreType.DMA((8,)),
+        ready=pltpu.SemaphoreType.REGULAR((z.levels,)),
+    )
+
+
+def silu_parts(value):
+    gate = 1.0 / (1.0 + jnp.exp(-value))
+    return gate, value * gate
+
+
+def fused_kernel(z, names, *refs):
+    r = dict(zip(names, refs))
+    g = lambda name: r[name]
+    seq, mp = lax.axis_index("seq"), lax.axis_index("mp")
+    links = Links(g("sems"), seq, mp)
+    lanes_all = z.C // LANE
+    first_block = mp * z.B
+
+    def lane_loop(step):
+        each(z.C // LANE, lambda index: step(cut(index * LANE, LANE)))
+
+    local = g("local")
+    mine_in = lambda k: g("wx").at[k, cut(seq * z.Ds, z.Ds), :]
+    loads = [
+        pltpu.make_async_copy(g("win").at[0], mine_in(0), local.at[0]),
+        pltpu.make_async_copy(g("win").at[1], mine_in(1), local.at[1]),
+        pltpu.make_async_copy(g("wout"), g("wo").at[seq], local.at[2]),
+    ]
+    for load in loads:
+        load.start()
+    for b in range(z.B):
+        g("tokg")[first_block + b] = g("tok")[:, b * z.Ds : (b + 1) * z.Ds]
+        tails = [
+            g("tok")[q * z.T + z.T - 16 : q * z.T + z.T, b * z.Ds : (b + 1) * z.Ds].astype(F32)[8:]
+            for q in range(z.Q)
+        ]
+        g("hals")[b] = jnp.concatenate(tails, axis=0).astype(BF16)
+
+    barrier = pltpu.get_barrier_semaphore()
+    ahead, behind = lax.rem(seq + 1, z.S), lax.rem(seq + z.S - 1, z.S)
+    partners = [(seq ^ (1 << level), mp) for level in range(z.levels)] + [(ahead, mp), (behind, mp)]
+    partners += [(seq, lax.rem(mp + away, z.M)) for away in range(1, z.M)]
+    for partner in partners:
+        pl.semaphore_signal(barrier, inc=1, device_id=partner, device_id_type=MESH)
+    pl.semaphore_wait(barrier, len(partners))
+
+    def of_in(k):
+        def half(owner, h):
+            return g("wx").at[k, cut(owner * z.Ds + h * (z.Ds // 2), z.Ds // 2), :]
+
+        return TreeGather(z, links, half, lambda owner: g("wx").at[k, cut(owner * z.Ds, z.Ds), :])
+
+    tree_x, tree_z = of_in(0), of_in(1)
+    tree_o = TreeGather(
+        z,
+        links,
+        lambda owner, h: g("wo").at[owner, pl.ds(h * (z.C // 2), z.C // 2), :],
+        lambda owner: g("wo").at[owner],
+    )
+    line_t = LineGather(z, links, lambda owner: g("tokg").at[pl.ds(owner * z.B, z.B)])
+    line_h = LineGather(z, links, lambda owner: g("halg").at[pl.ds(owner * z.B, z.B)])
+    line_d = LineGather(z, links, lambda owner: g("db").at[pl.ds(owner * z.B, z.B)])
+    depth = len(z.dims)
+
+    loads[0].wait()
+    tree_x.level(0)
+    line_t.step(0)
+    hal_send, hal_recv = links.sem(), links.sem()
+    hal_mine = g("halg").at[pl.ds(first_block, z.B)]
+    hal = links.copy(g("hals"), hal_mine, hal_send, hal_recv, seq=ahead)
+    hal.start()
+
+    def weight_of(q):
+        total = jnp.float32(0.0)
+        for group in range(g("groupw").shape[0]):
+            total = total + jnp.where(g("seqg")[q] == group, g("groupw")[group], 0.0)
+        return total
+
+    seq_weight = [weight_of(q) for q in range(z.Q)]
+    for q in range(z.Q):
+        rows = pl.ds(q * z.T, z.T)
+        for b in range(z.B):
+            part = g("cot")[rows, b * z.Ds : (b + 1) * z.Ds] * seq_weight[q]
+            g("db")[first_block + b, rows, :] = part.astype(BF16)
+
+    links.arrived(hal_mine, hal_recv)
+    line_h.step(0)
+    line_t.step(1)
+    line_h.step(1)
+    tree_x.level(1)
+    loads[1].wait()
+    tree_z.level(0)
+    for far in range(2, z.M):
+        line_t.step(far)
+        line_h.step(far)
+
+    def add_squares(j, total):
+        part = g("tokg")[j].astype(F32)
+        edge = g("halg")[j].astype(F32)
+        return (
+            total[0] + jnp.sum(part * part, axis=1, keepdims=True),
+            total[1] + jnp.sum(edge * edge, axis=1, keepdims=True),
+        )
+
+    squares = lax.fori_loop(
+        0, z.S, add_squares, (jnp.zeros((z.R, 1), F32), jnp.zeros((16, 1), F32))
+    )
+    inv = lax.rsqrt(squares[0] * (1.0 / z.D) + EPSILON)
+    inv_edge = lax.rsqrt(squares[1] * (1.0 / z.D) + EPSILON)
+    g("inv")[...] = jnp.broadcast_to(inv, (z.R, LANE))
+
+    def norm_block(j):
+        features = cut(j * z.Ds, z.Ds)
+        gain = g("gain")[:, features]
+        normed = g("tokg")[j].astype(F32) * wide(g("inv")[...], z.Ds // LANE) * gain
+        g("normed")[: z.R, features] = normed.astype(BF16)
+        edge = g("halg")[j].astype(F32) * inv_edge * gain
+        g("normed")[z.R :, features] = edge.astype(BF16)
+        g("normt")[features, :] = normed.T.astype(BF16)
+
+    each(z.S, norm_block)
+    for rest in range(2, depth + 1):
+        tree_x.level(rest)
+    tree_x.finish()
+
+    def x_chunk(index):
+        lanes = cut(index * 256, 256)
+        part = nn(g("normed")[...], g("wx")[0, :, lanes]).astype(BF16).astype(F32)
+        for q in range(z.Q):
+            edge = part[z.R + 8 * q : z.R + 8 * q + 8]
+            g("xpad")[q, 0:8, lanes] = jnp.where(seq > 0, edge, 0.0)
+            g("xpad")[q, 8 : 8 + z.T, lanes] = part[q * z.T : (q + 1) * z.T]
+
+    each(z.C // 256, x_chunk)
+
+    def conv_lanes(lanes):
+        for q in range(z.Q):
+            total = jnp.broadcast_to(g("convb")[:, lanes], (z.T, LANE))
+            for tap in range(4):
+                total = total + g("convw")[tap : tap + 1, lanes] * g("xpad")[q, 5 + tap : 5 + tap + z.T, lanes]
+            g("conv")[q * z.T : (q + 1) * z.T, lanes] = total
+            g("u")[q * z.T : (q + 1) * z.T, lanes] = silu_parts(total)[1].astype(BF16)
+
+    lane_loop(conv_lanes)
+
+    swap_low = Swap(z, links, lambda slot: g("lowp").at[slot])
+    swap_st = Swap(z, links, lambda slot: g("stp").at[slot])
+    low_mine, st_mine = g("lowp").at[z.M - 1], g("stp").at[z.M - 1]
+    st_mine[...] = nt(g("statewt")[...], g("u")[...])
+    swap_st.start(st_mine)
+    low_mine[...] = nn(g("u")[...], g("loww")[...]).astype(BF16)
+    swap_low.start(low_mine)
+    tree_z.level(1)
+    loads[2].wait()
+    tree_o.level(0)
+    swap_st.wait()
+    swap_low.wait()
+    st = g("stp")[0]
+    low = g("lowp")[0].astype(F32)
+    for slot in range(1, z.M):
+        st = st + g("stp")[slot]
+        low = low + g("lowp")[slot].astype(F32)
+    g("st")[...] = st
+    g("low")[...] = low.astype(BF16)
+
+    rows_i = lax.broadcasted_iota(jnp.int32, (z.R, GRP * z.N), 0)
+    cols_i = lax.broadcasted_iota(jnp.int32, (z.R, GRP * z.N), 1)
+    diagonal = lax.rem(rows_i, GRP) == cols_i // z.N
+    rep_n = lax.broadcasted_iota(jnp.int32, (2 * z.N, GRP * z.N), 0)
+    rep_j = lax.rem(lax.broadcasted_iota(jnp.int32, (2 * z.N, GRP * z.N), 1), z.N)
+    nat = jnp.concatenate([st, jnp.zeros((LANE - 2 * z.N, z.R), F32)], axis=0).T
+    nat16 = nat[:, : 2 * z.N].astype(BF16)
+    rep_b = (rep_n == rep_j).astype(BF16)
+    rep_c = (rep_n == rep_j + z.N).astype(BF16)
+    spread_b = jnp.where(diagonal, nn(nat16, rep_b), 0.0)
+    g("blkb")[...] = spread_b.astype(BF16)
+    g("blkk")[...] = (spread_b * spread_b).astype(BF16)
+    g("blkc")[...] = jnp.where(diagonal, nn(nat16, rep_c), 0.0).astype(BF16)
+    only_b = lax.broadcasted_iota(jnp.int32, (z.R, LANE), 1) < z.N
+    key_sq = jnp.sum(jnp.where(only_b, nat * nat, 0.0), axis=1, keepdims=True)
+
+    for q in range(z.Q):
+
+        def spread(index, turned):
+            for j in range(8):
+                g("bc")[q, index * 8 + j] = jnp.broadcast_to(turned[:, j : j + 1], (2 * z.N, LANE))
+            return pltpu.roll(turned, LANE - 8, 1)
+
+        lax.fori_loop(0, z.T // 8, spread, st[:, q * z.T : (q + 1) * z.T])
+
+    def raw_chunk(index):
+        lanes = cut(index * 256, 256)
+        g("s")[: z.R, lanes] = nn(g("low")[...], g("deltaw")[:, lanes])
+
+    each(z.C // 256, raw_chunk)
+
+    def step_lanes(lanes):
+        for q in range(z.Q):
+            rows = pl.ds(q * z.T, z.T)
+            raw = g("s")[rows, lanes] + g("dbias")[:, lanes]
+            beta = 1.0 / (1.0 + jnp.exp(-raw))
+            scale = 1.0 / (1.0 + beta * key_sq[q * z.T : (q + 1) * z.T])
+            step = beta * scale
+            g("s")[rows, lanes] = step
+            g("su")[rows, lanes] = step * g("u")[rows, lanes].astype(F32)
+            g("fac")[rows, lanes] = scale * step * (1.0 - beta)
+
+    lane_loop(step_lanes)
+
+    span = 512 if z.C % 512 == 0 else 256
+
+    def token(q, t):
+        return pl.ds(q * z.T + t, 1)
+
+    def totals(q):
+        def lane_part(index):
+            lanes = cut(index * span, span)
+
+            def tokens8(i, carry):
+                product, state = carry
+                for j in range(8):
+                    row = token(q, i * 8 + j)
+                    step, drive = g("s")[row, lanes], g("su")[row, lanes]
+                    key = g("bc")[q, i * 8 + j, : z.N, :]
+                    decay = 1.0 - step * wide(key * key, span // LANE)
+                    product = product * decay
+                    state = decay * state + drive * wide(key, span // LANE)
+                return product, state
+
+            start = (jnp.ones((z.N, span), F32), jnp.zeros((z.N, span), F32))
+            product, state = lax.fori_loop(0, z.T // 8, tokens8, start)
+            g("ptot")[q, :, lanes] = product
+            g("stot")[q, :, lanes] = state
+
+        each(z.C // span, lane_part)
+
+    for q in range(z.Q):
+        totals(q)
+
+    g("ppre")[...] = jnp.ones_like(g("ppre"))
+    g("spre")[...] = jnp.zeros_like(g("spre"))
+    carry_sems = [(links.sem(), links.sem()) for level in range(z.levels)]
+    carry_copies = []
+    for level in range(z.levels):
+        for q in range(z.Q):
+            g("csend")[level, q, 0] = g("ptot")[q].astype(BF16)
+            g("csend")[level, q, 1] = g("stot")[q].astype(BF16)
+        copy = links.copy(
+            g("csend").at[level], g("crecv").at[level], *carry_sems[level], seq=seq ^ (1 << level)
+        )
+        copy.start()
+        carry_copies.append(copy)
+        if level == 0:
+            for rest in range(2, depth + 1):
+                tree_z.level(rest)
+        if level == 1:
+            tree_o.level(1)
+        copy.wait_recv()
+        upper = lax.rem(seq // (1 << level), 2) == 1
+        for q in range(z.Q):
+            other_p, other_s = g("crecv")[level, q, 0].astype(F32), g("crecv")[level, q, 1].astype(F32)
+            mine_p, mine_s = g("ptot")[q], g("stot")[q]
+            pre_p, pre_s = g("ppre")[q], g("spre")[q]
+            g("spre")[q] = jnp.where(upper, pre_p * other_s + pre_s, pre_s)
+            g("ppre")[q] = jnp.where(upper, pre_p * other_p, pre_p)
+            g("stot")[q] = jnp.where(upper, mine_p * other_s + mine_s, other_p * mine_s + other_s)
+            g("ptot")[q] = mine_p * other_p
+
+    def past_rows(q, slot, count=1):
+        return pl.ds(pl.multiple_of((q * (z.T + 1) + slot) * z.N, z.N), count * z.N)
+
+    def walk(q):
+        g("hist")[past_rows(q, 0), :] = g("spre")[q].astype(BF16)
+
+        def lane_part(index):
+            lanes = cut(index * span, span)
+
+            def tokens8(i, state):
+                for j in range(8):
+                    row = token(q, i * 8 + j)
+                    step, drive = g("s")[row, lanes], g("su")[row, lanes]
+                    key = g("bc")[q, i * 8 + j, : z.N, :]
+                    decay = 1.0 - step * wide(key * key, span // LANE)
+                    state = decay * state + drive * wide(key, span // LANE)
+                    g("hist")[past_rows(q, i * 8 + j + 1), lanes] = state.astype(BF16)
+                return state
+
+            lax.fori_loop(0, z.T // 8, tokens8, g("spre")[q, :, lanes])
+
+        each(z.C // span, lane_part)
+
+        def read(i):
+            rows = cut(q * z.T + i * GRP, GRP)
+            past = g("hist")[past_rows(q, i * GRP + 1, GRP), :]
+            g("rd")[rows, :] = nn(g("blkc")[rows, :], past)
+
+        each(z.T // GRP, read)
+
+    for q in range(z.Q):
+        walk(q)
+
+    tree_z.finish()
+    line_d.step(0)
+    for rest in range(2, depth + 1):
+        tree_o.level(rest)
+
+    def z_chunk(index):
+        lanes = cut(index * 256, 256)
+        g("zp")[:, lanes] = nn(g("normed")[: z.R, :], g("wx")[1, :, lanes])
+
+    each(z.C // 256, z_chunk)
+
+    def gate_lanes(lanes):
+        for q in range(z.Q):
+            rows = pl.ds(q * z.T, z.T)
+            out = g("rd")[rows, lanes] + g("skip")[:, lanes] * g("u")[rows, lanes].astype(F32)
+            g("rd")[rows, lanes] = out
+            gated = out * silu_parts(g("zp")[rows, lanes])[1]
+            g("gat")[rows, lanes] = gated.astype(BF16)
+            g("gatt")[lanes, rows] = gated.T.astype(BF16)
+
+    lane_loop(gate_lanes)
+    for far in range(1, z.M):
+        line_d.step(far)
+    tree_o.finish()
+
+    swap_out = Swap(z, links, lambda slot: g("orecv").at[slot])
+
+    def partial_of(owner):
+        return g("normed").at[pl.ds(0, z.R), cut(owner * z.Df, z.Df)]
+
+    def branch_to(index):
+        away = index + 1
+        owner = lax.rem(mp + away, z.M)
+        for b in range(z.B):
+            j = owner * z.B + b
+            g("normed")[: z.R, cut(j * z.Ds, z.Ds)] = nn(g("gat")[...], g("wo")[j]).astype(BF16)
+
+        @pl.when(away < z.M)
+        def _():
+            swap_out.one(partial_of(owner), away).start()
+
+    each(z.M, branch_to)
+
+    g("dr")[...] = nt(g("db")[0], g("wo")[0])
+
+    def gated_grad(index):
+        g("dr")[...] += nt(g("db")[index + 1], g("wo")[index + 1])
+
+    each(z.S - 1, gated_grad)
+    g("vec")[...] = jnp.zeros_like(g("vec"))
+
+    def gate_back(lanes):
+        for q in range(z.Q):
+            rows = pl.ds(q * z.T, z.T)
+            part, grad, out = g("zp")[rows, lanes], g("dr")[rows, lanes], g("rd")[rows, lanes]
+            gate, silu = silu_parts(part)
+            d_read = grad * silu
+            g("dr")[rows, lanes] = d_read
+            g("dzr")[rows, lanes] = (grad * out * gate * (1.0 + part * (1.0 - gate))).astype(BF16)
+            g("vec")[6:7, lanes] += jnp.sum(
+                d_read * g("u")[rows, lanes].astype(F32), axis=0, keepdims=True
+            )
+
+    lane_loop(gate_back)
+
+    def into(near, term):
+        def make(device, mask):
+            block = near.block(mask // 2)
+            block[...] = term(device).astype(BF16)
+            return block
+
+        return make
+
+    def onto(sums, term):
+        def add(device, mask):
+            block = sums.block(mask // 2)
+            block[...] = (term(device) + block[...].astype(F32)).astype(BF16)
+
+        return add
+
+    half_s, slots = z.S // 2, slots_of(z)
+    sg_rows = z.rows_sg
+    near_o, near_i = Rows(g("near_o"), 0, z.C, half_s), Rows(g("near_i"), 0, z.Ds, half_s)
+    sum_o, far_o = Rows(g("sum_o"), 0, z.C, half_s), Rows(g("far_o"), 0, z.C // 2, slots)
+    sum_1, far_1 = Rows(g("sum_1"), 0, z.Ds, half_s), Rows(g("far_1"), 0, z.Ds // 2, slots)
+    sum_0 = Rows(g("hist"), 0, z.Ds, half_s)
+    far_0 = Rows(g("hist"), sum_0.end, z.Ds // 2, slots)
+    sum_s = Rows(g("hist"), far_0.end, sg_rows, half_s)
+    far_s = Rows(g("hist"), sum_s.end, sg_rows // 2, slots)
+    sgp = Rows(g("hist"), far_s.end, sg_rows, z.S)
+    small = Rows(g("hist"), sgp.end, sg_rows, z.S)
+    scatter_o = Scatter(z, links, None, sum_o, far_o, z.C)
+    scatter_1 = Scatter(z, links, None, sum_1, far_1, z.Ds)
+    scatter_0 = Scatter(z, links, None, sum_0, far_0, z.Ds)
+    scatter_s = Scatter(z, links, None, sum_s, far_s, sg_rows)
+    term_o = lambda device: nn(g("gatt")[...], g("db")[device])
+    term_1 = lambda device: nn(g("normt")[cut(device * z.Ds, z.Ds), :], g("dzr")[...])
+    term_0 = lambda device: nn(g("normt")[cut(device * z.Ds, z.Ds), :], g("dxr")[...])
+    scatter_o.first(into(near_o, term_o))
+    scatter_1.first(into(near_i, term_1))
+    scatter_o.second(onto(sum_o, term_o))
+    scatter_1.second(onto(sum_1, term_1))
+
+    def totals_back(q):
+        def lane_part(index):
+            lanes = cut(index * span, span)
+
+            def tokens8(i, tail):
+                for j in reversed(range(8)):
+                    t = z.T - 8 - i * 8 + j
+                    row = token(q, t)
+                    step, grad = g("s")[row, lanes], g("dr")[row, lanes]
+                    key, query = g("bc")[q, t, : z.N, :], g("bc")[q, t, z.N :, :]
+                    decay = 1.0 - step * wide(key * key, span // LANE)
+                    tail = decay * (grad * wide(query, span // LANE) + tail)
+                return tail
+
+            g("stot")[q, :, lanes] = lax.fori_loop(0, z.T // 8, tokens8, jnp.zeros((z.N, span), F32))
+
+        each(z.C // span, lane_part)
+
+    for q in range(z.Q):
+        totals_back(q)
+    g("ppre")[...] = jnp.ones_like(g("ppre"))
+    g("spre")[...] = jnp.zeros_like(g("spre"))
+    back_sems = [(links.sem(), links.sem()) for level in range(z.levels)]
+    for level in range(z.levels):
+        for q in range(z.Q):
+            g("bsend")[level, q] = g("stot")[q].astype(BF16)
+        copy = links.copy(
+            g("bsend").at[level], g("brecv").at[level], *back_sems[level], seq=seq ^ (1 << level)
+        )
+        copy.start()
+        carry_copies.append(copy)
+        if level == 0:
+            for step in range(depth - 1):
+                scatter_o.fold(step)
+        copy.wait_recv()
+        upper = lax.rem(seq // (1 << level), 2) == 1
+        for q in range(z.Q):
+            other = g("brecv")[level, q].astype(F32)
+            other_p, mine_p = g("crecv")[level, q, 0].astype(F32), g("csend")[level, q, 0].astype(F32)
+            mine, pre_p, pre = g("stot")[q], g("ppre")[q], g("spre")[q]
+            g("spre")[q] = jnp.where(upper, pre, pre + pre_p * other)
+            g("ppre")[q] = jnp.where(upper, pre_p, pre_p * other_p)
+            g("stot")[q] = jnp.where(upper, other + other_p * mine, mine + mine_p * other)
+
+    lane_index = lax.broadcasted_iota(jnp.int32, (z.N, LANE), 1)
+
+    def lane_sum(value):
+        total = value[:, :LANE]
+        for part in range(1, lanes_all):
+            total = total + value[:, part * LANE : (part + 1) * LANE]
+        return jnp.sum(total, axis=1, keepdims=True)
+
+    def walk_back(q):
+        def group(index, carry):
+            tail, sum_gh, sum_g, sum_h = carry
+            i = z.T // GRP - 1 - index
+            for j in reversed(range(GRP)):
+                t = i * GRP + j
+                row = token(q, t)
+                step, drive, grad = g("s")[row, :], g("su")[row, :], g("dr")[row, :]
+                key, query = g("bc")[q, t, : z.N, :], g("bc")[q, t, z.N :, :]
+                before = g("hist")[past_rows(q, t), :].astype(F32)
+                now = g("hist")[past_rows(q, t + 1), :].astype(F32)
+                state_grad = grad * wide(query, lanes_all) + tail
+                crossed = state_grad * before
+                g("gbuf")[j * z.N : (j + 1) * z.N, :] = state_grad.astype(BF16)
+                g("ghbuf")[j * z.N : (j + 1) * z.N, :] = crossed.astype(BF16)
+                here = lane_index == t
+                sum_gh = jnp.where(here, lane_sum(step * crossed), sum_gh)
+                sum_g = jnp.where(here, lane_sum(drive * state_grad), sum_g)
+                sum_h = jnp.where(here, lane_sum(grad * now), sum_h)
+                tail = (1.0 - step * wide(key * key, lanes_all)) * state_grad
+            rows = cut(q * z.T + i * GRP, GRP)
+            g("rd")[rows, :] = nn(g("blkb")[rows, :], g("gbuf")[...])
+            g("zp")[rows, :] = nn(g("blkk")[rows, :], g("ghbuf")[...])
+            return tail, sum_gh, sum_g, sum_h
+
+        zero = jnp.zeros((z.N, LANE), F32)
+        _, sum_gh, sum_g, sum_h = lax.fori_loop(0, z.T // GRP, group, (g("spre")[q], zero, zero, zero))
+        columns = pl.ds(q * z.T, z.T)
+        g("est")[0, :, columns] = sum_gh
+        g("est")[1, :, columns] = sum_g
+        g("est")[2, :, columns] = sum_h
+
+    for q in range(z.Q):
+        walk_back(q)
+        for step in range(depth - 1):
+            if q == 0:
+                scatter_1.fold(step)
+
+    for level in range(z.levels):
+        pl.semaphore_signal(
+            g("ready").at[level], inc=1, device_id=(seq ^ (1 << level), mp), device_id_type=MESH
+        )
+
+    def step_back(lanes):
+        for q in range(z.Q):
+            rows = pl.ds(q * z.T, z.T)
+            sum_b, step = g("rd")[rows, lanes], g("s")[rows, lanes]
+            d_step = g("u")[rows, lanes].astype(F32) * sum_b - g("zp")[rows, lanes]
+            g("rd")[rows, lanes] = step * sum_b
+            d_raw = d_step * g("fac")[rows, lanes]
+            g("ddr")[rows, lanes] = d_raw.astype(BF16)
+            g("gat")[rows, lanes] = (d_step * step * step).astype(BF16)
+            g("vec")[5:6, lanes] += jnp.sum(d_raw, axis=0, keepdims=True)
+
+    lane_loop(step_back)
+    swap_dlow = Swap(z, links, lambda slot: g("dlowp").at[slot])
+    swap_dst = Swap(z, links, lambda slot: g("dstp").at[slot])
+    dlow_mine, dst_mine = g("dlowp").at[z.M - 1], g("dstp").at[z.M - 1]
+    dlow_mine[...] = nt(g("ddr")[...], g("deltaw")[...]).astype(BF16)
+    swap_dlow.start(dlow_mine)
+    key_grad = nt(jnp.ones((16, z.C), BF16), g("gat")[...])[0:1]
+    keys = g("st")[: z.N]
+    d_key = g("est")[1] - 2.0 * keys * g("est")[0] - 2.0 * keys * key_grad
+    dst_mine[...] = jnp.concatenate([d_key, g("est")[2]], axis=0).astype(BF16)
+    swap_dst.start(dst_mine)
+
+    def put_small(first, value):
+        count, at = value.shape[0], 0
+        while at < count:
+            block, inside = divmod(first + at, sg_rows)
+            take = min(count - at, sg_rows - inside)
+            sgp.block(block, inside, take)[...] = value[at : at + take].astype(BF16)
+            at += take
+
+    low_t = g("low")[...].astype(F32).T.astype(BF16)
+    put_small(0, nn(low_t, g("ddr")[...]))
+    swap_dlow.wait()
+    swap_dst.wait()
+    dlow = g("dlowp")[0].astype(F32)
+    dst = g("dstp")[0].astype(F32)
+    for slot in range(1, z.M):
+        dlow = dlow + g("dlowp")[slot].astype(F32)
+        dst = dst + g("dstp")[slot].astype(F32)
+    dlow16, dst16 = dlow.astype(BF16), dst.astype(BF16)
+    dst_nat = jnp.concatenate([dst, jnp.zeros((LANE - 2 * z.N, z.R), F32)], axis=0).T
+    dst_nat16 = dst_nat[:, : 2 * z.N].astype(BF16)
+    g("low")[...] = dlow16
+
+    def inputs_chunk(index):
+        lanes = cut(index * 256, 256)
+        g("su")[:, lanes] = nt(g("low")[...], g("loww")[lanes, :]) + nn(dst_nat16, g("statewt")[:, lanes])
+
+    each(z.C // 256, inputs_chunk)
+
+    def conv_back(lanes):
+        for q in range(z.Q):
+            rows = pl.ds(q * z.T, z.T)
+            total = g("su")[rows, lanes] + g("rd")[rows, lanes] + g("skip")[:, lanes] * g("dr")[rows, lanes]
+            value = g("conv")[rows, lanes]
+            gate = silu_parts(value)[0]
+            d_conv = total * gate * (1.0 + value * (1.0 - gate))
+            g("dcp")[q, 0 : z.T, lanes] = d_conv
+            g("vec")[4:5, lanes] += jnp.sum(d_conv, axis=0, keepdims=True)
+            for tap in range(4):
+                g("vec")[tap : tap + 1, lanes] += jnp.sum(
+                    d_conv * g("xpad")[q, 5 + tap : 5 + tap + z.T, lanes], axis=0, keepdims=True
+                )
+
+    lane_loop(conv_back)
+    rim = [
+        links.copy(
+            g("dcp").at[q, pl.ds(0, 8), :],
+            g("dcp").at[q, pl.ds(z.T, 8), :],
+            links.sem(),
+            links.sem(),
+            seq=behind,
+        )
+        for q in range(z.Q)
+    ]
+    for copy in rim:
+        copy.start()
+    put_small(z.RK, nn(dlow.T.astype(BF16), g("u")[...]))
+    put_small(2 * z.RK, nn(dst16, g("u")[...]))
+    put_small(2 * z.RK + 2 * z.N, g("vec")[...])
+    used = 2 * z.RK + 2 * z.N + SGVEC
+    if used < z.S * sg_rows:
+        put_small(used, jnp.zeros((z.S * sg_rows - used, z.C), F32))
+    for copy in rim:
+        copy.wait_recv()
+
+    def x_back(lanes):
+        for q in range(z.Q):
+            edge = g("dcp")[q, z.T : z.T + 8, lanes]
+            g("dcp")[q, z.T : z.T + 8, lanes] = jnp.where(seq < z.S - 1, edge, 0.0)
+            total = jnp.zeros((z.T, LANE), F32)
+            for tap in range(4):
+                total = total + g("convw")[tap : tap + 1, lanes] * g("dcp")[q, 3 - tap : 3 - tap + z.T, lanes]
+            g("dxr")[q * z.T : (q + 1) * z.T, lanes] = total.astype(BF16)
+
+    lane_loop(x_back)
+
+    for level in range(z.levels):
+        pl.semaphore_wait(g("ready").at[level], 1)
+    scatter_s.first(lambda device, mask: sgp.block(device))
+    for copy in scatter_1.sent[: len(z.masks)]:
+        copy.wait_send()
+    scatter_1.sent = scatter_1.sent[len(z.masks) :]
+    scatter_0.first(into(near_i, term_0))
+
+    def add_small(device, mask):
+        block = sum_s.block(mask // 2)
+        block[...] = (block[...].astype(F32) + sgp.block(device)[...].astype(F32)).astype(BF16)
+
+    scatter_s.second(add_small)
+    scatter_0.second(onto(sum_0, term_0))
+
+    swap_out.wait()
+    for away in range(1, z.M):
+        owner = lax.rem(mp + away, z.M)
+        swap_out.one(partial_of(owner), away).wait_send()
+    for b in range(z.B):
+        features = slice(b * z.Ds, (b + 1) * z.Ds)
+        total = g("normed")[: z.R, cut((first_block + b) * z.Ds, z.Ds)].astype(F32)
+        for slot in range(z.M - 1):
+            total = total + g("orecv")[slot, :, features].astype(F32)
+        g("blk")[:, features] = (g("tok")[:, features].astype(F32) + total).astype(BF16)
+
+    swap_n = Swap(z, links, lambda slot: g("nrecv").at[slot])
+
+    def normed_to(index, means):
+        away = index + 1
+        owner = lax.rem(mp + away, z.M)
+        for b in range(z.B):
+            j = owner * z.B + b
+            features = cut(j * z.Ds, z.Ds)
+            part = nt(g("dxr")[...], g("wx")[0, features, :]) + nt(g("dzr")[...], g("wx")[1, features, :])
+            g("normed")[: z.R, features] = part.astype(BF16)
+            scaled = part * g("tokg")[j].astype(F32)
+            by_gain = jnp.sum(scaled * wide(g("inv")[...], z.Ds // LANE), axis=0, keepdims=True)
+            g("gv")[0, :, features] = jnp.broadcast_to(by_gain, (8, z.Ds))
+            means = means + jnp.sum(scaled * g("gain")[:, features], axis=1, keepdims=True)
+
+        @pl.when(away < z.M)
+        def _():
+            swap_n.one(partial_of(owner), away).start()
+
+        return means
+
+    means = lax.fori_loop(0, z.M, normed_to, jnp.zeros((z.R, 1), F32))
+    swap_m = Swap(z, links, lambda slot: g("mrow").at[slot])
+    mean_mine = g("mrow").at[z.M - 1]
+    mean_mine[...] = jnp.broadcast_to(means, (z.R, LANE)).T[0:8]
+    swap_m.start(mean_mine)
+
+    gain_copies = []
+    for level in range(z.levels):
+        copy = links.copy(
+            g("gv").at[level], g("gvr").at[level], links.sem(), links.sem(), seq=seq ^ (1 << level)
+        )
+        copy.start()
+        gain_copies.append(copy)
+        if level < depth - 1:
+            scatter_s.fold(level)
+        copy.wait_recv()
+        g("gv")[level + 1] = g("gv")[level] + g("gvr")[level]
+    swap_g = Swap(z, links, lambda slot: g("gvm").at[slot])
+    swap_g.start(g("gv").at[z.levels])
+    scatter_s.fold(depth - 1)
+
+    def write_small(rows, value):
+        small.block(seq, *rows)[...] = value.astype(BF16)
+
+    scatter_s.total(write_small)
+    tree_s = TreeGather(
+        z,
+        links,
+        lambda owner, h: small.block(owner, h * (sg_rows // 2), sg_rows // 2),
+        small.block,
+    )
+    tree_s.level(0)
+    for step in range(depth - 1):
+        scatter_0.fold(step)
+    for level in range(1, depth + 1):
+        tree_s.level(level)
+
+    swap_m.wait()
+    mean = g("mrow")[0]
+    for slot in range(1, z.M):
+        mean = mean + g("mrow")[slot]
+    mean = wide(jnp.concatenate([mean] * (LANE // 8), axis=0).T * (1.0 / z.D), z.Ds // LANE)
+    swap_n.wait()
+    inv_wide = wide(g("inv")[...], z.Ds // LANE)
+    for b in range(z.B):
+        j = first_block + b
+        here = slice(b * z.Ds, (b + 1) * z.Ds)
+        gain = g("gain")[:, cut(j * z.Ds, z.Ds)]
+        total = g("normed")[: z.R, cut(j * z.Ds, z.Ds)].astype(F32)
+        for slot in range(z.M - 1):
+            total = total + g("nrecv")[slot, :, here].astype(F32)
+        x = g("tok")[:, here].astype(F32)
+        value = inv_wide * (total * gain) - x * (inv_wide * inv_wide * inv_wide) * mean
+        for q in range(z.Q):
+            rows = slice(q * z.T, (q + 1) * z.T)
+            g("dtok")[rows, here] = value[rows] + g("cot")[rows, here] * seq_weight[q]
+
+    last = depth - 1
+    scatter_o.fold(last)
+
+    def write_out(rows, value):
+        g("dout")[pl.ds(*rows), :] = value
+
+    scatter_o.total(write_out)
+    scatter_1.fold(last)
+
+    def write_to(name):
+        def write(rows, value):
+            g(name)[pl.ds(*rows), :] = value
+
+        return write
+
+    scatter_1.total(write_to("fac"))
+    store_1 = pltpu.make_async_copy(g("fac").at[pl.ds(0, z.Ds)], g("din").at[1], local.at[3])
+    store_1.start()
+    swap_g.wait()
+    gains = g("gv")[z.levels]
+    for slot in range(z.M - 1):
+        gains = gains + g("gvm")[slot]
+    g("dgain")[...] = gains[0:1]
+    tree_s.finish()
+    for block in range(z.S):
+        count = min(sg_rows, g("sg").shape[0] - block * sg_rows)
+        if count > 0:
+            g("sg")[block * sg_rows : block * sg_rows + count, :] = small.block(block)[...].astype(F32)[:count]
+    scatter_0.fold(last)
+    scatter_0.total(write_to("s"))
+    store_0 = pltpu.make_async_copy(g("s").at[pl.ds(0, z.Ds)], g("din").at[0], local.at[4])
+    store_0.start()
+
+    hal.wait_send()
+    for tree in (tree_x, tree_z, tree_o, tree_s):
+        tree.drain()
+    for line in (line_t, line_h, line_d):
+        line.drain()
+    swap_st.drain(st_mine)
+    swap_low.drain(low_mine)
+    swap_dlow.drain(dlow_mine)
+    swap_dst.drain(dst_mine)
+    swap_m.drain(mean_mine)
+    swap_g.drain(g("gv").at[z.levels])
+    for away in range(1, z.M):
+        owner = lax.rem(mp + away, z.M)
+        swap_n.one(partial_of(owner), away).wait_send()
+    for copy in carry_copies + gain_copies + rim:
+        copy.wait_send()
+    for scatter in (scatter_o, scatter_1, scatter_0, scatter_s):
+        scatter.drain()
+    store_1.wait()
+    store_0.wait()
+
+
+def fused(z, tokens, norm_gain, in_weight, conv_weight, conv_bias, low_weight, state_weight, delta_weight,
+          delta_bias, skip_gain, out_weight, cotangent, seq_group, group_weight):
+    V = pl.BlockSpec(memory_space=pltpu.VMEM)
+    A = pl.BlockSpec(memory_space=pl.ANY)
+    SM = pl.BlockSpec(memory_space=pltpu.SMEM)
+    where = dict(win=A, wout=A, seqg=SM, groupw=SM)
+    row = lambda value: value.reshape(1, -1)
+    operands = (
+        tokens.reshape(z.R, z.Df),
+        cotangent.reshape(z.R, z.Df),
+        row(norm_gain),
+        in_weight,
+        out_weight,
+        conv_weight,
+        row(conv_bias),
+        row(delta_bias),
+        row(skip_gain),
+        low_weight,
+        state_weight.T,
+        delta_weight,
+        seq_group,
+        group_weight,
+    )
+    scratch = scratch_of(z)
+    sg_used = 2 * z.RK + 2 * z.N + SGVEC
+    outs = dict(
+        blk=((z.R, z.Df), BF16),
+        dtok=((z.R, z.Df), F32),
+        dgain=((1, z.D), F32),
+        din=((2, z.Ds, z.C), F32),
+        dout=((z.C, z.Ds), F32),
+        sg=((sg_used, z.C), F32),
+    )
+    result = pl.pallas_call(
+        functools.partial(fused_kernel, z, NAMES_IN + NAMES_OUT + list(scratch)),
+        out_shape=[jax.ShapeDtypeStruct(*outs[name]) for name in NAMES_OUT],
+        in_specs=[where.get(name, V) for name in NAMES_IN],
+        out_specs=[A if name == "din" else V for name in NAMES_OUT],
+        scratch_shapes=list(scratch.values()),
+        compiler_params=pltpu.CompilerParams(
+            collective_id=0, has_side_effects=True, vmem_limit_bytes=VMEM_BYTES
+        ),
+    )(*operands)
+    blk, dtok, dgain, din, dout, sg = result
+    a, b, c = z.RK, 2 * z.RK, 2 * z.RK + 2 * z.N
+    return (
+        blk.reshape(tokens.shape),
+        dtok.reshape(tokens.shape),
+        dgain[0],
+        din,
+        sg[c : c + 4],
+        sg[c + 4],
+        sg[a:b].T,
+        sg[b:c].T,
+        sg[:a],
+        sg[c + 5],
+        sg[c + 6],
+        dout,
+    )
+
+
+def local(mesh_shape, *arrays):
+    tokens, norm_gain, in_weight, conv_weight = arrays[:4]
+    state_weight, delta_weight = arrays[6], arrays[7]
+    z = Sizes(
+        mesh_shape,
+        tokens.shape[0],
+        tokens.shape[1],
+        tokens.shape[2],
+        norm_gain.shape[0],
+        in_weight.shape[2],
+        state_weight.shape[1] // 2,
+        delta_weight.shape[0],
+    )
+    if z.fits(conv_weight.shape[0]):
+        return fused(z, *arrays)
+    return plain(*arrays)
+
+
 def solution(mesh):
     placed = (
         P(None, "seq", "mp"),
@@ -323,7 +1518,7 @@
         P(),
     )
     return jax.shard_map(
-        local,
+        functools.partial(local, dict(mesh.shape)),
         mesh=mesh,
         in_specs=placed,
         out_specs=(

time: 1010 us -> 228 us (0.23); the launches traced: 991 us -> 227 us
  waiting for transfers between devices: 300 us -> 0 us
  other arithmetic: 226 us -> 0 us
  Pallas kernels: 0 us -> 214 us
  blocking collectives: 191 us -> 0 us
  local copies, waits for them, and re-layouts: 164 us -> 12.6 us
  matrix products: 79.1 us -> 0 us
  between operations: 16.1 us -> 0.67 us
    pallas_call x0 -> x1, Pallas kernels: none -> 214 us  [fused(): pl.pallas_call(functools.partial(fused_kernel, z, NAMES_IN + NAMES_OUT +...]
    reduce_scatter x4 -> x0, waiting for transfers between devices: 162 us -> none  [the longest x1 87.5 us: local(): lax.psum_scatter(acc_in, 'seq', scatter_dimension=1, tiled=True)]
    all_gather x10 -> x0, blocking collectives: 124 us -> none  [the longest x6 58.5 us: prefix(): pieces = jax.tree.map(lambda part: lax.all_gather(part, axis), value)]
    psum x2 -> x0, waiting for transfers between devices: 123 us -> none  [the longest x1 63 us: local(): d_normed = lax.psum(norm_part, 'mp')]
    dot_general x34 -> x0, matrix products: 79.1 us -> none  [the longest x2 13.8 us: local(): jnp.einsum('sci,scd->id', gated_round, d_branch, preferred_element_type=j...]
    dynamic_update_slice x64 -> x0, local copies, waits for them, and re-layouts: 70.1 us -> none  [local(): lax.scan(forward_block, (ones_state, zero_state), (delta_blocks, b_blocks...]
    psum x3 -> x0, blocking collectives: 66.6 us -> none  [the longest x1 24.9 us: local(): lax.psum((acc_gain, acc_conv, acc_cbias, acc_low, acc_state, acc_delta, a...]
    reduce_sum x72 -> x0, other arithmetic: 53.5 us -> none  [the longest x2 23.8 us: make_gates(): decays = 1.0 - step_size[:, :, None, :] * (b_state * b_state)[:, :, :, None]]
  transfers between devices with their start and end apart: 12 -> 0, of which waited for: 6 -> 0; matrix products, arithmetic and copies ran while one was open for 20% -> 0% of each run, Pallas kernels for 0% -> 0%
where the time goes in v1:
time: 228 us; the launch traced here: 227 us
  Pallas kernels  214 us (94%)
  local copies, waits for them, and re-layouts  12.6 us (6%)
    pallas_call x1, Pallas kernels, fused(): pl.pallas_call(functools.partial(fused_kernel, z, NAMES_IN + NAMES_OUT +...  214 us
    unnamed x16, local copies, waits for them, and re-layouts  6.03 us

profile of v1, /device:TPU:0, one launch (start us, length us, event | category | flops | bytes accessed | tf_op | source)
XLA Modules:
  0.0 227.2 jit_solution(6087998401175169977)
XLA Ops:
  0.6 213.9 %shard_map.229 = (bf16[256,512]{1,0:T(8,128)(2,1)}, f32[256,512]{1,0:T(8,128)}, f32[1,2048]{1,0:T(1,128)}, f32[2,256,1024]{2,1,0:T(8,128)}, f32[1024,256]{1,0:T(8,128)}, /*index=5*/f32[304,1024]{1,0:T(8,128)}) custom-call(bf16[256,512]{1,0:T(8,128)(2,1)} %bitcast.20, f32[256,512]{1,0:T(8,128)} %bitcast.18, f32[1,2048]{1,0:T(1,128)} %bitcast.22, ...), custom_call_target="tpu_custom_call" | custom-call | tf_op jit(solution)/shard_map/pallas_call | solution.py:1457
  214.6 1.5 fusion
  216.1 1.4 slice.21
  217.4 1.6 slice_bitcast_fusion.1
  219.0 0.0 copy-start.3
  219.0 2.1 fusion.1
  221.1 0.0 copy-start.2
  221.1 0.0 copy-start.4
  221.1 0.0 copy-start
  221.1 1.0 copy.26
  222.1 0.0 copy-done.3
  222.1 0.7 copy.32
  222.8 0.0 copy-done.2
  222.8 0.8 copy.33
  223.6 0.0 copy-done.4
  223.6 0.6 copy.34
  224.2 0.0 copy-done
  224.2 0.0 copy-start.1
  224.2 1.3 copy.35
  225.5 0.6 copy-done.1
  226.2 1.0 copy.36
Async XLA Ops:
  219.0 3.1 %copy-start.3 = (bf16[256,512]{1,0:T(8,128)(2,1)S(1)}, bf16[256,512]{1,0:T(8,128)(2,1)}, u32[]{:S(2)}) copy-start(bf16[256,512]{1,0:T(8,128)(2,1)} %get-tuple-element.18) | copy-start | bytes 786436
  221.1 1.7 copy-start.2
  221.1 2.5 %copy-start.4 = (f32[1,2048]{1,0:T(1,128)S(1)}, f32[1,2048]{1,0:T(1,128)}, u32[]{:S(2)}) copy-start(f32[1,2048]{1,0:T(1,128)} %get-tuple-element.20) | copy-start | bytes 24580
  221.1 3.1 %copy-start = (f32[2,256,1024]{2,1,0:T(8,128)S(1)}, f32[2,256,1024]{2,1,0:T(8,128)}, u32[]{:S(2)}) copy-start(f32[2,256,1024]{2,1,0:T(8,128)} %get-tuple-element.56) | copy-start | bytes 6291460
  224.2 2.0 copy-start.1

commit v2 on v1

v2 whole, which is shorter than its diff:
```python
import functools
import math

import jax
import jax.numpy as jnp
from jax import lax
from jax.experimental import pallas as pl
from jax.experimental.pallas import tpu as pltpu
from jax.sharding import PartitionSpec as P

SEQ_MB = 1
NMB = 2
EPSILON = 1e-05
VMEM_BYTES = 64 * 1024 * 1024 - 64 * 1024


def from_behind(value, axis, steps):
    count = lax.axis_size(axis)
    leading, last = (max(0, -steps), min(count, count - steps))
    return lax.ppermute(value, axis, [(source, source + steps) for source in range(leading, last)])


def prefix(value, axis, join, neutral, backward):
    count, mine = (lax.axis_size(axis), lax.axis_index(axis))
    pieces = jax.tree.map(lambda part: lax.all_gather(part, axis), value)
    if backward:
        pieces = jax.tree.map(lambda part: part[::-1], pieces)
        mine = count - 1 - mine
    subtotal = jax.tree.map(
        lambda part, zero: jnp.full_like(part, 0) + jnp.asarray(zero, part.dtype), value, neutral
    )

    def lap(position, subtotal):
        longer = join(subtotal, jax.tree.map(lambda part: part[position], pieces))
        return jax.tree.map(lambda new, old: jnp.where(position < mine, new, old), longer, subtotal)

    return lax.fori_loop(0, count - 1, lap, subtotal)


def combine(earlier, later):
    return (earlier[0] * later[0], later[0] * earlier[1] + later[1])


def make_gates(delta_raw, b_state, inputs):
    beta_gate = jax.nn.sigmoid(delta_raw)
    key_sq = jnp.sum(b_state * b_state, axis=-1, keepdims=True)
    step_size = beta_gate / (1.0 + beta_gate * key_sq)
    decays = 1.0 - step_size[:, :, None, :] * (b_state * b_state)[:, :, :, None]
    source = (step_size * inputs)[:, :, None, :] * b_state[:, :, :, None]
    return (decays, source)


def to_blocks(value, span_rows):
    old_shape = value.shape
    reshaped = value.reshape((old_shape[0], old_shape[1] // span_rows, span_rows) + old_shape[2:])
    return jnp.swapaxes(reshaped, 0, 1)


def from_blocks(value):
    joined = jnp.swapaxes(value, 0, 1)
    old_shape = joined.shape
    return joined.reshape((old_shape[0], old_shape[1] * old_shape[2]) + old_shape[3:])


def forward_block(carry_pair, block_items):
    delta_raw, b_state, inputs = block_items
    decays, source = make_gates(delta_raw, b_state, inputs)
    run_prod, run_state = carry_pair
    prod_list = []
    state_list = []
    for row_idx in range(decays.shape[1]):
        run_prod = run_prod * decays[:, row_idx]
        run_state = decays[:, row_idx] * run_state + source[:, row_idx]
        prod_list.append(run_prod)
        state_list.append(run_state)
    return ((run_prod, run_state), (jnp.stack(prod_list, axis=1), jnp.stack(state_list, axis=1)))


def backward_block(carry_trio, block_items):
    delta_raw, b_state, inputs, read_grad, c_state = block_items
    decays, _ = make_gates(delta_raw, b_state, inputs)
    grad_next, dec_next, tail_prod = carry_trio
    span_rows = decays.shape[1]
    grad_list = [None] * span_rows
    tail_list = [None] * span_rows
    for row_idx in reversed(range(span_rows)):
        drive_term = read_grad[:, row_idx][:, None, :] * c_state[:, row_idx][:, :, None]
        grad_next = drive_term + dec_next * grad_next
        tail_prod = dec_next * tail_prod
        grad_list[row_idx] = grad_next
        tail_list[row_idx] = tail_prod
        dec_next = decays[:, row_idx]
    return (
        (grad_next, dec_next, tail_prod),
        (jnp.stack(grad_list, axis=1), jnp.stack(tail_list, axis=1)),
    )


def silu_slope(value):
    sig_value = jax.nn.sigmoid(value)
    return sig_value * (1.0 + value * (1.0 - sig_value))


def plain(
    tokens,
    norm_gain,
    in_weight,
    conv_weight,
    conv_bias,
    low_weight,
    state_weight,
    delta_weight,
    delta_bias,
    skip_gain,
    out_weight,
    cotangent,
    seq_group,
    group_weight,
):
    stretch = tokens.shape[1]
    feature_dev = tokens.shape[2]
    channels = in_weight.shape[2]
    model_width = norm_gain.shape[0]
    num_taps = conv_weight.shape[0]
    nstate = state_weight.shape[1] // 2
    span_rows = math.gcd(stretch, 8)
    picks = (
        seq_group[:, None] == jnp.arange(group_weight.shape[0], dtype=jnp.int32)[None, :]
    ).astype(jnp.float32)
    seq_weight = jnp.sum(picks * group_weight[None, :], axis=1)
    feature_start = lax.axis_index("mp") * feature_dev
    ones_state = jnp.ones((SEQ_MB, nstate, channels), jnp.float32)
    zero_state = jnp.zeros_like(ones_state)
    acc_in = jnp.zeros((2, model_width, channels), jnp.float32)
    acc_out = jnp.zeros((channels, model_width), jnp.float32)
    acc_gain = jnp.zeros_like(norm_gain)
    acc_conv = jnp.zeros_like(conv_weight)
    acc_cbias = jnp.zeros_like(conv_bias)
    acc_low = jnp.zeros(low_weight.shape, jnp.float32)
    acc_state = jnp.zeros(state_weight.shape, jnp.float32)
    acc_delta = jnp.zeros(delta_weight.shape, jnp.float32)
    acc_dbias = jnp.zeros_like(delta_bias)
    acc_skip = jnp.zeros_like(skip_gain)
    outputs = []
    input_grads = []
    for micro_idx in range(NMB):
        whole_in, whole_out = (
            lax.all_gather(in_weight, "seq", axis=1, tiled=True),
            lax.all_gather(out_weight, "seq", axis=1, tiled=True),
        )
        first_seq = micro_idx * SEQ_MB
        block_tokens = tokens[first_seq : first_seq + SEQ_MB]
        full_tokens = lax.all_gather(block_tokens, "mp", axis=2, tiled=True).astype(jnp.float32)
        inv_rms = lax.rsqrt(jnp.mean(full_tokens * full_tokens, axis=-1, keepdims=True) + EPSILON)
        normed = (full_tokens * inv_rms * norm_gain).astype(jnp.bfloat16)
        both_parts = jnp.einsum(
            "scd,kdi->ksci", normed, whole_in, preferred_element_type=jnp.float32
        )
        x_round = both_parts[0].astype(jnp.bfloat16)
        z_part = both_parts[1]
        rim_rows = from_behind(x_round[:, stretch - (num_taps - 1) :], "seq", 1)
        padded = jnp.concatenate([rim_rows, x_round], axis=1).astype(jnp.float32)
        conv_sum = conv_bias + jnp.zeros((SEQ_MB, stretch, channels), jnp.float32)
        for tap_index in range(num_taps):
            conv_sum = (
                conv_sum + conv_weight[tap_index] * padded[:, tap_index : tap_index + stretch]
            )
        inputs_round = jax.nn.silu(conv_sum).astype(jnp.bfloat16)
        inputs_f = inputs_round.astype(jnp.float32)
        low_part = jnp.einsum(
            "sci,ir->scr", inputs_round, low_weight, preferred_element_type=jnp.float32
        )
        state_part = jnp.einsum(
            "sci,ir->scr", inputs_round, state_weight, preferred_element_type=jnp.float32
        )
        delta_low, state_proj = lax.psum((low_part, state_part), "mp")
        delta_round = delta_low.astype(jnp.bfloat16)
        delta_raw = (
            jnp.einsum("scr,ri->sci", delta_round, delta_weight, preferred_element_type=jnp.float32)
            + delta_bias
        )
        b_state = state_proj[..., :nstate]
        c_state = state_proj[..., nstate:]
        delta_blocks = to_blocks(delta_raw, span_rows)
        b_blocks = to_blocks(b_state, span_rows)
        c_blocks = to_blocks(c_state, span_rows)
        in_blocks = to_blocks(inputs_f, span_rows)
        stretch_pair, (prod_blocks, local_blocks) = lax.scan(
            forward_block, (ones_state, zero_state), (delta_blocks, b_blocks, in_blocks)
        )
        carried = prefix(stretch_pair, "seq", combine, (ones_state, zero_state), False)
        states = from_blocks(local_blocks) + from_blocks(prod_blocks) * carried[1][:, None]
        before = jnp.concatenate([carried[1][:, None], states[:, :-1]], axis=1)
        read_rec = jnp.einsum("scni,scn->sci", states, c_state)
        read_out = read_rec + skip_gain * inputs_f
        z_gate = jax.nn.silu(z_part)
        gated_round = (read_out * z_gate).astype(jnp.bfloat16)
        out_part = jnp.einsum(
            "sci,id->scd", gated_round, whole_out, preferred_element_type=jnp.float32
        )
        branch = lax.psum_scatter(out_part, "mp", scatter_dimension=2, tiled=True)
        outputs.append((block_tokens.astype(jnp.float32) + branch).astype(jnp.bfloat16))
        d_out = (
            cotangent[first_seq : first_seq + SEQ_MB]
            * seq_weight[first_seq : first_seq + SEQ_MB][:, None, None]
        )
        d_branch = lax.all_gather(d_out.astype(jnp.bfloat16), "mp", axis=2, tiled=True)
        acc_out = acc_out + jnp.einsum(
            "sci,scd->id", gated_round, d_branch, preferred_element_type=jnp.float32
        )
        d_gated = jnp.einsum("scd,id->sci", d_branch, whole_out, preferred_element_type=jnp.float32)
        d_read = d_gated * z_gate
        d_zpart = d_gated * read_out * silu_slope(z_part)
        acc_skip = acc_skip + jnp.sum(d_read * inputs_f, axis=(0, 1))
        read_blocks_grad = to_blocks(d_read, span_rows)
        (last_grad, first_dec, _), (grad_blocks, tail_blocks) = lax.scan(
            backward_block,
            (zero_state, ones_state, ones_state),
            (delta_blocks, b_blocks, in_blocks, read_blocks_grad, c_blocks),
            reverse=True,
        )
        tail_grad = first_dec * last_grad
        crossing = prefix(
            (stretch_pair[0], tail_grad), "seq", combine, (ones_state, zero_state), True
        )
        state_grad = from_blocks(grad_blocks) + from_blocks(tail_blocks) * crossing[1][:, None]
        _, gate_pullback = jax.vjp(make_gates, delta_raw, b_state, inputs_f)
        d_delta, d_bstate, d_inputs_state = gate_pullback((state_grad * before, state_grad))
        d_cstate = jnp.einsum("scni,sci->scn", states, d_read)
        acc_dbias = acc_dbias + jnp.sum(d_delta, axis=(0, 1))
        d_delta_round = d_delta.astype(jnp.bfloat16)
        acc_delta = acc_delta + jnp.einsum(
            "scr,sci->ri", delta_round, d_delta_round, preferred_element_type=jnp.float32
        )
        low_grad_part = jnp.einsum(
            "sci,ri->scr", d_delta_round, delta_weight, preferred_element_type=jnp.float32
        )
        state_grad_part = jnp.concatenate([d_bstate, d_cstate], axis=-1)
        d_low, d_state = lax.psum((low_grad_part, state_grad_part), "mp")
        d_low_round = d_low.astype(jnp.bfloat16)
        d_state_round = d_state.astype(jnp.bfloat16)
        acc_low = acc_low + jnp.einsum(
            "sci,scr->ir", inputs_round, d_low_round, preferred_element_type=jnp.float32
        )
        acc_state = acc_state + jnp.einsum(
            "sci,scr->ir", inputs_round, d_state_round, preferred_element_type=jnp.float32
        )
        d_inputs = d_read * skip_gain + d_inputs_state
        d_inputs = d_inputs + jnp.einsum(
            "scr,ir->sci", d_low_round, low_weight, preferred_element_type=jnp.float32
        )
        d_inputs = d_inputs + jnp.einsum(
            "scr,ir->sci", d_state_round, state_weight, preferred_element_type=jnp.float32
        )
        d_conv = d_inputs * silu_slope(conv_sum)
        acc_cbias = acc_cbias + jnp.sum(d_conv, axis=(0, 1))
        tap_grads = []
        d_padded = jnp.zeros((SEQ_MB, stretch + num_taps - 1, channels), jnp.float32)
        for tap_index in range(num_taps):
            tap_grads.append(
                jnp.sum(d_conv * padded[:, tap_index : tap_index + stretch], axis=(0, 1))
            )
            d_padded = d_padded + jnp.pad(
                conv_weight[tap_index] * d_conv,
                ((0, 0), (tap_index, num_taps - 1 - tap_index), (0, 0)),
            )
        acc_conv = acc_conv + jnp.stack(tap_grads)
        back_rim = from_behind(d_padded[:, : num_taps - 1], "seq", -1)
        d_xpart = d_padded[:, num_taps - 1 :] + jnp.pad(
            back_rim, ((0, 0), (stretch - (num_taps - 1), 0), (0, 0))
        )
        d_parts_round = jnp.stack([d_xpart, d_zpart]).astype(jnp.bfloat16)
        acc_in = acc_in + jnp.einsum(
            "scd,ksci->kdi", normed, d_parts_round, preferred_element_type=jnp.float32
        )
        norm_part = jnp.einsum(
            "ksci,kdi->scd", d_parts_round, whole_in, preferred_element_type=jnp.float32
        )
        d_normed = lax.psum(norm_part, "mp")
        acc_gain = acc_gain + jnp.sum(d_normed * full_tokens * inv_rms, axis=(0, 1))
        scaled = d_normed * norm_gain
        d_full = inv_rms * scaled - full_tokens * (inv_rms * inv_rms * inv_rms) * jnp.mean(
            scaled * full_tokens, axis=-1, keepdims=True
        )
        d_mine = lax.dynamic_slice_in_dim(d_full, feature_start, feature_dev, 2)
        input_grads.append(d_out + d_mine)
    d_in_weight, d_out_weight = (
        lax.psum_scatter(acc_in, "seq", scatter_dimension=1, tiled=True),
        lax.psum_scatter(acc_out, "seq", scatter_dimension=1, tiled=True),
    )
    summed = lax.psum(
        (acc_gain, acc_conv, acc_cbias, acc_low, acc_state, acc_delta, acc_dbias, acc_skip), "seq"
    )
    return (
        jnp.concatenate(outputs, axis=0),
        jnp.concatenate(input_grads, axis=0),
        summed[0],
        d_in_weight,
        summed[1],
        summed[2],
        summed[3],
        summed[4],
        summed[5],
        summed[6],
        summed[7],
        d_out_weight,
    )


MESH = pl.DeviceIdType.MESH
F32 = jnp.float32
BF16 = jnp.bfloat16
LANE = 128
GRP = 16
PADV = 8
SGVEC = 16


def nn(a, b):
    return lax.dot_general(a, b, (((1,), (0,)), ((), ())), preferred_element_type=F32)


def nt(a, b):
    return lax.dot_general(a, b, (((1,), (1,)), ((), ())), preferred_element_type=F32)


def tn(a, b):
    return lax.dot_general(a, b, (((0,), (0,)), ((), ())), preferred_element_type=F32)


def cut(start, size):
    return pl.ds(pl.multiple_of(start, size), size)


def each(count, step):
    lax.fori_loop(0, count, lambda index, unused: (step(index), unused)[1], 0)


def wide(value, times):
    return jnp.concatenate([value] * times, axis=1) if times > 1 else value


class Sizes:
    def __init__(self, mesh_shape, nseq, stretch, feature_dev, model, channels, nstate, rank):
        self.S, self.M = mesh_shape["seq"], mesh_shape["mp"]
        self.Q, self.T, self.Df, self.D, self.C = nseq, stretch, feature_dev, model, channels
        self.N, self.RK = nstate, rank
        self.R = nseq * stretch
        self.Ds = model // self.S
        self.B = max(1, feature_dev // self.Ds)
        self.levels = self.S.bit_length() - 1
        self.dims = [1 << bit for bit in range(1, self.levels)]
        self.masks = [2 * value for value in range(self.S // 2)]
        self.rows_sg = -(-(2 * rank + 2 * nstate + SGVEC) // (self.S * 16)) * 16
        self.E = max(self.R, self.Ds)

    def order(self, half):
        turn = half * (len(self.dims) // 2)
        return self.dims[turn:] + self.dims[:turn]

    def fits(self, taps):
        return (
            self.S in (4, 8)
            and self.M > 1
            and self.Q == 2
            and self.T == LANE
            and self.Ds % 256 == 0
            and self.Df % self.Ds == 0
            and self.C % 256 == 0
            and self.N == GRP
            and self.RK == LANE
            and taps == 4
            and self.C * self.D <= (1 << 21)
        )


class Bunch:
    def __init__(self, names, values):
        self.__dict__.update(zip(names, values))


class Rows:
    def __init__(self, ref, base, rows, count):
        self.ref, self.base, self.rows, self.end = ref, base, rows, base + rows * count

    def block(self, index, start=0, size=None):
        first = pl.multiple_of(self.base + index * self.rows + start, 16)
        return self.ref.at[pl.ds(first, self.rows if size is None else size), :]


class Links:
    def __init__(self, sems, seq, mp):
        self.sems, self.used, self.seq, self.mp = sems, 0, seq, mp

    def sem(self, count=1):
        first = self.used
        self.used += count
        return first

    def copy(self, src, dst, send, recv, seq=None, mp=None):
        target = (self.seq if seq is None else seq, self.mp if mp is None else mp)
        return pltpu.make_async_remote_copy(
            src_ref=src,
            dst_ref=dst,
            send_sem=self.sems.at[send],
            recv_sem=self.sems.at[recv],
            device_id=target,
            device_id_type=MESH,
        )

    def arrived(self, dst, recv):
        self.copy(dst, dst, recv, recv).wait_recv()


class TreeGather:
    def __init__(self, z, links, half_view, whole_view):
        self.z, self.links, self.half, self.whole = z, links, half_view, whole_view
        self.recv = {(mask, h): links.sem() for mask in z.masks[1:] for h in range(2)}
        self.near = {mask: links.sem() for mask in z.masks}
        self.sent = []

    def push(self, mask, h, dim):
        view = self.half(self.links.seq ^ mask, h)
        copy = self.links.copy(
            view, view, self.links.sem(), self.recv[mask | dim, h], seq=self.links.seq ^ dim
        )
        copy.start()
        self.sent.append(copy)

    def take(self, mask, h):
        self.links.arrived(self.half(self.links.seq ^ mask, h), self.recv[mask, h])

    def hand(self, mask):
        view = self.whole(self.links.seq ^ mask)
        copy = self.links.copy(view, view, self.links.sem(), self.near[mask], seq=self.links.seq ^ 1)
        copy.start()
        self.sent.append(copy)

    def first(self):
        for h in range(2):
            self.push(0, h, self.z.order(h)[0])

    def second(self):
        for h in range(2):
            for dim in self.z.order(h)[1:]:
                self.push(0, h, dim)
        self.hand(0)

    def forward(self):
        for h in range(2):
            order = self.z.order(h)
            if len(order) > 1:
                self.take(order[0], h)
                self.push(order[0], h, order[1])

    def settle(self):
        for mask in sorted(self.z.masks[1:], key=lambda mask: bin(mask).count("1")):
            for h in range(2):
                order = self.z.order(h)
                if len(order) == 1 or mask != order[0]:
                    self.take(mask, h)
            self.hand(mask)

    def finish(self):
        for mask in self.z.masks:
            self.links.arrived(self.whole(self.links.seq ^ 1 ^ mask), self.near[mask])

    def drain(self):
        for copy in self.sent:
            copy.wait_send()


class LineGather:
    def __init__(self, z, links, view):
        self.z, self.links, self.view = z, links, view
        self.recv = links.sem(z.M)
        self.send = links.sem(2 * z.M)

    def parts(self, depth):
        for side, way in enumerate((1, -1)):
            owner, target = self.links.mp - way * depth, self.links.mp + way
            held = (owner >= 0) & (owner < self.z.M)
            more = held & (target >= 0) & (target < self.z.M)
            yield side, owner, target, held, more

    def copy(self, side, depth, owner, target):
        view = self.view(owner)
        return self.links.copy(view, view, self.send + 2 * depth + side, self.recv + owner, mp=target)

    def step(self, depth):
        for side, owner, target, held, more in self.parts(depth):
            if depth:

                @pl.when(held)
                def _():
                    self.links.arrived(self.view(owner), self.recv + owner)

            @pl.when(more)
            def _():
                self.copy(side, depth, owner, target).start()

    def drain(self):
        for depth in range(self.z.M):
            for side, owner, target, held, more in self.parts(depth):

                @pl.when(more)
                def _():
                    self.copy(side, depth, owner, target).wait_send()


class Swap:
    def __init__(self, z, links, slot):
        self.z, self.links, self.slot = z, links, slot
        self.recv = links.sem(z.M)
        self.send = links.sem(z.M)

    def one(self, src, away):
        target = lax.rem(self.links.mp + away, self.z.M)
        return self.links.copy(src, self.slot(away - 1), self.send + away, self.recv + away, mp=target)

    def start(self, src):
        for away in range(1, self.z.M):
            self.one(src, away).start()

    def wait(self):
        for away in range(1, self.z.M):
            self.links.arrived(self.slot(away - 1), self.recv + away)

    def drain(self, src):
        for away in range(1, self.z.M):
            self.one(src, away).wait_send()


def halves(rows):
    first = -(-rows // 32) * 16
    return (0, first), (first, rows - first)


class Scatter:
    def __init__(self, z, links, out, sums, far, rows):
        self.z, self.links, self.out, self.sums, self.far, self.rows = z, links, out, sums, far, rows
        self.near = {mask: links.sem() for mask in z.masks}
        self.near_send = {mask: links.sem() for mask in z.masks}
        self.sent = []
        self.hops = {}
        place = 0
        for h in range(2):
            order = z.order(h)
            for step, dim in enumerate(order):
                for mask in z.masks:
                    if mask & dim and not any(mask & other for other in order[:step]):
                        self.hops[h, step, mask] = (dim, links.sem(), links.sem(), place)
                        place += 1
        self.slots = place

    def half(self, mask, h):
        start, size = halves(self.rows)[h]
        return self.sums.block(mask // 2, start, size)

    def came(self, h, place):
        return self.far.block(place, 0, halves(self.rows)[h][1])

    def first(self, make):
        z, links = self.z, self.links
        for mask in z.masks:
            src = make(links.seq ^ 1 ^ mask, mask)
            copy = links.copy(src, self.sums.block(mask // 2), self.near_send[mask], self.near[mask], seq=links.seq ^ 1)
            copy.start()
            self.sent.append(copy)

    def second(self, add):
        z, links = self.z, self.links
        by_need = sorted(z.masks, key=lambda mask: -bin(mask).count("1"))
        for mask in by_need:
            links.arrived(self.sums.block(mask // 2), self.near[mask])
            add(links.seq ^ mask, mask)

    def send(self, step, part=None):
        links = self.links
        count = {0: 0, 1: 0}
        for (h, at, mask), (dim, send, recv, place) in self.hops.items():
            if at == step:
                count[h] += 1
                if part is None or (count[h] > 1) == (part == 1):
                    copy = links.copy(
                        self.half(mask, h), self.came(h, place), send, recv, seq=links.seq ^ dim
                    )
                    copy.start()
                    self.sent.append(copy)

    def fold(self, step):
        links = self.links
        for (h, at, mask), (dim, send, recv, place) in self.hops.items():
            if at != step:
                continue
            links.arrived(self.came(h, place), recv)
            if step < len(self.z.dims) - 1:
                half = self.half(mask ^ dim, h)
                half[...] = (half[...].astype(F32) + self.came(h, place)[...].astype(F32)).astype(BF16)
        if step < len(self.z.dims) - 1:
            self.send(step + 1)

    def total(self, write):
        last = len(self.z.dims) - 1
        for (h, at, mask), (dim, send, recv, place) in self.hops.items():
            if at == last:
                value = self.half(0, h)[...].astype(F32) + self.came(h, place)[...].astype(F32)
                write(halves(self.rows)[h], value)

    def drain(self):
        for copy in self.sent:
            copy.wait_send()


def slots_of(z):
    return Scatter(z, Links(None, 0, 0), None, None, None, 0).slots


def scratch_of(z):
    V = pltpu.VMEM
    half = z.S // 2
    slots = slots_of(z)
    return dict(
        tokg=V((z.S, z.R, z.Ds), BF16),
        halg=V((z.S, 16, z.Ds), BF16),
        hals=V((z.B, 16, z.Ds), BF16),
        db=V((z.S, z.R, z.Ds), BF16),
        inv=V((z.R, LANE), F32),
        normed=V((z.R + 16, z.D), BF16),
        normt=V((z.D, z.R), BF16),
        wx=V((2, z.D, z.C), BF16),
        wo=V((z.S, z.C, z.Ds), BF16),
        xpad=V((z.Q, 8 + z.T, z.C), F32),
        dcp=V((z.Q, z.T + 8, z.C), F32),
        conv=V((z.E, z.C), F32),
        s=V((z.E, z.C), F32),
        su=V((z.R, z.C), F32),
        fac=V((z.E, z.C), F32),
        zp=V((z.R, z.C), F32),
        rd=V((z.R, z.C), F32),
        dr=V((z.R, z.C), F32),
        u=V((z.R, z.C), BF16),
        gat=V((z.R, z.C), BF16),
        gatt=V((z.C, z.R), BF16),
        ddr=V((z.R, z.C), BF16),
        dzr=V((z.R, z.C), BF16),
        dxr=V((z.R, z.C), BF16),
        lowp=V((z.Q, z.M, z.T, z.RK), BF16),
        stp=V((z.Q, z.M, 2 * z.N, z.T), F32),
        low=V((z.R, z.RK), BF16),
        dlow=V((z.R, z.RK), BF16),
        dlowt=V((z.RK, z.R), BF16),
        dst=V((2 * z.N, z.R), BF16),
        st=V((2 * z.N, z.R), F32),
        blkb=V((z.R, GRP * z.N), BF16),
        blkk=V((z.R, GRP * z.N), BF16),
        blkc=V((z.R, GRP * z.N), BF16),
        bc=V((z.Q, z.T, 2 * z.N, LANE), F32),
        hist=V((z.Q * (z.T + 1) * z.N, z.C), BF16),
        gbuf=V((GRP * z.N, z.C), BF16),
        ghbuf=V((GRP * z.N, z.C), BF16),
        ptot=V((z.Q, z.N, z.C), F32),
        stot=V((z.Q, z.N, z.C), F32),
        ppre=V((z.Q, z.N, z.C), F32),
        spre=V((z.Q, z.N, z.C), F32),
        csend=V((z.levels, z.Q, 2, z.N, z.C), BF16),
        crecv=V((z.levels, z.Q, 2, z.N, z.C), BF16),
        bsend=V((z.levels, z.Q, z.N, z.C), BF16),
        brecv=V((z.levels, z.Q, z.N, z.C), BF16),
        est=V((3, z.N, z.R), F32),
        dlowp=V((z.Q, z.M, z.T, z.RK), BF16),
        dstp=V((z.Q, z.M, 2 * z.N, z.T), BF16),
        orecv=V((z.M - 1, z.R, z.Df), BF16),
        nrecv=V((z.M - 1, z.R, z.Df), BF16),
        near_o=V((half * z.C, z.Ds), BF16),
        sum_o=V((half * z.C, z.Ds), BF16),
        far_o=V((slots * (z.C // 2), z.Ds), BF16),
        near_i=V((half * z.Ds, z.C), BF16),
        sum_1=V((half * z.Ds, z.C), BF16),
        far_1=V((slots * (z.Ds // 2), z.C), BF16),
        vec=V((SGVEC, z.C), F32),
        gv=V((z.levels + 1, 8, z.D), F32),
        gvr=V((z.levels, 8, z.D), F32),
        gvm=V((z.M - 1, 8, z.D), F32),
        mrow=V((z.M, 8, z.R), F32),
        sems=pltpu.SemaphoreType.DMA((420,)),
        local=pltpu.SemaphoreType.DMA((8,)),
        ready=pltpu.SemaphoreType.REGULAR((z.levels,)),
    )


def silu_parts(value):
    gate = 1.0 / (1.0 + jnp.exp(-value))
    return gate, value * gate


def fused_kernel(z, names, *refs):
    r = Bunch(names, refs)
    seq, mp = lax.axis_index("seq"), lax.axis_index("mp")
    links = Links(r.sems, seq, mp)
    lanes_all = z.C // LANE
    first_block = mp * z.B

    def lane_loop(step):
        each(z.C // LANE, lambda index: step(cut(index * LANE, LANE)))

    local = r.local
    mine_in = lambda k: r.wx.at[k, cut(seq * z.Ds, z.Ds), :]
    loads = [
        pltpu.make_async_copy(r.win.at[0], mine_in(0), local.at[0]),
        pltpu.make_async_copy(r.win.at[1], mine_in(1), local.at[1]),
        pltpu.make_async_copy(r.wout, r.wo.at[seq], local.at[2]),
    ]
    for load in loads:
        load.start()
    for b in range(z.B):
        r.tokg[first_block + b] = r.tok[:, b * z.Ds : (b + 1) * z.Ds]
        tails = [
            r.tok[q * z.T + z.T - 16 : q * z.T + z.T, b * z.Ds : (b + 1) * z.Ds].astype(F32)[8:]
            for q in range(z.Q)
        ]
        r.hals[b] = jnp.concatenate(tails, axis=0).astype(BF16)

    barrier = pltpu.get_barrier_semaphore()
    ahead, behind = lax.rem(seq + 1, z.S), lax.rem(seq + z.S - 1, z.S)
    partners = [(seq ^ (1 << level), mp) for level in range(z.levels)] + [(ahead, mp), (behind, mp)]
    partners += [(seq, lax.rem(mp + away, z.M)) for away in range(1, z.M)]
    for partner in partners:
        pl.semaphore_signal(barrier, inc=1, device_id=partner, device_id_type=MESH)
    pl.semaphore_wait(barrier, len(partners))

    def of_in(k):
        def half(owner, h):
            return r.wx.at[k, cut(owner * z.Ds + h * (z.Ds // 2), z.Ds // 2), :]

        return TreeGather(z, links, half, lambda owner: r.wx.at[k, cut(owner * z.Ds, z.Ds), :])

    tree_x, tree_z = of_in(0), of_in(1)
    tree_o = TreeGather(
        z,
        links,
        lambda owner, h: r.wo.at[owner, pl.ds(h * (z.C // 2), z.C // 2), :],
        lambda owner: r.wo.at[owner],
    )
    line_t = LineGather(z, links, lambda owner: r.tokg.at[pl.ds(owner * z.B, z.B)])
    line_h = LineGather(z, links, lambda owner: r.halg.at[pl.ds(owner * z.B, z.B)])
    line_d = LineGather(z, links, lambda owner: r.db.at[pl.ds(owner * z.B, z.B)])
    depth = len(z.dims)

    hal_send, hal_recv = links.sem(), links.sem()
    hal_mine = r.halg.at[pl.ds(first_block, z.B)]
    hal = links.copy(r.hals, hal_mine, hal_send, hal_recv, seq=ahead)
    hal.start()
    line_t.step(0)
    loads[0].wait()
    tree_x.first()
    tree_x.second()

    def weight_of(q):
        total = jnp.float32(0.0)
        for group in range(r.groupw.shape[0]):
            total = total + jnp.where(r.seqg[q] == group, r.groupw[group], 0.0)
        return total

    seq_weight = [weight_of(q) for q in range(z.Q)]
    for q in range(z.Q):
        rows = pl.ds(q * z.T, z.T)
        for b in range(z.B):
            part = r.cot[rows, b * z.Ds : (b + 1) * z.Ds] * seq_weight[q]
            r.db[first_block + b, rows, :] = part.astype(BF16)

    links.arrived(hal_mine, hal_recv)
    line_h.step(0)
    line_t.step(1)
    tree_x.forward()
    loads[1].wait()
    tree_z.first()
    tree_z.second()
    line_h.step(1)
    for far in range(2, z.M):
        line_t.step(far)
        line_h.step(far)
    line_d.step(0)

    def add_squares(j, total):
        part = r.tokg[j].astype(F32)
        edge = r.halg[j].astype(F32)
        return (
            total[0] + jnp.sum(part * part, axis=1, keepdims=True),
            total[1] + jnp.sum(edge * edge, axis=1, keepdims=True),
        )

    squares = lax.fori_loop(
        0, z.S, add_squares, (jnp.zeros((z.R, 1), F32), jnp.zeros((16, 1), F32))
    )
    inv = lax.rsqrt(squares[0] * (1.0 / z.D) + EPSILON)
    inv_edge = lax.rsqrt(squares[1] * (1.0 / z.D) + EPSILON)
    r.inv[...] = jnp.broadcast_to(inv, (z.R, LANE))

    def norm_block(j):
        features = cut(j * z.Ds, z.Ds)
        gain = r.gain[:, features]
        normed = r.tokg[j].astype(F32) * wide(r.inv[...], z.Ds // LANE) * gain
        r.normed[: z.R, features] = normed.astype(BF16)
        edge = r.halg[j].astype(F32) * inv_edge * gain
        r.normed[z.R :, features] = edge.astype(BF16)
        r.normt[features, :] = normed.T.astype(BF16)

    each(z.S, norm_block)
    tree_x.settle()
    tree_x.finish()

    def x_chunk(index):
        lanes = cut(index * 256, 256)
        part = nn(r.normed[...], r.wx[0, :, lanes]).astype(BF16).astype(F32)
        for q in range(z.Q):
            edge = part[z.R + 8 * q : z.R + 8 * q + 8]
            r.xpad[q, 0:8, lanes] = jnp.where(seq > 0, edge, 0.0)
            r.xpad[q, 8 : 8 + z.T, lanes] = part[q * z.T : (q + 1) * z.T]

    each(z.C // 256, x_chunk)

    def rows_of(q):
        return pl.ds(q * z.T, z.T)

    def conv(q):
        def conv_lanes(lanes):
            total = jnp.broadcast_to(r.convb[:, lanes], (z.T, LANE))
            for tap in range(4):
                total = total + r.convw[tap : tap + 1, lanes] * r.xpad[q, 5 + tap : 5 + tap + z.T, lanes]
            r.conv[rows_of(q), lanes] = total
            r.u[rows_of(q), lanes] = silu_parts(total)[1].astype(BF16)

        lane_loop(conv_lanes)

    swap_low = [Swap(z, links, lambda slot, q=q: r.lowp.at[q, slot]) for q in range(z.Q)]
    swap_st = [Swap(z, links, lambda slot, q=q: r.stp.at[q, slot]) for q in range(z.Q)]
    low_mine = [r.lowp.at[q, z.M - 1] for q in range(z.Q)]
    st_mine = [r.stp.at[q, z.M - 1] for q in range(z.Q)]

    def project(q):
        u = r.u[rows_of(q), :]
        st_mine[q][...] = nt(r.statewt[...], u)
        swap_st[q].start(st_mine[q])
        low_mine[q][...] = nn(u, r.loww[...]).astype(BF16)
        swap_low[q].start(low_mine[q])

    rows_i = lax.broadcasted_iota(jnp.int32, (z.T, GRP * z.N), 0)
    cols_i = lax.broadcasted_iota(jnp.int32, (z.T, GRP * z.N), 1)
    diagonal = lax.rem(rows_i, GRP) == cols_i // z.N
    rep_n = lax.broadcasted_iota(jnp.int32, (2 * z.N, GRP * z.N), 0)
    rep_j = lax.rem(lax.broadcasted_iota(jnp.int32, (2 * z.N, GRP * z.N), 1), z.N)
    rep_b = (rep_n == rep_j).astype(BF16)
    rep_c = (rep_n == rep_j + z.N).astype(BF16)
    only_b = lax.broadcasted_iota(jnp.int32, (z.T, LANE), 1) < z.N

    def columns_of(value):
        return jnp.concatenate([value, jnp.zeros((LANE - 2 * z.N, z.T), F32)], axis=0).T

    def keys(q):
        swap_st[q].wait()
        st = r.stp[q, 0]
        for slot in range(1, z.M):
            st = st + r.stp[q, slot]
        r.st[:, rows_of(q)] = st

        def spread(index, turned):
            for j in range(16):
                r.bc[q, index * 16 + j] = jnp.broadcast_to(turned[:, j : j + 1], (2 * z.N, LANE))
            return pltpu.roll(turned, LANE - 16, 1)

        lax.fori_loop(0, z.T // 16, spread, st)
        swap_low[q].wait()
        low = r.lowp[q, 0].astype(F32)
        for slot in range(1, z.M):
            low = low + r.lowp[q, slot].astype(F32)
        low = low.astype(BF16)
        r.low[rows_of(q), :] = low
        nat = columns_of(st)
        nat16 = nat[:, : 2 * z.N].astype(BF16)
        key_sq = jnp.sum(jnp.where(only_b, nat * nat, 0.0), axis=1, keepdims=True)
        spread_b = jnp.where(diagonal, nn(nat16, rep_b), 0.0)
        r.blkb[rows_of(q), :] = spread_b.astype(BF16)
        r.blkk[rows_of(q), :] = (spread_b * spread_b).astype(BF16)
        r.blkc[rows_of(q), :] = jnp.where(diagonal, nn(nat16, rep_c), 0.0).astype(BF16)

        def raw_chunk(index):
            lanes = cut(index * 256, 256)
            r.s[rows_of(q), lanes] = nn(low, r.deltaw[:, lanes])

        each(z.C // 256, raw_chunk)

        def step_lanes(lanes):
            raw = r.s[rows_of(q), lanes] + r.dbias[:, lanes]
            beta = 1.0 / (1.0 + jnp.exp(-raw))
            scale = 1.0 / (1.0 + beta * key_sq)
            step = beta * scale
            r.s[rows_of(q), lanes] = step
            r.su[rows_of(q), lanes] = step * r.u[rows_of(q), lanes].astype(F32)
            r.fac[rows_of(q), lanes] = scale * step * (1.0 - beta)

        lane_loop(step_lanes)

    span = 512 if z.C % 512 == 0 else 256

    def token(q, t):
        return pl.ds(q * z.T + t, 1)

    def totals(q):
        def lane_part(index):
            lanes = cut(index * span, span)

            def tokens8(i, carry):
                product, state = carry
                for j in range(8):
                    row = token(q, i * 8 + j)
                    step, drive = r.s[row, lanes], r.su[row, lanes]
                    key = r.bc[q, i * 8 + j, : z.N, :]
                    decay = 1.0 - step * wide(key * key, span // LANE)
                    product = product * decay
                    state = decay * state + drive * wide(key, span // LANE)
                return product, state

            start = (jnp.ones((z.N, span), F32), jnp.zeros((z.N, span), F32))
            product, state = lax.fori_loop(0, z.T // 8, tokens8, start)
            r.ptot[q, :, lanes] = product
            r.stot[q, :, lanes] = state

        each(z.C // span, lane_part)

    carry_sems = [[(links.sem(), links.sem()) for q in range(z.Q)] for level in range(z.levels)]
    back_sems = [[(links.sem(), links.sem()) for q in range(z.Q)] for level in range(z.levels)]
    carry_copies = []

    def upper_at(level):
        return lax.rem(seq // (1 << level), 2) == 1

    def carry_send(level, q):
        r.csend[level, q, 0] = r.ptot[q].astype(BF16)
        r.csend[level, q, 1] = r.stot[q].astype(BF16)
        copy = links.copy(
            r.csend.at[level, q], r.crecv.at[level, q], *carry_sems[level][q], seq=seq ^ (1 << level)
        )
        copy.start()
        carry_copies.append(copy)

    def carry_take(level, q):
        links.arrived(r.crecv.at[level, q], carry_sems[level][q][1])
        upper = upper_at(level)
        other_p, other_s = r.crecv[level, q, 0].astype(F32), r.crecv[level, q, 1].astype(F32)
        mine_p, mine_s = r.ptot[q], r.stot[q]
        if level == 0:
            r.spre[q] = jnp.where(upper, other_s, 0.0)
            r.ppre[q] = jnp.where(upper, other_p, 1.0)
        else:
            pre_p, pre_s = r.ppre[q], r.spre[q]
            r.spre[q] = jnp.where(upper, pre_p * other_s + pre_s, pre_s)
            r.ppre[q] = jnp.where(upper, pre_p * other_p, pre_p)
        if level < z.levels - 1:
            r.stot[q] = jnp.where(upper, mine_p * other_s + mine_s, other_p * mine_s + other_s)
            r.ptot[q] = mine_p * other_p

    def back_send(level, q):
        r.bsend[level, q] = r.stot[q].astype(BF16)
        copy = links.copy(
            r.bsend.at[level, q], r.brecv.at[level, q], *back_sems[level][q], seq=seq ^ (1 << level)
        )
        copy.start()
        carry_copies.append(copy)

    def back_take(level, q):
        links.arrived(r.brecv.at[level, q], back_sems[level][q][1])
        upper = upper_at(level)
        other = r.brecv[level, q].astype(F32)
        other_p, mine_p = r.crecv[level, q, 0].astype(F32), r.csend[level, q, 0].astype(F32)
        mine = r.stot[q]
        if level == 0:
            r.spre[q] = jnp.where(upper, 0.0, other)
            r.ppre[q] = jnp.where(upper, 1.0, other_p)
        else:
            pre_p, pre = r.ppre[q], r.spre[q]
            r.spre[q] = jnp.where(upper, pre, pre + pre_p * other)
            r.ppre[q] = jnp.where(upper, pre_p, pre_p * other_p)
        if level < z.levels - 1:
            r.stot[q] = jnp.where(upper, other + other_p * mine, mine + mine_p * other)

    def past_rows(q, slot, count=1):
        return pl.ds(pl.multiple_of((q * (z.T + 1) + slot) * z.N, z.N), count * z.N)

    def walk(q):
        r.hist[past_rows(q, 0), :] = r.spre[q].astype(BF16)

        def lane_part(index):
            lanes = cut(index * span, span)

            def tokens8(i, state):
                for j in range(8):
                    row = token(q, i * 8 + j)
                    step, drive = r.s[row, lanes], r.su[row, lanes]
                    key = r.bc[q, i * 8 + j, : z.N, :]
                    decay = 1.0 - step * wide(key * key, span // LANE)
                    state = decay * state + drive * wide(key, span // LANE)
                    r.hist[past_rows(q, i * 8 + j + 1), lanes] = state.astype(BF16)
                return state

            lax.fori_loop(0, z.T // 8, tokens8, r.spre[q, :, lanes])

        each(z.C // span, lane_part)

        def read(i):
            rows = cut(q * z.T + i * GRP, GRP)
            past = r.hist[past_rows(q, i * GRP + 1, GRP), :]
            r.rd[rows, :] = nn(r.blkc[rows, :], past)

        each(z.T // GRP, read)

    conv(0)
    project(0)
    conv(1)
    project(1)
    tree_z.forward()
    loads[2].wait()
    tree_o.first()
    line_d.step(1)
    keys(0)
    totals(0)
    carry_send(0, 0)
    keys(1)
    totals(1)
    carry_send(0, 1)
    line_d.step(2)
    carry_take(0, 0)
    carry_send(1, 0)
    carry_take(0, 1)
    carry_send(1, 1)
    tree_o.second()
    tree_z.settle()
    tree_z.finish()

    def z_chunk(index):
        lanes = cut(index * 256, 256)
        r.zp[:, lanes] = nn(r.normed[: z.R, :], r.wx[1, :, lanes])

    each(z.C // 256, z_chunk)
    for level in range(1, z.levels):
        for q in range(z.Q):
            carry_take(level, q)
            if level < z.levels - 1:
                carry_send(level + 1, q)
    for far in range(3, z.M):
        line_d.step(far)
    walk(0)
    tree_o.forward()
    walk(1)
    tree_o.settle()
    tree_o.finish()

    r.dr[...] = nt(r.db[0], r.wo[0])

    def gated_grad(index):
        r.dr[...] += nt(r.db[index + 1], r.wo[index + 1])

    each(z.S - 1, gated_grad)
    r.vec[...] = jnp.zeros_like(r.vec)

    def gate_lanes(lanes):
        for q in range(z.Q):
            rows = rows_of(q)
            u = r.u[rows, lanes].astype(F32)
            out = r.rd[rows, lanes] + r.skip[:, lanes] * u
            part, grad = r.zp[rows, lanes], r.dr[rows, lanes]
            gate, silu = silu_parts(part)
            gated = out * silu
            r.gat[rows, lanes] = gated.astype(BF16)
            r.gatt[lanes, rows] = gated.T.astype(BF16)
            d_read = grad * silu
            r.dr[rows, lanes] = d_read
            r.dzr[rows, lanes] = (grad * out * gate * (1.0 + part * (1.0 - gate))).astype(BF16)
            r.vec[6:7, lanes] += jnp.sum(d_read * u, axis=0, keepdims=True)

    lane_loop(gate_lanes)

    swap_out = Swap(z, links, lambda slot: r.orecv.at[slot])

    def partial_of(owner):
        return r.normed.at[pl.ds(0, z.R), cut(owner * z.Df, z.Df)]

    def branch_to(index):
        away = index + 1
        owner = lax.rem(mp + away, z.M)
        for b in range(z.B):
            j = owner * z.B + b
            r.normed[: z.R, cut(j * z.Ds, z.Ds)] = nn(r.gat[...], r.wo[j]).astype(BF16)

        @pl.when(away < z.M)
        def _():
            swap_out.one(partial_of(owner), away).start()

    def into(near, term):
        def make(device, mask):
            block = near.block(mask // 2)
            block[...] = term(device).astype(BF16)
            return block

        return make

    def onto(sums, term):
        def add(device, mask):
            block = sums.block(mask // 2)
            block[...] = (term(device) + block[...].astype(F32)).astype(BF16)

        return add

    half_s, slots = z.S // 2, slots_of(z)
    sg_rows = z.rows_sg
    near_o, near_i = Rows(r.near_o, 0, z.C, half_s), Rows(r.near_i, 0, z.Ds, half_s)
    sum_o, far_o = Rows(r.sum_o, 0, z.C, half_s), Rows(r.far_o, 0, z.C // 2, slots)
    sum_1, far_1 = Rows(r.sum_1, 0, z.Ds, half_s), Rows(r.far_1, 0, z.Ds // 2, slots)
    sum_0 = Rows(r.hist, 0, z.Ds, half_s)
    far_0 = Rows(r.hist, sum_0.end, z.Ds // 2, slots)
    sum_s = Rows(r.hist, far_0.end, sg_rows, half_s)
    far_s = Rows(r.hist, sum_s.end, halves(sg_rows)[0][1], slots)
    sgp = Rows(r.hist, far_s.end, sg_rows, z.S)
    small = Rows(r.hist, sgp.end, sg_rows, z.S)
    scatter_o = Scatter(z, links, None, sum_o, far_o, z.C)
    scatter_1 = Scatter(z, links, None, sum_1, far_1, z.Ds)
    scatter_0 = Scatter(z, links, None, sum_0, far_0, z.Ds)
    scatter_s = Scatter(z, links, None, sum_s, far_s, sg_rows)
    term_o = lambda device: nn(r.gatt[...], r.db[device])
    term_1 = lambda device: nn(r.normt[cut(device * z.Ds, z.Ds), :], r.dzr[...])
    term_0 = lambda device: nn(r.normt[cut(device * z.Ds, z.Ds), :], r.dxr[...])

    def totals_back(q):
        def lane_part(index):
            lanes = cut(index * span, span)

            def tokens8(i, tail):
                for j in reversed(range(8)):
                    t = z.T - 8 - i * 8 + j
                    row = token(q, t)
                    step, grad = r.s[row, lanes], r.dr[row, lanes]
                    key, query = r.bc[q, t, : z.N, :], r.bc[q, t, z.N :, :]
                    decay = 1.0 - step * wide(key * key, span // LANE)
                    tail = decay * (grad * wide(query, span // LANE) + tail)
                return tail

            r.stot[q, :, lanes] = lax.fori_loop(0, z.T // 8, tokens8, jnp.zeros((z.N, span), F32))

        each(z.C // span, lane_part)

    lane_index = lax.broadcasted_iota(jnp.int32, (z.N, LANE), 1)

    def lane_sum(value):
        total = value[:, :LANE]
        for part in range(1, lanes_all):
            total = total + value[:, part * LANE : (part + 1) * LANE]
        return jnp.sum(total, axis=1, keepdims=True)

    def walk_back(q):
        def group(index, carry):
            tail, sum_gh, sum_g, sum_h = carry
            i = z.T // GRP - 1 - index
            for j in reversed(range(GRP)):
                t = i * GRP + j
                row = token(q, t)
                step, drive, grad = r.s[row, :], r.su[row, :], r.dr[row, :]
                key, query = r.bc[q, t, : z.N, :], r.bc[q, t, z.N :, :]
                before = r.hist[past_rows(q, t), :].astype(F32)
                now = r.hist[past_rows(q, t + 1), :].astype(F32)
                state_grad = grad * wide(query, lanes_all) + tail
                crossed = state_grad * before
                r.gbuf[j * z.N : (j + 1) * z.N, :] = state_grad.astype(BF16)
                r.ghbuf[j * z.N : (j + 1) * z.N, :] = crossed.astype(BF16)
                here = lane_index == t
                sum_gh = jnp.where(here, lane_sum(step * crossed), sum_gh)
                sum_g = jnp.where(here, lane_sum(drive * state_grad), sum_g)
                sum_h = jnp.where(here, lane_sum(grad * now), sum_h)
                tail = (1.0 - step * wide(key * key, lanes_all)) * state_grad
            rows = cut(q * z.T + i * GRP, GRP)
            r.rd[rows, :] = nn(r.blkb[rows, :], r.gbuf[...])
            r.zp[rows, :] = nn(r.blkk[rows, :], r.ghbuf[...])
            return tail, sum_gh, sum_g, sum_h

        zero = jnp.zeros((z.N, LANE), F32)
        _, sum_gh, sum_g, sum_h = lax.fori_loop(0, z.T // GRP, group, (r.spre[q], zero, zero, zero))
        columns = pl.ds(q * z.T, z.T)
        r.est[0, :, columns] = sum_gh
        r.est[1, :, columns] = sum_g
        r.est[2, :, columns] = sum_h

    def step_back(q):
        rows = rows_of(q)

        def step_lanes(lanes):
            sum_b, step = r.rd[rows, lanes], r.s[rows, lanes]
            d_step = r.u[rows, lanes].astype(F32) * sum_b - r.zp[rows, lanes]
            r.rd[rows, lanes] = step * sum_b
            d_raw = d_step * r.fac[rows, lanes]
            r.ddr[rows, lanes] = d_raw.astype(BF16)
            r.gat[rows, lanes] = (d_step * step * step).astype(BF16)
            r.vec[5:6, lanes] += jnp.sum(d_raw, axis=0, keepdims=True)

        lane_loop(step_lanes)

    swap_dlow = [Swap(z, links, lambda slot, q=q: r.dlowp.at[q, slot]) for q in range(z.Q)]
    swap_dst = [Swap(z, links, lambda slot, q=q: r.dstp.at[q, slot]) for q in range(z.Q)]
    dlow_mine = [r.dlowp.at[q, z.M - 1] for q in range(z.Q)]
    dst_mine = [r.dstp.at[q, z.M - 1] for q in range(z.Q)]

    def project_back(q):
        rows = rows_of(q)
        key_grad = nt(jnp.ones((16, z.C), BF16), r.gat[rows, :])[0:1]
        now = r.st[: z.N, rows]
        d_key = r.est[1, :, rows] - 2.0 * now * r.est[0, :, rows] - 2.0 * now * key_grad
        dst_mine[q][...] = jnp.concatenate([d_key, r.est[2, :, rows]], axis=0).astype(BF16)
        swap_dst[q].start(dst_mine[q])
        dlow_mine[q][...] = nt(r.ddr[rows, :], r.deltaw[...]).astype(BF16)
        swap_dlow[q].start(dlow_mine[q])

    def sums_back(q):
        rows = rows_of(q)
        swap_dlow[q].wait()
        swap_dst[q].wait()
        dlow = r.dlowp[q, 0].astype(F32)
        dst = r.dstp[q, 0].astype(F32)
        for slot in range(1, z.M):
            dlow = dlow + r.dlowp[q, slot].astype(F32)
            dst = dst + r.dstp[q, slot].astype(F32)
        r.dlow[rows, :] = dlow.astype(BF16)
        r.dlowt[:, rows] = dlow.T.astype(BF16)
        r.dst[:, rows] = dst.astype(BF16)
        dlow16, dst16 = dlow.astype(BF16), columns_of(dst)[:, : 2 * z.N].astype(BF16)

        def inputs_chunk(index):
            lanes = cut(index * 256, 256)
            r.su[rows, lanes] = nt(dlow16, r.loww[lanes, :]) + nn(dst16, r.statewt[:, lanes])

        each(z.C // 256, inputs_chunk)

    rim = [
        links.copy(
            r.dcp.at[q, pl.ds(0, 8), :],
            r.dcp.at[q, pl.ds(z.T, 8), :],
            links.sem(),
            links.sem(),
            seq=behind,
        )
        for q in range(z.Q)
    ]

    def conv_back(q):
        rows = rows_of(q)

        def conv_lanes(lanes):
            total = r.su[rows, lanes] + r.rd[rows, lanes] + r.skip[:, lanes] * r.dr[rows, lanes]
            value = r.conv[rows, lanes]
            gate = silu_parts(value)[0]
            d_conv = total * gate * (1.0 + value * (1.0 - gate))
            r.dcp[q, 0 : z.T, lanes] = d_conv
            r.vec[4:5, lanes] += jnp.sum(d_conv, axis=0, keepdims=True)
            for tap in range(4):
                r.vec[tap : tap + 1, lanes] += jnp.sum(
                    d_conv * r.xpad[q, 5 + tap : 5 + tap + z.T, lanes], axis=0, keepdims=True
                )

        lane_loop(conv_lanes)
        rim[q].start()

    def x_back(q):
        rim[q].wait_recv()

        def x_lanes(lanes):
            edge = r.dcp[q, z.T : z.T + 8, lanes]
            r.dcp[q, z.T : z.T + 8, lanes] = jnp.where(seq < z.S - 1, edge, 0.0)
            total = jnp.zeros((z.T, LANE), F32)
            for tap in range(4):
                total = total + r.convw[tap : tap + 1, lanes] * r.dcp[q, 3 - tap : 3 - tap + z.T, lanes]
            r.dxr[rows_of(q), lanes] = total.astype(BF16)

        lane_loop(x_lanes)

    scatter_o.first(into(near_o, term_o))
    scatter_o.second(onto(sum_o, term_o))
    scatter_o.send(0, 0)
    totals_back(0)
    back_send(0, 0)
    totals_back(1)
    back_send(0, 1)
    for level in range(z.levels):
        for q in range(z.Q):
            back_take(level, q)
            if level < z.levels - 1:
                back_send(level + 1, q)
        if level == 0:
            each(z.M, branch_to)
            scatter_1.first(into(near_i, term_1))
        if level == 1:
            scatter_o.send(0, 1)
            scatter_1.second(onto(sum_1, term_1))
    scatter_1.send(0)
    walk_back(0)
    step_back(0)
    project_back(0)
    walk_back(1)
    for level in range(z.levels):
        pl.semaphore_signal(
            r.ready.at[level], inc=1, device_id=(seq ^ (1 << level), mp), device_id_type=MESH
        )
    step_back(1)
    project_back(1)
    for step in range(depth - 1):
        scatter_o.fold(step)
    sums_back(0)
    conv_back(0)
    sums_back(1)
    conv_back(1)
    for step in range(depth - 1):
        scatter_1.fold(step)

    def put_small(first, value):
        count, at = value.shape[0], 0
        while at < count:
            block, inside = divmod(first + at, sg_rows)
            take = min(count - at, sg_rows - inside)
            sgp.block(block, inside, take)[...] = value[at : at + take].astype(BF16)
            at += take

    low_t = r.low[...].astype(F32).T.astype(BF16)
    put_small(0, nn(low_t, r.ddr[...]))
    put_small(z.RK, nn(r.dlowt[...], r.u[...]))
    put_small(2 * z.RK, nn(r.dst[...], r.u[...]))
    put_small(2 * z.RK + 2 * z.N, r.vec[...])
    used = 2 * z.RK + 2 * z.N + SGVEC
    if used < z.S * sg_rows:
        put_small(used, jnp.zeros((z.S * sg_rows - used, z.C), F32))
    x_back(0)
    x_back(1)

    for level in range(z.levels):
        pl.semaphore_wait(r.ready.at[level], 1)
    scatter_s.first(lambda device, mask: sgp.block(device))
    for copy in scatter_1.sent[: len(z.masks)]:
        copy.wait_send()
    scatter_1.sent = scatter_1.sent[len(z.masks) :]
    scatter_0.first(into(near_i, term_0))

    def add_small(device, mask):
        block = sum_s.block(mask // 2)
        block[...] = (block[...].astype(F32) + sgp.block(device)[...].astype(F32)).astype(BF16)

    scatter_s.second(add_small)
    scatter_s.send(0)
    scatter_0.second(onto(sum_0, term_0))
    scatter_0.send(0)

    swap_out.wait()
    for away in range(1, z.M):
        owner = lax.rem(mp + away, z.M)
        swap_out.one(partial_of(owner), away).wait_send()
    for b in range(z.B):
        features = slice(b * z.Ds, (b + 1) * z.Ds)
        total = r.normed[: z.R, cut((first_block + b) * z.Ds, z.Ds)].astype(F32)
        for slot in range(z.M - 1):
            total = total + r.orecv[slot, :, features].astype(F32)
        r.blk[:, features] = (r.tok[:, features].astype(F32) + total).astype(BF16)

    swap_n = Swap(z, links, lambda slot: r.nrecv.at[slot])

    def normed_to(index, means):
        away = index + 1
        owner = lax.rem(mp + away, z.M)
        for b in range(z.B):
            j = owner * z.B + b
            features = cut(j * z.Ds, z.Ds)
            part = nt(r.dxr[...], r.wx[0, features, :]) + nt(r.dzr[...], r.wx[1, features, :])
            r.normed[: z.R, features] = part.astype(BF16)
            scaled = part * r.tokg[j].astype(F32)
            by_gain = jnp.sum(scaled * wide(r.inv[...], z.Ds // LANE), axis=0, keepdims=True)
            r.gv[0, :, features] = jnp.broadcast_to(by_gain, (8, z.Ds))
            means = means + jnp.sum(scaled * r.gain[:, features], axis=1, keepdims=True)

        @pl.when(away < z.M)
        def _():
            swap_n.one(partial_of(owner), away).start()

        return means

    means = lax.fori_loop(0, z.M, normed_to, jnp.zeros((z.R, 1), F32))
    swap_m = Swap(z, links, lambda slot: r.mrow.at[slot])
    mean_mine = r.mrow.at[z.M - 1]
    mean_mine[...] = jnp.broadcast_to(means, (z.R, LANE)).T[0:8]
    swap_m.start(mean_mine)

    gain_copies = []
    for level in range(z.levels):
        copy = links.copy(
            r.gv.at[level], r.gvr.at[level], links.sem(), links.sem(), seq=seq ^ (1 << level)
        )
        copy.start()
        gain_copies.append(copy)
        if level < depth - 1:
            scatter_s.fold(level)
        copy.wait_recv()
        r.gv[level + 1] = r.gv[level] + r.gvr[level]
    swap_g = Swap(z, links, lambda slot: r.gvm.at[slot])
    swap_g.start(r.gv.at[z.levels])
    scatter_s.fold(depth - 1)

    def write_small(rows, value):
        small.block(seq, *rows)[...] = value.astype(BF16)

    scatter_s.total(write_small)
    tree_s = TreeGather(
        z,
        links,
        lambda owner, h: small.block(owner, *halves(sg_rows)[h]),
        small.block,
    )
    tree_s.first()
    tree_s.second()
    for step in range(depth - 1):
        scatter_0.fold(step)
    tree_s.forward()
    tree_s.settle()

    swap_m.wait()
    mean = r.mrow[0]
    for slot in range(1, z.M):
        mean = mean + r.mrow[slot]
    mean = wide(jnp.concatenate([mean] * (LANE // 8), axis=0).T * (1.0 / z.D), z.Ds // LANE)
    swap_n.wait()
    inv_wide = wide(r.inv[...], z.Ds // LANE)
    for b in range(z.B):
        j = first_block + b
        here = slice(b * z.Ds, (b + 1) * z.Ds)
        gain = r.gain[:, cut(j * z.Ds, z.Ds)]
        total = r.normed[: z.R, cut(j * z.Ds, z.Ds)].astype(F32)
        for slot in range(z.M - 1):
            total = total + r.nrecv[slot, :, here].astype(F32)
        x = r.tok[:, here].astype(F32)
        value = inv_wide * (total * gain) - x * (inv_wide * inv_wide * inv_wide) * mean
        for q in range(z.Q):
            rows = slice(q * z.T, (q + 1) * z.T)
            r.dtok[rows, here] = value[rows] + r.cot[rows, here] * seq_weight[q]

    last = depth - 1
    scatter_o.fold(last)

    def write_out(rows, value):
        r.dout[pl.ds(*rows), :] = value

    scatter_o.total(write_out)
    scatter_1.fold(last)

    def write_to(ref):
        def write(rows, value):
            ref[pl.ds(*rows), :] = value

        return write

    scatter_1.total(write_to(r.fac))
    store_1 = pltpu.make_async_copy(r.fac.at[pl.ds(0, z.Ds)], r.din.at[1], local.at[3])
    store_1.start()
    swap_g.wait()
    gains = r.gv[z.levels]
    for slot in range(z.M - 1):
        gains = gains + r.gvm[slot]
    r.dgain[...] = gains[0:1]
    tree_s.finish()
    for block in range(z.S):
        count = min(sg_rows, r.sg.shape[0] - block * sg_rows)
        if count > 0:
            r.sg[block * sg_rows : block * sg_rows + count, :] = small.block(block)[...].astype(F32)[:count]
    scatter_0.fold(last)
    scatter_0.total(write_to(r.s))
    store_0 = pltpu.make_async_copy(r.s.at[pl.ds(0, z.Ds)], r.din.at[0], local.at[4])
    store_0.start()

    hal.wait_send()
    for tree in (tree_x, tree_z, tree_o, tree_s):
        tree.drain()
    for line in (line_t, line_h, line_d):
        line.drain()
    for q in range(z.Q):
        swap_st[q].drain(st_mine[q])
        swap_low[q].drain(low_mine[q])
        swap_dlow[q].drain(dlow_mine[q])
        swap_dst[q].drain(dst_mine[q])
    swap_m.drain(mean_mine)
    swap_g.drain(r.gv.at[z.levels])
    for away in range(1, z.M):
        owner = lax.rem(mp + away, z.M)
        swap_n.one(partial_of(owner), away).wait_send()
    for copy in carry_copies + gain_copies + rim:
        copy.wait_send()
    for scatter in (scatter_o, scatter_1, scatter_0, scatter_s):
        scatter.drain()
    store_1.wait()
    store_0.wait()


def finish_kernel(z, blk, dtok, dgain, din, dout, sg, *outs):
    a, b, c = z.RK, 2 * z.RK, 2 * z.RK + 2 * z.N
    o_blk, o_dtok, o_dgain, o_din, o_convw, o_convb, o_low, o_state, o_delta, o_dbias, o_skip, o_dout, sems = outs
    copies = [
        pltpu.make_async_copy(src, dst, sems.at[index])
        for index, (src, dst) in enumerate([(din, o_din), (dout, o_dout), (dtok, o_dtok), (blk, o_blk)])
    ]
    for copy in copies:
        copy.start()
    o_dgain[...] = dgain[...]
    o_delta[...] = sg[0:a, :]
    o_convw[...] = sg[c : c + 4, :]
    o_convb[...] = sg[c + 4 : c + 5, :]
    o_dbias[...] = sg[c + 5 : c + 6, :]
    o_skip[...] = sg[c + 6 : c + 7, :]
    for at in range(0, z.C, LANE):
        o_low[at : at + LANE, :] = sg[a:b, at : at + LANE].T
        part = jnp.concatenate([sg[b:c, at : at + LANE], jnp.zeros((LANE - 2 * z.N, LANE), F32)], axis=0)
        o_state[at : at + LANE, :] = part.T[:, : 2 * z.N]
    for copy in copies:
        copy.wait()


def fused(z, tokens, norm_gain, in_weight, conv_weight, conv_bias, low_weight, state_weight, delta_weight,
          delta_bias, skip_gain, out_weight, cotangent, seq_group, group_weight):
    V = pl.BlockSpec(memory_space=pltpu.VMEM)
    A = pl.BlockSpec(memory_space=pl.ANY)
    SM = pl.BlockSpec(memory_space=pltpu.SMEM)
    row = lambda value: value.reshape(1, -1)
    operands = dict(
        tok=(V, tokens.reshape(z.R, z.Df)),
        cot=(V, cotangent.reshape(z.R, z.Df)),
        gain=(V, row(norm_gain)),
        win=(A, in_weight),
        wout=(A, out_weight),
        convw=(V, conv_weight),
        convb=(V, row(conv_bias)),
        dbias=(V, row(delta_bias)),
        skip=(V, row(skip_gain)),
        loww=(V, low_weight),
        statewt=(V, state_weight.T),
        deltaw=(V, delta_weight),
        seqg=(SM, seq_group),
        groupw=(SM, group_weight),
    )
    scratch = scratch_of(z)
    sg_used = 2 * z.RK + 2 * z.N + SGVEC
    outs = dict(
        blk=(V, (z.R, z.Df), BF16),
        dtok=(V, (z.R, z.Df), F32),
        dgain=(V, (1, z.D), F32),
        din=(A, (2, z.Ds, z.C), F32),
        dout=(V, (z.C, z.Ds), F32),
        sg=(V, (sg_used, z.C), F32),
    )
    result = pl.pallas_call(
        functools.partial(fused_kernel, z, [*operands, *outs, *scratch]),
        out_shape=[jax.ShapeDtypeStruct(shape, kind) for _, shape, kind in outs.values()],
        in_specs=[spec for spec, _ in operands.values()],
        out_specs=[spec for spec, _, _ in outs.values()],
        scratch_shapes=list(scratch.values()),
        compiler_params=pltpu.CompilerParams(
            collective_id=0, has_side_effects=True, vmem_limit_bytes=VMEM_BYTES
        ),
    )(*[value for _, value in operands.values()])
    whole = (V, (1, z.C), F32)
    last = dict(
        blk=(A, (z.R, z.Df), BF16),
        dtok=(A, (z.R, z.Df), F32),
        dgain=(V, (1, z.D), F32),
        din=(A, (2, z.Ds, z.C), F32),
        convw=(V, (4, z.C), F32),
        convb=whole,
        low=(V, (z.C, z.RK), F32),
        state=(V, (z.C, 2 * z.N), F32),
        delta=(V, (z.RK, z.C), F32),
        dbias=whole,
        skip=whole,
        dout=(A, (z.C, z.Ds), F32),
    )
    done = pl.pallas_call(
        functools.partial(finish_kernel, z),
        out_shape=[jax.ShapeDtypeStruct(shape, kind) for _, shape, kind in last.values()],
        in_specs=[A, A, V, A, A, V],
        out_specs=[spec for spec, _, _ in last.values()],
        scratch_shapes=[pltpu.SemaphoreType.DMA((4,))],
        compiler_params=pltpu.CompilerParams(vmem_limit_bytes=VMEM_BYTES),
    )(*result)
    shapes = [tokens.shape, tokens.shape, (z.D,), None, None, (z.C,), None, None, None, (z.C,), (z.C,), None]
    return tuple(value if shape is None else value.reshape(shape) for value, shape in zip(done, shapes))


def local(mesh_shape, *arrays):
    tokens, norm_gain, in_weight, conv_weight = arrays[:4]
    state_weight, delta_weight = arrays[6], arrays[7]
    z = Sizes(
        mesh_shape,
        tokens.shape[0],
        tokens.shape[1],
        tokens.shape[2],
        norm_gain.shape[0],
        in_weight.shape[2],
        state_weight.shape[1] // 2,
        delta_weight.shape[0],
    )
    if z.fits(conv_weight.shape[0]):
        return fused(z, *arrays)
    return plain(*arrays)


def solution(mesh):
    placed = (
        P(None, "seq", "mp"),
        P(),
        P(None, "seq", "mp"),
        P(None, "mp"),
        P("mp"),
        P("mp", None),
        P("mp", None),
        P(None, "mp"),
        P("mp"),
        P("mp"),
        P("mp", "seq"),
        P(None, "seq", "mp"),
        P(),
        P(),
    )
    return jax.shard_map(
        functools.partial(local, dict(mesh.shape)),
        mesh=mesh,
        in_specs=placed,
        out_specs=(
            P(None, "seq", "mp"),
            P(None, "seq", "mp"),
            P(),
            P(None, "seq", "mp"),
            P(None, "mp"),
            P("mp"),
            P("mp", None),
            P("mp", None),
            P(None, "mp"),
            P("mp"),
            P("mp"),
            P("mp", "seq"),
        ),
        check_vma=False,
    )
```

time: 228 us -> 293 us (1.29)
  Pallas kernels: 214 us -> 290 us
  local copies, waits for them, and re-layouts: 12.6 us -> 1.87 us
    pallas_call x1 -> x2, Pallas kernels: 214 us -> 290 us  [the longest x1 167 us: fused(): pl.pallas_call(functools.partial(fused_kernel, z, [*operands, *outs, *scr...]
    slice x3 -> x0, local copies, waits for them, and re-layouts: 4.97 us -> none  [the longest x1 2.13 us: fused(): sg[:a]]
    unnamed x16 -> x1, local copies, waits for them, and re-layouts: 6.03 us -> 1.87 us
where the time goes in v2:
time: 293 us; the launch traced here: 292 us
  Pallas kernels  290 us (99%)
    pallas_call x1, Pallas kernels, fused(): pl.pallas_call(functools.partial(fused_kernel, z, [*operands, *outs, *scr...  167 us
    pallas_call x1, Pallas kernels, fused(): pl.pallas_call(functools.partial(finish_kernel, z), out_shape=[jax.ShapeD...  123 us

profile of v2, /device:TPU:0, one launch (start us, length us, event | category | flops | bytes accessed | tf_op | source)
XLA Modules:
  0.0 292.4 jit_solution(11601199906713105545)
XLA Ops:
  0.6 167.1 %shard_map.229 = (bf16[256,512]{1,0:T(8,128)(2,1)}, f32[256,512]{1,0:T(8,128)}, f32[1,2048]{1,0:T(1,128)}, f32[2,256,1024]{2,1,0:T(8,128)}, f32[1024,256]{1,0:T(8,128)}, /*index=5*/f32[304,1024]{1,0:T(8,128)}) custom-call(bf16[256,512]{1,0:T(8,128)(2,1)} %bitcast.14, f32[256,512]{1,0:T(8,128)} %bitcast.13, f32[1,2048]{1,0:T(1,128)} %bitcast.16, ...), custom_call_target="tpu_custom_call" | custom-call | tf_op jit(solution)/shard_map/pallas_call | solution.py:1557
  167.8 122.7 %shard_map.230 = (bf16[256,512]{1,0:T(8,128)(2,1)}, f32[256,512]{1,0:T(8,128)}, f32[1,2048]{1,0:T(1,128)}, f32[2,256,1024]{2,1,0:T(8,128)}, f32[4,1024]{1,0:T(4,...) custom-call(bf16[256,512]{1,0:T(8,128)(2,1)} %get-tuple-element.30.b, ...), custom_call_target="tpu_custom_call" | custom-call | tf_op jit(solution)/shard_map/pallas_call | solution.py:1582
  290.5 1.9 copy.26

commit v3 on v2

--- a/solution.py
+++ b/solution.py
@@ -336,8 +336,17 @@
     lax.fori_loop(0, count, lambda index, unused: (step(index), unused)[1], 0)
 
 
+def by_rows(count, step):
+    size = 32 if count % 32 == 0 else 16
+    each(count // size, lambda index: step(cut(index * size, size)))
+
+
 def wide(value, times):
     return jnp.concatenate([value] * times, axis=1) if times > 1 else value
+
+
+def groups_fit(channels):
+    return (LANE // GRP) % min(LANE // GRP, channels // (GRP * GRP)) == 0
 
 
 class Sizes:
@@ -364,12 +373,14 @@
             and self.M > 1
             and self.Q == 2
             and self.T == LANE
-            and self.Ds % 256 == 0
+            and self.Ds == 256
             and self.Df % self.Ds == 0
-            and self.C % 256 == 0
+            and self.C % 512 == 0
             and self.N == GRP
             and self.RK == LANE
             and taps == 4
+            and self.D >= 2 * self.C
+            and groups_fit(self.C)
             and self.C * self.D <= (1 << 21)
         )
 
@@ -529,6 +540,27 @@
     def drain(self, src):
         for away in range(1, self.z.M):
             self.one(src, away).wait_send()
+
+
+class SwapSeq:
+    def __init__(self, z, links, slot):
+        self.links, self.slot = links, slot
+        self.pairs = [(other, links.sem(), links.sem()) for other in range(1, z.S)]
+        self.sent = []
+
+    def start(self, src):
+        for other, send, recv in self.pairs:
+            copy = self.links.copy(src, self.slot(other - 1), send, recv, seq=self.links.seq ^ other)
+            copy.start()
+            self.sent.append(copy)
+
+    def wait(self):
+        for other, send, recv in self.pairs:
+            self.links.arrived(self.slot(other - 1), recv)
+
+    def drain(self):
+        for copy in self.sent:
+            copy.wait_send()
 
 
 def halves(rows):
@@ -595,8 +627,12 @@
                 continue
             links.arrived(self.came(h, place), recv)
             if step < len(self.z.dims) - 1:
-                half = self.half(mask ^ dim, h)
-                half[...] = (half[...].astype(F32) + self.came(h, place)[...].astype(F32)).astype(BF16)
+                half, came = self.half(mask ^ dim, h), self.came(h, place)
+
+                def add(rows):
+                    half[rows, :] = (half[rows, :].astype(F32) + came[rows, :].astype(F32)).astype(BF16)
+
+                by_rows(halves(self.rows)[h][1], add)
         if step < len(self.z.dims) - 1:
             self.send(step + 1)
 
@@ -604,8 +640,14 @@
         last = len(self.z.dims) - 1
         for (h, at, mask), (dim, send, recv, place) in self.hops.items():
             if at == last:
-                value = self.half(0, h)[...].astype(F32) + self.came(h, place)[...].astype(F32)
-                write(halves(self.rows)[h], value)
+                half, came = self.half(0, h), self.came(h, place)
+                first, count = halves(self.rows)[h]
+
+                def add(rows):
+                    value = half[rows, :].astype(F32) + came[rows, :].astype(F32)
+                    write(pl.ds(pl.multiple_of(first + rows.start, 16), rows.size), value)
+
+                by_rows(count, add)
 
     def drain(self):
         for copy in self.sent:
@@ -624,12 +666,12 @@
         tokg=V((z.S, z.R, z.Ds), BF16),
         halg=V((z.S, 16, z.Ds), BF16),
         hals=V((z.B, 16, z.Ds), BF16),
-        db=V((z.S, z.R, z.Ds), BF16),
+        db=V((z.R, z.D), BF16),
         inv=V((z.R, LANE), F32),
         normed=V((z.R + 16, z.D), BF16),
         normt=V((z.D, z.R), BF16),
         wx=V((2, z.D, z.C), BF16),
-        wo=V((z.S, z.C, z.Ds), BF16),
+        wo=V((z.C, z.D), BF16),
         xpad=V((z.Q, 8 + z.T, z.C), F32),
         dcp=V((z.Q, z.T + 8, z.C), F32),
         conv=V((z.E, z.C), F32),
@@ -657,8 +699,6 @@
         blkc=V((z.R, GRP * z.N), BF16),
         bc=V((z.Q, z.T, 2 * z.N, LANE), F32),
         hist=V((z.Q * (z.T + 1) * z.N, z.C), BF16),
-        gbuf=V((GRP * z.N, z.C), BF16),
-        ghbuf=V((GRP * z.N, z.C), BF16),
         ptot=V((z.Q, z.N, z.C), F32),
         stot=V((z.Q, z.N, z.C), F32),
         ppre=V((z.Q, z.N, z.C), F32),
@@ -679,9 +719,11 @@
         sum_1=V((half * z.Ds, z.C), BF16),
         far_1=V((slots * (z.Ds // 2), z.C), BF16),
         vec=V((SGVEC, z.C), F32),
-        gv=V((z.levels + 1, 8, z.D), F32),
-        gvr=V((z.levels, 8, z.D), F32),
-        gvm=V((z.M - 1, 8, z.D), F32),
+        gv=V((z.D // LANE, LANE), F32),
+        gvs=V((z.D // LANE, LANE), F32),
+        gvr=V((z.S - 1, z.D // LANE, LANE), F32),
+        gvm=V((z.M - 1, z.D // LANE, LANE), F32),
+        mean=V((z.R, LANE), F32),
         mrow=V((z.M, 8, z.R), F32),
         sems=pltpu.SemaphoreType.DMA((420,)),
         local=pltpu.SemaphoreType.DMA((8,)),
@@ -709,7 +751,7 @@
     loads = [
         pltpu.make_async_copy(r.win.at[0], mine_in(0), local.at[0]),
         pltpu.make_async_copy(r.win.at[1], mine_in(1), local.at[1]),
-        pltpu.make_async_copy(r.wout, r.wo.at[seq], local.at[2]),
+        pltpu.make_async_copy(r.wout, r.wo.at[:, cut(seq * z.Ds, z.Ds)], local.at[2]),
     ]
     for load in loads:
         load.start()
@@ -723,7 +765,7 @@
 
     barrier = pltpu.get_barrier_semaphore()
     ahead, behind = lax.rem(seq + 1, z.S), lax.rem(seq + z.S - 1, z.S)
-    partners = [(seq ^ (1 << level), mp) for level in range(z.levels)] + [(ahead, mp), (behind, mp)]
+    partners = [(seq ^ other, mp) for other in range(1, z.S)] + [(ahead, mp), (behind, mp)]
     partners += [(seq, lax.rem(mp + away, z.M)) for away in range(1, z.M)]
     for partner in partners:
         pl.semaphore_signal(barrier, inc=1, device_id=partner, device_id_type=MESH)
@@ -739,12 +781,12 @@
     tree_o = TreeGather(
         z,
         links,
-        lambda owner, h: r.wo.at[owner, pl.ds(h * (z.C // 2), z.C // 2), :],
-        lambda owner: r.wo.at[owner],
+        lambda owner, h: r.wo.at[pl.ds(h * (z.C // 2), z.C // 2), cut(owner * z.Ds, z.Ds)],
+        lambda owner: r.wo.at[:, cut(owner * z.Ds, z.Ds)],
     )
     line_t = LineGather(z, links, lambda owner: r.tokg.at[pl.ds(owner * z.B, z.B)])
     line_h = LineGather(z, links, lambda owner: r.halg.at[pl.ds(owner * z.B, z.B)])
-    line_d = LineGather(z, links, lambda owner: r.db.at[pl.ds(owner * z.B, z.B)])
+    line_d = LineGather(z, links, lambda owner: r.db.at[:, cut(owner * z.Df, z.Df)])
     depth = len(z.dims)
 
     hal_send, hal_recv = links.sem(), links.sem()
@@ -767,7 +809,7 @@
         rows = pl.ds(q * z.T, z.T)
         for b in range(z.B):
             part = r.cot[rows, b * z.Ds : (b + 1) * z.Ds] * seq_weight[q]
-            r.db[first_block + b, rows, :] = part.astype(BF16)
+            r.db[rows, cut((first_block + b) * z.Ds, z.Ds)] = part.astype(BF16)
 
     links.arrived(hal_mine, hal_recv)
     line_h.step(0)
@@ -780,7 +822,6 @@
     for far in range(2, z.M):
         line_t.step(far)
         line_h.step(far)
-    line_d.step(0)
 
     def add_squares(j, total):
         part = r.tokg[j].astype(F32)
@@ -864,34 +905,24 @@
             st = st + r.stp[q, slot]
         r.st[:, rows_of(q)] = st
 
-        def spread(index, turned):
-            for j in range(16):
-                r.bc[q, index * 16 + j] = jnp.broadcast_to(turned[:, j : j + 1], (2 * z.N, LANE))
-            return pltpu.roll(turned, LANE - 16, 1)
-
-        lax.fori_loop(0, z.T // 16, spread, st)
+        def spread(index):
+            turned = pltpu.roll(st, lax.rem(z.T - index * 32, z.T), 1)
+            for j in range(32):
+                r.bc[q, index * 32 + j] = jnp.broadcast_to(turned[:, j : j + 1], (2 * z.N, LANE))
+
+        each(z.T // 32, spread)
+        nat = columns_of(st)
+        key_sq = jnp.sum(jnp.where(only_b, nat * nat, 0.0), axis=1, keepdims=True)
         swap_low[q].wait()
         low = r.lowp[q, 0].astype(F32)
         for slot in range(1, z.M):
             low = low + r.lowp[q, slot].astype(F32)
         low = low.astype(BF16)
         r.low[rows_of(q), :] = low
-        nat = columns_of(st)
-        nat16 = nat[:, : 2 * z.N].astype(BF16)
-        key_sq = jnp.sum(jnp.where(only_b, nat * nat, 0.0), axis=1, keepdims=True)
-        spread_b = jnp.where(diagonal, nn(nat16, rep_b), 0.0)
-        r.blkb[rows_of(q), :] = spread_b.astype(BF16)
-        r.blkk[rows_of(q), :] = (spread_b * spread_b).astype(BF16)
-        r.blkc[rows_of(q), :] = jnp.where(diagonal, nn(nat16, rep_c), 0.0).astype(BF16)
-
-        def raw_chunk(index):
+
+        def step_chunk(index):
             lanes = cut(index * 256, 256)
-            r.s[rows_of(q), lanes] = nn(low, r.deltaw[:, lanes])
-
-        each(z.C // 256, raw_chunk)
-
-        def step_lanes(lanes):
-            raw = r.s[rows_of(q), lanes] + r.dbias[:, lanes]
+            raw = nn(low, r.deltaw[:, lanes]) + r.dbias[:, lanes]
             beta = 1.0 / (1.0 + jnp.exp(-raw))
             scale = 1.0 / (1.0 + beta * key_sq)
             step = beta * scale
@@ -899,7 +930,14 @@
             r.su[rows_of(q), lanes] = step * r.u[rows_of(q), lanes].astype(F32)
             r.fac[rows_of(q), lanes] = scale * step * (1.0 - beta)
 
-        lane_loop(step_lanes)
+        each(z.C // 256, step_chunk)
+
+    def key_blocks(q):
+        nat16 = columns_of(r.st[:, rows_of(q)])[:, : 2 * z.N].astype(BF16)
+        spread_b = jnp.where(diagonal, nn(nat16, rep_b), 0.0)
+        r.blkb[rows_of(q), :] = spread_b.astype(BF16)
+        r.blkk[rows_of(q), :] = (spread_b * spread_b).astype(BF16)
+        r.blkc[rows_of(q), :] = jnp.where(diagonal, nn(nat16, rep_c), 0.0).astype(BF16)
 
     span = 512 if z.C % 512 == 0 else 256
 
@@ -987,6 +1025,8 @@
     def past_rows(q, slot, count=1):
         return pl.ds(pl.multiple_of((q * (z.T + 1) + slot) * z.N, z.N), count * z.N)
 
+    groups = z.T // GRP
+
     def walk(q):
         r.hist[past_rows(q, 0), :] = r.spre[q].astype(BF16)
 
@@ -1006,61 +1046,62 @@
             lax.fori_loop(0, z.T // 8, tokens8, r.spre[q, :, lanes])
 
         each(z.C // span, lane_part)
-
-        def read(i):
-            rows = cut(q * z.T + i * GRP, GRP)
-            past = r.hist[past_rows(q, i * GRP + 1, GRP), :]
-            r.rd[rows, :] = nn(r.blkc[rows, :], past)
-
-        each(z.T // GRP, read)
+        reads = []
+        for i in range(groups):
+            rows = pl.ds(q * z.T + i * GRP, GRP)
+            reads.append((rows, nn(r.blkc[rows, :], r.hist[past_rows(q, i * GRP + 1, GRP), :])))
+        for rows, value in reads:
+            r.rd[rows, :] = value
+
+    def z_chunk(index):
+        lanes = cut(index * 256, 256)
+        r.zp[:, lanes] = nn(r.normed[: z.R, :], r.wx[1, :, lanes])
 
     conv(0)
     project(0)
     conv(1)
     project(1)
+    line_d.step(0)
     tree_z.forward()
     loads[2].wait()
     tree_o.first()
-    line_d.step(1)
     keys(0)
     totals(0)
     carry_send(0, 0)
+    line_d.step(1)
     keys(1)
+    carry_take(0, 0)
+    carry_send(1, 0)
     totals(1)
     carry_send(0, 1)
-    line_d.step(2)
-    carry_take(0, 0)
-    carry_send(1, 0)
-    carry_take(0, 1)
-    carry_send(1, 1)
-    tree_o.second()
-    tree_z.settle()
-    tree_z.finish()
-
-    def z_chunk(index):
-        lanes = cut(index * 256, 256)
-        r.zp[:, lanes] = nn(r.normed[: z.R, :], r.wx[1, :, lanes])
-
-    each(z.C // 256, z_chunk)
     for level in range(1, z.levels):
-        for q in range(z.Q):
-            carry_take(level, q)
-            if level < z.levels - 1:
-                carry_send(level + 1, q)
+        carry_take(level, 0)
+        if level < z.levels - 1:
+            carry_send(level + 1, 0)
+        carry_take(level - 1, 1)
+        carry_send(level, 1)
+        if level == 1:
+            tree_o.second()
+            line_d.step(2)
+            tree_z.settle()
+            key_blocks(0)
+            key_blocks(1)
+            tree_z.finish()
+            each(z.C // 256, z_chunk)
+    tree_o.forward()
+    walk(0)
+    carry_take(z.levels - 1, 1)
     for far in range(3, z.M):
         line_d.step(far)
-    walk(0)
-    tree_o.forward()
     walk(1)
     tree_o.settle()
     tree_o.finish()
 
-    r.dr[...] = nt(r.db[0], r.wo[0])
-
     def gated_grad(index):
-        r.dr[...] += nt(r.db[index + 1], r.wo[index + 1])
-
-    each(z.S - 1, gated_grad)
+        lanes = cut(index * 256, 256)
+        r.dr[:, lanes] = nt(r.db[...], r.wo[lanes, :])
+
+    each(z.C // 256, gated_grad)
     r.vec[...] = jnp.zeros_like(r.vec)
 
     def gate_lanes(lanes):
@@ -1090,7 +1131,7 @@
         owner = lax.rem(mp + away, z.M)
         for b in range(z.B):
             j = owner * z.B + b
-            r.normed[: z.R, cut(j * z.Ds, z.Ds)] = nn(r.gat[...], r.wo[j]).astype(BF16)
+            r.normed[: z.R, cut(j * z.Ds, z.Ds)] = nn(r.gat[...], r.wo[:, cut(j * z.Ds, z.Ds)]).astype(BF16)
 
         @pl.when(away < z.M)
         def _():
@@ -1126,7 +1167,7 @@
     scatter_1 = Scatter(z, links, None, sum_1, far_1, z.Ds)
     scatter_0 = Scatter(z, links, None, sum_0, far_0, z.Ds)
     scatter_s = Scatter(z, links, None, sum_s, far_s, sg_rows)
-    term_o = lambda device: nn(r.gatt[...], r.db[device])
+    term_o = lambda device: nn(r.gatt[...], r.db[:, cut(device * z.Ds, z.Ds)])
     term_1 = lambda device: nn(r.normt[cut(device * z.Ds, z.Ds), :], r.dzr[...])
     term_0 = lambda device: nn(r.normt[cut(device * z.Ds, z.Ds), :], r.dxr[...])
 
@@ -1156,10 +1197,12 @@
             total = total + value[:, part * LANE : (part + 1) * LANE]
         return jnp.sum(total, axis=1, keepdims=True)
 
+    batch = min(groups, z.C // (GRP * z.N))
+
     def walk_back(q):
         def group(index, carry):
             tail, sum_gh, sum_g, sum_h = carry
-            i = z.T // GRP - 1 - index
+            i = groups - 1 - index
             for j in reversed(range(GRP)):
                 t = i * GRP + j
                 row = token(q, t)
@@ -1169,24 +1212,37 @@
                 now = r.hist[past_rows(q, t + 1), :].astype(F32)
                 state_grad = grad * wide(query, lanes_all) + tail
                 crossed = state_grad * before
-                r.gbuf[j * z.N : (j + 1) * z.N, :] = state_grad.astype(BF16)
-                r.ghbuf[j * z.N : (j + 1) * z.N, :] = crossed.astype(BF16)
+                place = pl.ds(pl.multiple_of(lax.rem(i, batch) * GRP * z.N + j * z.N, z.N), z.N)
+                r.wo[place, : z.C] = state_grad.astype(BF16)
+                r.wo[place, z.C : 2 * z.C] = crossed.astype(BF16)
                 here = lane_index == t
                 sum_gh = jnp.where(here, lane_sum(step * crossed), sum_gh)
                 sum_g = jnp.where(here, lane_sum(drive * state_grad), sum_g)
                 sum_h = jnp.where(here, lane_sum(grad * now), sum_h)
                 tail = (1.0 - step * wide(key * key, lanes_all)) * state_grad
-            rows = cut(q * z.T + i * GRP, GRP)
-            r.rd[rows, :] = nn(r.blkb[rows, :], r.gbuf[...])
-            r.zp[rows, :] = nn(r.blkk[rows, :], r.ghbuf[...])
             return tail, sum_gh, sum_g, sum_h
 
         zero = jnp.zeros((z.N, LANE), F32)
-        _, sum_gh, sum_g, sum_h = lax.fori_loop(0, z.T // GRP, group, (r.spre[q], zero, zero, zero))
-        columns = pl.ds(q * z.T, z.T)
-        r.est[0, :, columns] = sum_gh
-        r.est[1, :, columns] = sum_g
-        r.est[2, :, columns] = sum_h
+        carry = (r.spre[q], zero, zero, zero)
+        for start in range(0, groups, batch):
+            carry = lax.fori_loop(start, start + batch, group, carry)
+            sums = []
+            for slot in range(batch):
+                rows = pl.ds(q * z.T + (groups - start - batch + slot) * GRP, GRP)
+                place = pl.ds(slot * GRP * z.N, GRP * z.N)
+                sums.append(
+                    (
+                        rows,
+                        nn(r.blkb[rows, :], r.wo[place, : z.C]),
+                        nn(r.blkk[rows, :], r.wo[place, z.C : 2 * z.C]),
+                    )
+                )
+            for rows, by_key, by_square in sums:
+                r.rd[rows, :] = by_key
+                r.zp[rows, :] = by_square
+        columns = rows_of(q)
+        for part in range(3):
+            r.est[part, :, columns] = carry[1 + part]
 
     def step_back(q):
         rows = rows_of(q)
@@ -1280,27 +1336,35 @@
         lane_loop(x_lanes)
 
     scatter_o.first(into(near_o, term_o))
-    scatter_o.second(onto(sum_o, term_o))
-    scatter_o.send(0, 0)
     totals_back(0)
     back_send(0, 0)
+    scatter_o.second(onto(sum_o, term_o))
+    back_take(0, 0)
+    back_send(1, 0)
     totals_back(1)
     back_send(0, 1)
-    for level in range(z.levels):
-        for q in range(z.Q):
-            back_take(level, q)
-            if level < z.levels - 1:
-                back_send(level + 1, q)
-        if level == 0:
+    for level in range(1, z.levels):
+        back_take(level, 0)
+        if level < z.levels - 1:
+            back_send(level + 1, 0)
+        back_take(level - 1, 1)
+        back_send(level, 1)
+        if level == 1:
             each(z.M, branch_to)
             scatter_1.first(into(near_i, term_1))
-        if level == 1:
-            scatter_o.send(0, 1)
-            scatter_1.second(onto(sum_1, term_1))
+    scatter_o.send(0)
+    back_take(z.levels - 1, 1)
+    scatter_1.second(onto(sum_1, term_1))
     scatter_1.send(0)
+    for copy in scatter_1.sent[: len(z.masks)]:
+        copy.wait_send()
+    scatter_1.sent = scatter_1.sent[len(z.masks) :]
+    tree_o.drain()
     walk_back(0)
     step_back(0)
     project_back(0)
+    for step in range(depth - 1):
+        scatter_o.fold(step)
     walk_back(1)
     for level in range(z.levels):
         pl.semaphore_signal(
@@ -1308,61 +1372,76 @@
         )
     step_back(1)
     project_back(1)
-    for step in range(depth - 1):
-        scatter_o.fold(step)
     sums_back(0)
     conv_back(0)
+    for step in range(depth - 1):
+        scatter_1.fold(step)
+
+    last = depth - 1
+    scatter_o.fold(last)
+
+    def write_to(ref):
+        def write(rows, value):
+            ref[rows, :] = value
+
+        return write
+
+    scatter_o.total(write_to(r.dout))
+    swap_out.wait()
+    for away in range(1, z.M):
+        owner = lax.rem(mp + away, z.M)
+        swap_out.one(partial_of(owner), away).wait_send()
+
+    def block_lanes(index):
+        here = cut(index * LANE, LANE)
+        total = r.normed[: z.R, cut(mp * z.Df + index * LANE, LANE)].astype(F32)
+        for slot in range(z.M - 1):
+            total = total + r.orecv[slot, :, here].astype(F32)
+        r.blk[:, here] = (r.tok[:, here].astype(F32) + total).astype(BF16)
+
+    each(z.Df // LANE, block_lanes)
     sums_back(1)
     conv_back(1)
-    for step in range(depth - 1):
-        scatter_1.fold(step)
-
-    def put_small(first, value):
+
+    def put_small(first, lanes, value):
         count, at = value.shape[0], 0
         while at < count:
             block, inside = divmod(first + at, sg_rows)
             take = min(count - at, sg_rows - inside)
-            sgp.block(block, inside, take)[...] = value[at : at + take].astype(BF16)
+            sgp.block(block, inside, take)[:, lanes] = value[at : at + take].astype(BF16)
             at += take
 
     low_t = r.low[...].astype(F32).T.astype(BF16)
-    put_small(0, nn(low_t, r.ddr[...]))
-    put_small(z.RK, nn(r.dlowt[...], r.u[...]))
-    put_small(2 * z.RK, nn(r.dst[...], r.u[...]))
-    put_small(2 * z.RK + 2 * z.N, r.vec[...])
     used = 2 * z.RK + 2 * z.N + SGVEC
-    if used < z.S * sg_rows:
-        put_small(used, jnp.zeros((z.S * sg_rows - used, z.C), F32))
-    x_back(0)
-    x_back(1)
-
+
+    def small_chunk(index):
+        lanes = cut(index * 256, 256)
+        put_small(0, lanes, nn(low_t, r.ddr[:, lanes]))
+        put_small(z.RK, lanes, nn(r.dlowt[...], r.u[:, lanes]))
+        put_small(2 * z.RK, lanes, nn(r.dst[...], r.u[:, lanes]))
+        put_small(2 * z.RK + 2 * z.N, lanes, r.vec[:, lanes])
+        if used < z.S * sg_rows:
+            put_small(used, lanes, jnp.zeros((z.S * sg_rows - used, 256), F32))
+
+    each(z.C // 256, small_chunk)
     for level in range(z.levels):
         pl.semaphore_wait(r.ready.at[level], 1)
     scatter_s.first(lambda device, mask: sgp.block(device))
-    for copy in scatter_1.sent[: len(z.masks)]:
-        copy.wait_send()
-    scatter_1.sent = scatter_1.sent[len(z.masks) :]
+    x_back(0)
+    x_back(1)
+
     scatter_0.first(into(near_i, term_0))
 
     def add_small(device, mask):
-        block = sum_s.block(mask // 2)
-        block[...] = (block[...].astype(F32) + sgp.block(device)[...].astype(F32)).astype(BF16)
+        block, term = sum_s.block(mask // 2), sgp.block(device)
+
+        def one(rows):
+            block[rows, :] = (block[rows, :].astype(F32) + term[rows, :].astype(F32)).astype(BF16)
+
+        by_rows(sg_rows, one)
 
     scatter_s.second(add_small)
     scatter_s.send(0)
-    scatter_0.second(onto(sum_0, term_0))
-    scatter_0.send(0)
-
-    swap_out.wait()
-    for away in range(1, z.M):
-        owner = lax.rem(mp + away, z.M)
-        swap_out.one(partial_of(owner), away).wait_send()
-    for b in range(z.B):
-        features = slice(b * z.Ds, (b + 1) * z.Ds)
-        total = r.normed[: z.R, cut((first_block + b) * z.Ds, z.Ds)].astype(F32)
-        for slot in range(z.M - 1):
-            total = total + r.orecv[slot, :, features].astype(F32)
-        r.blk[:, features] = (r.tok[:, features].astype(F32) + total).astype(BF16)
 
     swap_n = Swap(z, links, lambda slot: r.nrecv.at[slot])
 
@@ -1376,7 +1455,8 @@
             r.normed[: z.R, features] = part.astype(BF16)
             scaled = part * r.tokg[j].astype(F32)
             by_gain = jnp.sum(scaled * wide(r.inv[...], z.Ds // LANE), axis=0, keepdims=True)
-            r.gv[0, :, features] = jnp.broadcast_to(by_gain, (8, z.Ds))
+            for part in range(z.Ds // LANE):
+                r.gv[pl.ds(j * (z.Ds // LANE) + part, 1), :] = by_gain[:, part * LANE : (part + 1) * LANE]
             means = means + jnp.sum(scaled * r.gain[:, features], axis=1, keepdims=True)
 
         @pl.when(away < z.M)
@@ -1391,23 +1471,23 @@
     mean_mine[...] = jnp.broadcast_to(means, (z.R, LANE)).T[0:8]
     swap_m.start(mean_mine)
 
-    gain_copies = []
-    for level in range(z.levels):
-        copy = links.copy(
-            r.gv.at[level], r.gvr.at[level], links.sem(), links.sem(), seq=seq ^ (1 << level)
-        )
-        copy.start()
-        gain_copies.append(copy)
-        if level < depth - 1:
-            scatter_s.fold(level)
-        copy.wait_recv()
-        r.gv[level + 1] = r.gv[level] + r.gvr[level]
+    gain_seq = SwapSeq(z, links, lambda slot: r.gvr.at[slot])
+    gain_seq.start(r.gv)
+    for step in range(depth - 1):
+        scatter_s.fold(step)
+    scatter_0.second(onto(sum_0, term_0))
+    scatter_0.send(0)
+    gain_seq.wait()
+    gains = r.gv[...]
+    for slot in range(z.S - 1):
+        gains = gains + r.gvr[slot]
+    r.gvs[...] = gains
     swap_g = Swap(z, links, lambda slot: r.gvm.at[slot])
-    swap_g.start(r.gv.at[z.levels])
-    scatter_s.fold(depth - 1)
+    swap_g.start(r.gvs)
+    scatter_s.fold(last)
 
     def write_small(rows, value):
-        small.block(seq, *rows)[...] = value.astype(BF16)
+        small.block(seq)[rows, :] = value.astype(BF16)
 
     scatter_s.total(write_small)
     tree_s = TreeGather(
@@ -1418,6 +1498,10 @@
     )
     tree_s.first()
     tree_s.second()
+    scatter_1.fold(last)
+    scatter_1.total(write_to(r.fac))
+    store_1 = pltpu.make_async_copy(r.fac.at[pl.ds(0, z.Ds)], r.din.at[1], local.at[3])
+    store_1.start()
     for step in range(depth - 1):
         scatter_0.fold(step)
     tree_s.forward()
@@ -1427,57 +1511,40 @@
     mean = r.mrow[0]
     for slot in range(1, z.M):
         mean = mean + r.mrow[slot]
-    mean = wide(jnp.concatenate([mean] * (LANE // 8), axis=0).T * (1.0 / z.D), z.Ds // LANE)
+    r.mean[...] = jnp.concatenate([mean] * (LANE // 8), axis=0).T * (1.0 / z.D)
     swap_n.wait()
-    inv_wide = wide(r.inv[...], z.Ds // LANE)
-    for b in range(z.B):
-        j = first_block + b
-        here = slice(b * z.Ds, (b + 1) * z.Ds)
-        gain = r.gain[:, cut(j * z.Ds, z.Ds)]
-        total = r.normed[: z.R, cut(j * z.Ds, z.Ds)].astype(F32)
-        for slot in range(z.M - 1):
-            total = total + r.nrecv[slot, :, here].astype(F32)
-        x = r.tok[:, here].astype(F32)
-        value = inv_wide * (total * gain) - x * (inv_wide * inv_wide * inv_wide) * mean
+
+    def token_lanes(index):
+        here = cut(index * LANE, LANE)
+        inside = cut(mp * z.Df + index * LANE, LANE)
         for q in range(z.Q):
-            rows = slice(q * z.T, (q + 1) * z.T)
-            r.dtok[rows, here] = value[rows] + r.cot[rows, here] * seq_weight[q]
-
-    last = depth - 1
-    scatter_o.fold(last)
-
-    def write_out(rows, value):
-        r.dout[pl.ds(*rows), :] = value
-
-    scatter_o.total(write_out)
-    scatter_1.fold(last)
-
-    def write_to(ref):
-        def write(rows, value):
-            ref[pl.ds(*rows), :] = value
-
-        return write
-
-    scatter_1.total(write_to(r.fac))
-    store_1 = pltpu.make_async_copy(r.fac.at[pl.ds(0, z.Ds)], r.din.at[1], local.at[3])
-    store_1.start()
-    swap_g.wait()
-    gains = r.gv[z.levels]
-    for slot in range(z.M - 1):
-        gains = gains + r.gvm[slot]
-    r.dgain[...] = gains[0:1]
+            rows = rows_of(q)
+            total = r.normed[rows, inside].astype(F32)
+            for slot in range(z.M - 1):
+                total = total + r.nrecv[slot, rows, here].astype(F32)
+            inv, x = r.inv[rows, :], r.tok[rows, here].astype(F32)
+            value = inv * (total * r.gain[:, inside]) - x * (inv * inv * inv) * r.mean[rows, :]
+            r.dtok[rows, here] = value + r.cot[rows, here] * seq_weight[q]
+
+    each(z.Df // LANE, token_lanes)
+
+    scatter_0.fold(last)
+    scatter_0.total(write_to(r.s))
+    store_0 = pltpu.make_async_copy(r.s.at[pl.ds(0, z.Ds)], r.din.at[0], local.at[4])
+    store_0.start()
     tree_s.finish()
     for block in range(z.S):
         count = min(sg_rows, r.sg.shape[0] - block * sg_rows)
         if count > 0:
-            r.sg[block * sg_rows : block * sg_rows + count, :] = small.block(block)[...].astype(F32)[:count]
-    scatter_0.fold(last)
-    scatter_0.total(write_to(r.s))
-    store_0 = pltpu.make_async_copy(r.s.at[pl.ds(0, z.Ds)], r.din.at[0], local.at[4])
-    store_0.start()
+            r.sg[block * sg_rows : block * sg_rows + count, :] = small.block(block, 0, count)[...].astype(F32)
+    swap_g.wait()
+    gains = r.gvs[...]
+    for slot in range(z.M - 1):
+        gains = gains + r.gvm[slot]
+    r.dgain[...] = gains
 
     hal.wait_send()
-    for tree in (tree_x, tree_z, tree_o, tree_s):
+    for tree in (tree_x, tree_z, tree_s):
         tree.drain()
     for line in (line_t, line_h, line_d):
         line.drain()
@@ -1487,11 +1554,12 @@
         swap_dlow[q].drain(dlow_mine[q])
         swap_dst[q].drain(dst_mine[q])
     swap_m.drain(mean_mine)
-    swap_g.drain(r.gv.at[z.levels])
+    swap_g.drain(r.gvs)
+    gain_seq.drain()
     for away in range(1, z.M):
         owner = lax.rem(mp + away, z.M)
         swap_n.one(partial_of(owner), away).wait_send()
-    for copy in carry_copies + gain_copies + rim:
+    for copy in carry_copies + rim:
         copy.wait_send()
     for scatter in (scatter_o, scatter_1, scatter_0, scatter_s):
         scatter.drain()
@@ -1501,25 +1569,20 @@
 
 def finish_kernel(z, blk, dtok, dgain, din, dout, sg, *outs):
     a, b, c = z.RK, 2 * z.RK, 2 * z.RK + 2 * z.N
-    o_blk, o_dtok, o_dgain, o_din, o_convw, o_convb, o_low, o_state, o_delta, o_dbias, o_skip, o_dout, sems = outs
-    copies = [
-        pltpu.make_async_copy(src, dst, sems.at[index])
-        for index, (src, dst) in enumerate([(din, o_din), (dout, o_dout), (dtok, o_dtok), (blk, o_blk)])
-    ]
-    for copy in copies:
-        copy.start()
+    o_blk, o_dtok, o_dgain, o_din, o_convw, o_convb, o_low, o_state, o_delta, o_dbias, o_skip, o_dout = outs
+    o_blk[...] = blk[...]
+    o_dtok[...] = dtok[...]
     o_dgain[...] = dgain[...]
+    o_din[...] = din[...]
+    o_dout[...] = dout[...]
     o_delta[...] = sg[0:a, :]
+    o_state[...] = sg[b:c, :]
     o_convw[...] = sg[c : c + 4, :]
     o_convb[...] = sg[c + 4 : c + 5, :]
     o_dbias[...] = sg[c + 5 : c + 6, :]
     o_skip[...] = sg[c + 6 : c + 7, :]
     for at in range(0, z.C, LANE):
         o_low[at : at + LANE, :] = sg[a:b, at : at + LANE].T
-        part = jnp.concatenate([sg[b:c, at : at + LANE], jnp.zeros((LANE - 2 * z.N, LANE), F32)], axis=0)
-        o_state[at : at + LANE, :] = part.T[:, : 2 * z.N]
-    for copy in copies:
-        copy.wait()
 
 
 def fused(z, tokens, norm_gain, in_weight, conv_weight, conv_bias, low_weight, state_weight, delta_weight,
@@ -1549,7 +1612,7 @@
     outs = dict(
         blk=(V, (z.R, z.Df), BF16),
         dtok=(V, (z.R, z.Df), F32),
-        dgain=(V, (1, z.D), F32),
+        dgain=(V, (z.D // LANE, LANE), F32),
         din=(A, (2, z.Ds, z.C), F32),
         dout=(V, (z.C, z.Ds), F32),
         sg=(V, (sg_used, z.C), F32),
@@ -1566,29 +1629,31 @@
     )(*[value for _, value in operands.values()])
     whole = (V, (1, z.C), F32)
     last = dict(
-        blk=(A, (z.R, z.Df), BF16),
-        dtok=(A, (z.R, z.Df), F32),
-        dgain=(V, (1, z.D), F32),
-        din=(A, (2, z.Ds, z.C), F32),
+        blk=(V, (z.R, z.Df), BF16),
+        dtok=(V, (z.R, z.Df), F32),
+        dgain=(V, (z.D // LANE, LANE), F32),
+        din=(V, (2, z.Ds, z.C), F32),
         convw=(V, (4, z.C), F32),
         convb=whole,
         low=(V, (z.C, z.RK), F32),
-        state=(V, (z.C, 2 * z.N), F32),
+        state=(V, (2 * z.N, z.C), F32),
         delta=(V, (z.RK, z.C), F32),
         dbias=whole,
         skip=whole,
-        dout=(A, (z.C, z.Ds), F32),
+        dout=(V, (z.C, z.Ds), F32),
     )
     done = pl.pallas_call(
         functools.partial(finish_kernel, z),
         out_shape=[jax.ShapeDtypeStruct(shape, kind) for _, shape, kind in last.values()],
-        in_specs=[A, A, V, A, A, V],
+        in_specs=[V] * 6,
         out_specs=[spec for spec, _, _ in last.values()],
-        scratch_shapes=[pltpu.SemaphoreType.DMA((4,))],
         compiler_params=pltpu.CompilerParams(vmem_limit_bytes=VMEM_BYTES),
     )(*result)
-    shapes = [tokens.shape, tokens.shape, (z.D,), None, None, (z.C,), None, None, None, (z.C,), (z.C,), None]
-    return tuple(value if shape is None else value.reshape(shape) for value, shape in zip(done, shapes))
+    done = dict(zip(last, done))
+    done.update(blk=done["blk"].reshape(tokens.shape), dtok=done["dtok"].reshape(tokens.shape))
+    done.update(dgain=done["dgain"].reshape(z.D), state=done["state"].T)
+    done.update({name: done[name][0] for name in ("convb", "dbias", "skip")})
+    return tuple(done.values())
 
 
 def local(mesh_shape, *arrays):

time: 293 us -> 163 us (0.56)
  Pallas kernels: 290 us -> 162 us
    pallas_call x1, Pallas kernels: 123 us -> 4.98 us  [fused(): pl.pallas_call(functools.partial(finish_kernel, z), out_shape=[jax.ShapeD...]
    pallas_call x1, Pallas kernels: 167 us -> 157 us  [fused(): pl.pallas_call(functools.partial(fused_kernel, z, [*operands, *outs, *scr...]
where the time goes in v3:
time: 163 us
  Pallas kernels  162 us (99%)
    pallas_call x1, Pallas kernels, fused(): pl.pallas_call(functools.partial(fused_kernel, z, [*operands, *outs, *scr...  157 us
    pallas_call x1, Pallas kernels, fused(): pl.pallas_call(functools.partial(finish_kernel, z), out_shape=[jax.ShapeD...  4.98 us

profile of v3, /device:TPU:0, one launch (start us, length us, event | category | flops | bytes accessed | tf_op | source)
XLA Modules:
  0.0 163.1 jit_solution(13740215606475146273)
XLA Ops:
  0.6 157.5 %shard_map.229 = (bf16[256,512]{1,0:T(8,128)(2,1)}, f32[256,512]{1,0:T(8,128)}, f32[16,128]{1,0:T(8,128)}, f32[2,256,1024]{2,1,0:T(8,128)}, f32[1024,256]{1,0:T(8,128)}, /*index=5*/f32[304,1024]{1,0:T(8,128)}) custom-call(bf16[256,512]{1,0:T(8,128)(2,1)} %bitcast.15, f32[256,512]{1,0:T(8,128)} %bitcast.14, f32[1,2048]{1,0:T(1,128)} %bitcast.17, ...), custom_call_target="tpu_custom_call" | custom-call | tf_op jit(solution)/shard_map/pallas_call | solution.py:1620
  158.1 5.0 %shard_map.230 = (bf16[256,512]{1,0:T(8,128)(2,1)}, f32[256,512]{1,0:T(8,128)}, f32[16,128]{1,0:T(8,128)}, f32[2,256,1024]{2,1,0:T(8,128)}, f32[4,1024]{1,0:T(4,...) custom-call(bf16[256,512]{1,0:T(8,128)(2,1)} %get-tuple-element.30.b, ...), custom_call_target="tpu_custom_call" | custom-call | tf_op jit(solution)/shard_map/pallas_call | solution.py:1645

commit v4 on v3

--- a/solution.py
+++ b/solution.py
@@ -451,21 +451,22 @@
         for h in range(2):
             self.push(0, h, self.z.order(h)[0])
 
-    def second(self):
-        for h in range(2):
-            for dim in self.z.order(h)[1:]:
-                self.push(0, h, dim)
-        self.hand(0)
-
-    def forward(self):
-        for h in range(2):
-            order = self.z.order(h)
-            if len(order) > 1:
-                self.take(order[0], h)
-                self.push(order[0], h, order[1])
-
-    def settle(self):
+    def second(self, h):
+        for dim in self.z.order(h)[1:]:
+            self.push(0, h, dim)
+        if h == 0:
+            self.hand(0)
+
+    def forward(self, h):
+        order = self.z.order(h)
+        if len(order) > 1:
+            self.take(order[0], h)
+            self.push(order[0], h, order[1])
+
+    def settle(self, far=None):
         for mask in sorted(self.z.masks[1:], key=lambda mask: bin(mask).count("1")):
+            if far is not None and far != (bin(mask).count("1") > 1):
+                continue
             for h in range(2):
                 order = self.z.order(h)
                 if len(order) == 1 or mask != order[0]:
@@ -593,32 +594,33 @@
         return self.far.block(place, 0, halves(self.rows)[h][1])
 
     def first(self, make):
-        z, links = self.z, self.links
-        for mask in z.masks:
+        links = self.links
+        for mask in self.by_need():
             src = make(links.seq ^ 1 ^ mask, mask)
             copy = links.copy(src, self.sums.block(mask // 2), self.near_send[mask], self.near[mask], seq=links.seq ^ 1)
             copy.start()
             self.sent.append(copy)
 
-    def second(self, add):
-        z, links = self.z, self.links
-        by_need = sorted(z.masks, key=lambda mask: -bin(mask).count("1"))
-        for mask in by_need:
+    def by_need(self):
+        return sorted(self.z.masks, key=lambda mask: -bin(mask).count("1"))
+
+    def second(self, add, send=False, masks=None):
+        links = self.links
+        for mask in self.by_need() if masks is None else masks:
             links.arrived(self.sums.block(mask // 2), self.near[mask])
             add(links.seq ^ mask, mask)
-
-    def send(self, step, part=None):
+            if send:
+                self.send(0, mask)
+
+    def send(self, step, only=None):
         links = self.links
-        count = {0: 0, 1: 0}
         for (h, at, mask), (dim, send, recv, place) in self.hops.items():
-            if at == step:
-                count[h] += 1
-                if part is None or (count[h] > 1) == (part == 1):
-                    copy = links.copy(
-                        self.half(mask, h), self.came(h, place), send, recv, seq=links.seq ^ dim
-                    )
-                    copy.start()
-                    self.sent.append(copy)
+            if at == step and only in (None, mask):
+                copy = links.copy(
+                    self.half(mask, h), self.came(h, place), send, recv, seq=links.seq ^ dim
+                )
+                copy.start()
+                self.sent.append(copy)
 
     def fold(self, step):
         links = self.links
@@ -784,7 +786,10 @@
         lambda owner, h: r.wo.at[pl.ds(h * (z.C // 2), z.C // 2), cut(owner * z.Ds, z.Ds)],
         lambda owner: r.wo.at[:, cut(owner * z.Ds, z.Ds)],
     )
-    line_t = LineGather(z, links, lambda owner: r.tokg.at[pl.ds(owner * z.B, z.B)])
+    line_t = [
+        LineGather(z, links, lambda owner, q=q: r.tokg.at[pl.ds(owner * z.B, z.B), pl.ds(q * z.T, z.T), :])
+        for q in range(z.Q)
+    ]
     line_h = LineGather(z, links, lambda owner: r.halg.at[pl.ds(owner * z.B, z.B)])
     line_d = LineGather(z, links, lambda owner: r.db.at[:, cut(owner * z.Df, z.Df)])
     depth = len(z.dims)
@@ -793,10 +798,12 @@
     hal_mine = r.halg.at[pl.ds(first_block, z.B)]
     hal = links.copy(r.hals, hal_mine, hal_send, hal_recv, seq=ahead)
     hal.start()
-    line_t.step(0)
+    for line in line_t:
+        line.step(0)
     loads[0].wait()
     tree_x.first()
-    tree_x.second()
+    tree_x.second(0)
+    tree_x.second(1)
 
     def weight_of(q):
         total = jnp.float32(0.0)
@@ -813,15 +820,24 @@
 
     links.arrived(hal_mine, hal_recv)
     line_h.step(0)
-    line_t.step(1)
-    tree_x.forward()
+    for line in line_t:
+        line.step(1)
+    tree_x.forward(0)
+    tree_x.forward(1)
     loads[1].wait()
     tree_z.first()
-    tree_z.second()
+    tree_z.second(0)
+    tree_z.second(1)
     line_h.step(1)
     for far in range(2, z.M):
-        line_t.step(far)
+        for line in line_t:
+            line.step(far)
         line_h.step(far)
+        if far == 2:
+            tree_x.settle(False)
+    if z.M == 2:
+        tree_x.settle(False)
+    line_d.step(0)
 
     def add_squares(j, total):
         part = r.tokg[j].astype(F32)
@@ -848,7 +864,7 @@
         r.normt[features, :] = normed.T.astype(BF16)
 
     each(z.S, norm_block)
-    tree_x.settle()
+    tree_x.settle(True)
     tree_x.finish()
 
     def x_chunk(index):
@@ -860,6 +876,11 @@
             r.xpad[q, 8 : 8 + z.T, lanes] = part[q * z.T : (q + 1) * z.T]
 
     each(z.C // 256, x_chunk)
+    tree_z.forward(0)
+    tree_z.forward(1)
+    loads[2].wait()
+    tree_o.first()
+    tree_o.second(0)
 
     def rows_of(q):
         return pl.ds(q * z.T, z.T)
@@ -1061,40 +1082,38 @@
     project(0)
     conv(1)
     project(1)
-    line_d.step(0)
-    tree_z.forward()
-    loads[2].wait()
-    tree_o.first()
+    line_d.step(1)
     keys(0)
     totals(0)
     carry_send(0, 0)
-    line_d.step(1)
     keys(1)
     carry_take(0, 0)
     carry_send(1, 0)
     totals(1)
     carry_send(0, 1)
-    for level in range(1, z.levels):
-        carry_take(level, 0)
-        if level < z.levels - 1:
-            carry_send(level + 1, 0)
-        carry_take(level - 1, 1)
-        carry_send(level, 1)
-        if level == 1:
-            tree_o.second()
-            line_d.step(2)
-            tree_z.settle()
-            key_blocks(0)
-            key_blocks(1)
-            tree_z.finish()
-            each(z.C // 256, z_chunk)
-    tree_o.forward()
+    carry_take(0, 1)
+    carry_send(1, 1)
+    tree_o.second(1)
+    tree_o.forward(1)
+    line_d.step(2)
+    tree_z.settle()
+    key_blocks(0)
+    key_blocks(1)
+    for level in range(1, z.levels - 1):
+        for q in range(z.Q):
+            carry_take(level, q)
+            carry_send(level + 1, q)
+    tree_o.forward(0)
+    tree_z.finish()
+    each(z.C // 256, z_chunk)
+    carry_take(z.levels - 1, 0)
     walk(0)
-    carry_take(z.levels - 1, 1)
     for far in range(3, z.M):
         line_d.step(far)
+    tree_o.settle(False)
+    carry_take(z.levels - 1, 1)
     walk(1)
-    tree_o.settle()
+    tree_o.settle(True)
     tree_o.finish()
 
     def gated_grad(index):
@@ -1335,27 +1354,71 @@
 
         lane_loop(x_lanes)
 
+    swap_n = [Swap(z, links, lambda slot, q=q: r.nrecv.at[slot, rows_of(q), :]) for q in range(z.Q)]
+
+    def normed_of(q, owner):
+        return r.normed.at[rows_of(q), cut(owner * z.Df, z.Df)]
+
+    def normed_part(q):
+        rows = rows_of(q)
+
+        def normed_to(index, means):
+            away = index + 1
+            owner = lax.rem(mp + away, z.M)
+            for b in range(z.B):
+                j = owner * z.B + b
+                features = cut(j * z.Ds, z.Ds)
+                part = nt(r.dxr[rows, :], r.wx[0, features, :]) + nt(r.dzr[rows, :], r.wx[1, features, :])
+                r.normed[rows, features] = part.astype(BF16)
+                scaled = part * r.tokg[j, rows, :].astype(F32)
+                by_gain = jnp.sum(scaled * wide(r.inv[rows, :], z.Ds // LANE), axis=0, keepdims=True)
+                for piece in range(z.Ds // LANE):
+                    place = pl.ds(j * (z.Ds // LANE) + piece, 1)
+                    value = by_gain[:, piece * LANE : (piece + 1) * LANE]
+                    r.gv[place, :] = value if q == 0 else r.gv[place, :] + value
+                means = means + jnp.sum(scaled * r.gain[:, features], axis=1, keepdims=True)
+
+            @pl.when(away < z.M)
+            def _():
+                swap_n[q].one(normed_of(q, owner), away).start()
+
+            return means
+
+        means = lax.fori_loop(0, z.M, normed_to, jnp.zeros((z.T, 1), F32))
+        mean_mine[:, rows] = jnp.broadcast_to(means, (z.T, LANE)).T[0:8]
+
+    swap_m = Swap(z, links, lambda slot: r.mrow.at[slot])
+    mean_mine = r.mrow.at[z.M - 1]
+
+    def settle_back(level, q):
+        back_take(level, q)
+        if level < z.levels - 1:
+            back_send(level + 1, q)
+
+    most = scatter_o.by_need()
     scatter_o.first(into(near_o, term_o))
+    scatter_o.second(onto(sum_o, term_o), send=True, masks=most[:1])
     totals_back(0)
     back_send(0, 0)
-    scatter_o.second(onto(sum_o, term_o))
-    back_take(0, 0)
-    back_send(1, 0)
+    each(z.M, branch_to)
+    scatter_o.second(onto(sum_o, term_o), masks=most[1:])
+    settle_back(0, 0)
     totals_back(1)
     back_send(0, 1)
-    for level in range(1, z.levels):
-        back_take(level, 0)
-        if level < z.levels - 1:
-            back_send(level + 1, 0)
-        back_take(level - 1, 1)
-        back_send(level, 1)
-        if level == 1:
-            each(z.M, branch_to)
-            scatter_1.first(into(near_i, term_1))
-    scatter_o.send(0)
-    back_take(z.levels - 1, 1)
-    scatter_1.second(onto(sum_1, term_1))
-    scatter_1.send(0)
+    settle_back(0, 1)
+    for mask in most[1:]:
+        if mask & z.dims[0]:
+            scatter_o.send(0, mask)
+    scatter_1.first(into(near_i, term_1))
+    for level in range(1, z.levels - 1):
+        for q in range(z.Q):
+            settle_back(level, q)
+    for mask in most[1:]:
+        if not mask & z.dims[0]:
+            scatter_o.send(0, mask)
+    scatter_1.second(onto(sum_1, term_1), send=True)
+    for q in range(z.Q):
+        back_take(z.levels - 1, q)
     for copy in scatter_1.sent[: len(z.masks)]:
         copy.wait_send()
     scatter_1.sent = scatter_1.sent[len(z.masks) :]
@@ -1372,10 +1435,10 @@
         )
     step_back(1)
     project_back(1)
+    for step in range(depth - 1):
+        scatter_1.fold(step)
     sums_back(0)
     conv_back(0)
-    for step in range(depth - 1):
-        scatter_1.fold(step)
 
     last = depth - 1
     scatter_o.fold(last)
@@ -1400,6 +1463,8 @@
         r.blk[:, here] = (r.tok[:, here].astype(F32) + total).astype(BF16)
 
     each(z.Df // LANE, block_lanes)
+    x_back(0)
+    normed_part(0)
     sums_back(1)
     conv_back(1)
 
@@ -1427,10 +1492,7 @@
     for level in range(z.levels):
         pl.semaphore_wait(r.ready.at[level], 1)
     scatter_s.first(lambda device, mask: sgp.block(device))
-    x_back(0)
     x_back(1)
-
-    scatter_0.first(into(near_i, term_0))
 
     def add_small(device, mask):
         block, term = sum_s.block(mask // 2), sgp.block(device)
@@ -1440,50 +1502,18 @@
 
         by_rows(sg_rows, one)
 
-    scatter_s.second(add_small)
-    scatter_s.send(0)
-
-    swap_n = Swap(z, links, lambda slot: r.nrecv.at[slot])
-
-    def normed_to(index, means):
-        away = index + 1
-        owner = lax.rem(mp + away, z.M)
-        for b in range(z.B):
-            j = owner * z.B + b
-            features = cut(j * z.Ds, z.Ds)
-            part = nt(r.dxr[...], r.wx[0, features, :]) + nt(r.dzr[...], r.wx[1, features, :])
-            r.normed[: z.R, features] = part.astype(BF16)
-            scaled = part * r.tokg[j].astype(F32)
-            by_gain = jnp.sum(scaled * wide(r.inv[...], z.Ds // LANE), axis=0, keepdims=True)
-            for part in range(z.Ds // LANE):
-                r.gv[pl.ds(j * (z.Ds // LANE) + part, 1), :] = by_gain[:, part * LANE : (part + 1) * LANE]
-            means = means + jnp.sum(scaled * r.gain[:, features], axis=1, keepdims=True)
-
-        @pl.when(away < z.M)
-        def _():
-            swap_n.one(partial_of(owner), away).start()
-
-        return means
-
-    means = lax.fori_loop(0, z.M, normed_to, jnp.zeros((z.R, 1), F32))
-    swap_m = Swap(z, links, lambda slot: r.mrow.at[slot])
-    mean_mine = r.mrow.at[z.M - 1]
-    mean_mine[...] = jnp.broadcast_to(means, (z.R, LANE)).T[0:8]
+    scatter_s.second(add_small, send=True)
+    scatter_0.first(into(near_i, term_0))
+    scatter_0.second(onto(sum_0, term_0), send=True, masks=most[:1])
+    for step in range(depth - 1):
+        scatter_s.fold(step)
+    scatter_0.second(onto(sum_0, term_0), send=True, masks=most[1:])
+
+    normed_part(1)
     swap_m.start(mean_mine)
 
     gain_seq = SwapSeq(z, links, lambda slot: r.gvr.at[slot])
     gain_seq.start(r.gv)
-    for step in range(depth - 1):
-        scatter_s.fold(step)
-    scatter_0.second(onto(sum_0, term_0))
-    scatter_0.send(0)
-    gain_seq.wait()
-    gains = r.gv[...]
-    for slot in range(z.S - 1):
-        gains = gains + r.gvr[slot]
-    r.gvs[...] = gains
-    swap_g = Swap(z, links, lambda slot: r.gvm.at[slot])
-    swap_g.start(r.gvs)
     scatter_s.fold(last)
 
     def write_small(rows, value):
@@ -1497,14 +1527,23 @@
         small.block,
     )
     tree_s.first()
-    tree_s.second()
+    tree_s.second(0)
+    tree_s.second(1)
+    for step in range(depth - 1):
+        scatter_0.fold(step)
+    gain_seq.wait()
+    gains = r.gv[...]
+    for slot in range(z.S - 1):
+        gains = gains + r.gvr[slot]
+    r.gvs[...] = gains
+    swap_g = Swap(z, links, lambda slot: r.gvm.at[slot])
+    swap_g.start(r.gvs)
+    tree_s.forward(0)
+    tree_s.forward(1)
     scatter_1.fold(last)
     scatter_1.total(write_to(r.fac))
     store_1 = pltpu.make_async_copy(r.fac.at[pl.ds(0, z.Ds)], r.din.at[1], local.at[3])
     store_1.start()
-    for step in range(depth - 1):
-        scatter_0.fold(step)
-    tree_s.forward()
     tree_s.settle()
 
     swap_m.wait()
@@ -1512,7 +1551,8 @@
     for slot in range(1, z.M):
         mean = mean + r.mrow[slot]
     r.mean[...] = jnp.concatenate([mean] * (LANE // 8), axis=0).T * (1.0 / z.D)
-    swap_n.wait()
+    for swap in swap_n:
+        swap.wait()
 
     def token_lanes(index):
         here = cut(index * LANE, LANE)
@@ -1546,7 +1586,7 @@
     hal.wait_send()
     for tree in (tree_x, tree_z, tree_s):
         tree.drain()
-    for line in (line_t, line_h, line_d):
+    for line in (*line_t, line_h, line_d):
         line.drain()
     for q in range(z.Q):
         swap_st[q].drain(st_mine[q])
@@ -1558,7 +1598,8 @@
     gain_seq.drain()
     for away in range(1, z.M):
         owner = lax.rem(mp + away, z.M)
-        swap_n.one(partial_of(owner), away).wait_send()
+        for q in range(z.Q):
+            swap_n[q].one(normed_of(q, owner), away).wait_send()
     for copy in carry_copies + rim:
         copy.wait_send()
     for scatter in (scatter_o, scatter_1, scatter_0, scatter_s):

time: 163 us -> 156 us (0.957)
  Pallas kernels: 162 us -> 155 us
    pallas_call x1, Pallas kernels: 157 us -> 150 us  [fused(): pl.pallas_call(functools.partial(fused_kernel, z, [*operands, *outs, *scr...]
where the time goes in v4:
time: 156 us; the launch traced here: 155 us
  Pallas kernels  155 us (99%)
    pallas_call x1, Pallas kernels, fused(): pl.pallas_call(functools.partial(fused_kernel, z, [*operands, *outs, *scr...  150 us
    pallas_call x1, Pallas kernels, fused(): pl.pallas_call(functools.partial(finish_kernel, z), out_shape=[jax.ShapeD...  4.98 us

profile of v4, /device:TPU:0, one launch (start us, length us, event | category | flops | bytes accessed | tf_op | source)
XLA Modules:
  0.0 155.5 jit_solution(17370836147303565375)
XLA Ops:
  0.6 149.8 %shard_map.229 = (bf16[256,512]{1,0:T(8,128)(2,1)}, f32[256,512]{1,0:T(8,128)}, f32[16,128]{1,0:T(8,128)}, f32[2,256,1024]{2,1,0:T(8,128)}, f32[1024,256]{1,0:T(8,128)}, /*index=5*/f32[304,1024]{1,0:T(8,128)}) custom-call(bf16[256,512]{1,0:T(8,128)(2,1)} %bitcast.15, f32[256,512]{1,0:T(8,128)} %bitcast.14, f32[1,2048]{1,0:T(1,128)} %bitcast.17, ...), custom_call_target="tpu_custom_call" | custom-call | tf_op jit(solution)/shard_map/pallas_call | solution.py:1661
  150.5 5.0 %shard_map.230 = (bf16[256,512]{1,0:T(8,128)(2,1)}, f32[256,512]{1,0:T(8,128)}, f32[16,128]{1,0:T(8,128)}, f32[2,256,1024]{2,1,0:T(8,128)}, f32[4,1024]{1,0:T(4,...) custom-call(bf16[256,512]{1,0:T(8,128)(2,1)} %get-tuple-element.30.b, ...), custom_call_target="tpu_custom_call" | custom-call | tf_op jit(solution)/shard_map/pallas_call | solution.py:1686

commit v5 on v4

--- a/solution.py
+++ b/solution.py
@@ -665,6 +665,16 @@
     half = z.S // 2
     slots = slots_of(z)
     return dict(
+        tok=V((z.R, z.Df), BF16),
+        cot=V((z.R, z.Df), F32),
+        gain=V((1, z.D), F32),
+        convw=V((4, z.C), F32),
+        convb=V((1, z.C), F32),
+        dbias=V((1, z.C), F32),
+        skip=V((1, z.C), F32),
+        loww=V((z.C, z.RK), BF16),
+        statewt=V((2 * z.N, z.C), BF16),
+        deltaw=V((z.RK, z.C), BF16),
         tokg=V((z.S, z.R, z.Ds), BF16),
         halg=V((z.S, 16, z.Ds), BF16),
         hals=V((z.B, 16, z.Ds), BF16),
@@ -728,7 +738,7 @@
         mean=V((z.R, LANE), F32),
         mrow=V((z.M, 8, z.R), F32),
         sems=pltpu.SemaphoreType.DMA((420,)),
-        local=pltpu.SemaphoreType.DMA((8,)),
+        local=pltpu.SemaphoreType.DMA((16,)),
         ready=pltpu.SemaphoreType.REGULAR((z.levels,)),
     )
 
@@ -755,8 +765,25 @@
         pltpu.make_async_copy(r.win.at[1], mine_in(1), local.at[1]),
         pltpu.make_async_copy(r.wout, r.wo.at[:, cut(seq * z.Ds, z.Ds)], local.at[2]),
     ]
+    pairs = [
+        (r.tok_in, r.tok),
+        (r.cot_in, r.cot),
+        (r.gain_in, r.gain),
+        (r.convw_in, r.convw),
+        (r.convb_in, r.convb),
+        (r.dbias_in, r.dbias),
+        (r.skip_in, r.skip),
+        (r.loww_in, r.loww),
+        (r.statewt_in, r.statewt),
+        (r.deltaw_in, r.deltaw),
+    ]
+    own = [pltpu.make_async_copy(src, dst, local.at[5 + index]) for index, (src, dst) in enumerate(pairs)]
+    own[0].start()
     for load in loads:
         load.start()
+    for copy in own[1:]:
+        copy.start()
+    own[0].wait()
     for b in range(z.B):
         r.tokg[first_block + b] = r.tok[:, b * z.Ds : (b + 1) * z.Ds]
         tails = [
@@ -804,6 +831,9 @@
     tree_x.first()
     tree_x.second(0)
     tree_x.second(1)
+
+    for copy in own[1:]:
+        copy.wait()
 
     def weight_of(q):
         total = jnp.float32(0.0)
@@ -1113,48 +1143,18 @@
     tree_o.settle(False)
     carry_take(z.levels - 1, 1)
     walk(1)
-    tree_o.settle(True)
-    tree_o.finish()
-
-    def gated_grad(index):
-        lanes = cut(index * 256, 256)
-        r.dr[:, lanes] = nt(r.db[...], r.wo[lanes, :])
-
-    each(z.C // 256, gated_grad)
     r.vec[...] = jnp.zeros_like(r.vec)
 
     def gate_lanes(lanes):
         for q in range(z.Q):
             rows = rows_of(q)
-            u = r.u[rows, lanes].astype(F32)
-            out = r.rd[rows, lanes] + r.skip[:, lanes] * u
-            part, grad = r.zp[rows, lanes], r.dr[rows, lanes]
-            gate, silu = silu_parts(part)
-            gated = out * silu
+            out = r.rd[rows, lanes] + r.skip[:, lanes] * r.u[rows, lanes].astype(F32)
+            r.rd[rows, lanes] = out
+            gated = out * silu_parts(r.zp[rows, lanes])[1]
             r.gat[rows, lanes] = gated.astype(BF16)
             r.gatt[lanes, rows] = gated.T.astype(BF16)
-            d_read = grad * silu
-            r.dr[rows, lanes] = d_read
-            r.dzr[rows, lanes] = (grad * out * gate * (1.0 + part * (1.0 - gate))).astype(BF16)
-            r.vec[6:7, lanes] += jnp.sum(d_read * u, axis=0, keepdims=True)
 
     lane_loop(gate_lanes)
-
-    swap_out = Swap(z, links, lambda slot: r.orecv.at[slot])
-
-    def partial_of(owner):
-        return r.normed.at[pl.ds(0, z.R), cut(owner * z.Df, z.Df)]
-
-    def branch_to(index):
-        away = index + 1
-        owner = lax.rem(mp + away, z.M)
-        for b in range(z.B):
-            j = owner * z.B + b
-            r.normed[: z.R, cut(j * z.Ds, z.Ds)] = nn(r.gat[...], r.wo[:, cut(j * z.Ds, z.Ds)]).astype(BF16)
-
-        @pl.when(away < z.M)
-        def _():
-            swap_out.one(partial_of(owner), away).start()
 
     def into(near, term):
         def make(device, mask):
@@ -1190,6 +1190,46 @@
     term_1 = lambda device: nn(r.normt[cut(device * z.Ds, z.Ds), :], r.dzr[...])
     term_0 = lambda device: nn(r.normt[cut(device * z.Ds, z.Ds), :], r.dxr[...])
 
+    tree_o.settle(True)
+    most = scatter_o.by_need()
+    scatter_o.first(into(near_o, term_o))
+    scatter_o.second(onto(sum_o, term_o), send=True, masks=most[:1])
+    tree_o.finish()
+
+    def gated_grad(index):
+        lanes = cut(index * 256, 256)
+        r.dr[:, lanes] = nt(r.db[...], r.wo[lanes, :])
+
+    each(z.C // 256, gated_grad)
+
+    def gate_back(lanes):
+        for q in range(z.Q):
+            rows = rows_of(q)
+            part, grad = r.zp[rows, lanes], r.dr[rows, lanes]
+            gate, silu = silu_parts(part)
+            d_read = grad * silu
+            r.dr[rows, lanes] = d_read
+            r.dzr[rows, lanes] = (grad * r.rd[rows, lanes] * gate * (1.0 + part * (1.0 - gate))).astype(BF16)
+            r.vec[6:7, lanes] += jnp.sum(d_read * r.u[rows, lanes].astype(F32), axis=0, keepdims=True)
+
+    lane_loop(gate_back)
+
+    swap_out = Swap(z, links, lambda slot: r.orecv.at[slot])
+
+    def partial_of(owner):
+        return r.normed.at[pl.ds(0, z.R), cut(owner * z.Df, z.Df)]
+
+    def branch_to(index):
+        away = index + 1
+        owner = lax.rem(mp + away, z.M)
+        for b in range(z.B):
+            j = owner * z.B + b
+            r.normed[: z.R, cut(j * z.Ds, z.Ds)] = nn(r.gat[...], r.wo[:, cut(j * z.Ds, z.Ds)]).astype(BF16)
+
+        @pl.when(away < z.M)
+        def _():
+            swap_out.one(partial_of(owner), away).start()
+
     def totals_back(q):
         def lane_part(index):
             lanes = cut(index * span, span)
@@ -1220,7 +1260,7 @@
 
     def walk_back(q):
         def group(index, carry):
-            tail, sum_gh, sum_g, sum_h = carry
+            tail, sum_gh, sum_g = carry
             i = groups - 1 - index
             for j in reversed(range(GRP)):
                 t = i * GRP + j
@@ -1228,7 +1268,6 @@
                 step, drive, grad = r.s[row, :], r.su[row, :], r.dr[row, :]
                 key, query = r.bc[q, t, : z.N, :], r.bc[q, t, z.N :, :]
                 before = r.hist[past_rows(q, t), :].astype(F32)
-                now = r.hist[past_rows(q, t + 1), :].astype(F32)
                 state_grad = grad * wide(query, lanes_all) + tail
                 crossed = state_grad * before
                 place = pl.ds(pl.multiple_of(lax.rem(i, batch) * GRP * z.N + j * z.N, z.N), z.N)
@@ -1237,12 +1276,11 @@
                 here = lane_index == t
                 sum_gh = jnp.where(here, lane_sum(step * crossed), sum_gh)
                 sum_g = jnp.where(here, lane_sum(drive * state_grad), sum_g)
-                sum_h = jnp.where(here, lane_sum(grad * now), sum_h)
                 tail = (1.0 - step * wide(key * key, lanes_all)) * state_grad
-            return tail, sum_gh, sum_g, sum_h
+            return tail, sum_gh, sum_g
 
         zero = jnp.zeros((z.N, LANE), F32)
-        carry = (r.spre[q], zero, zero, zero)
+        carry = (r.spre[q], zero, zero)
         for start in range(0, groups, batch):
             carry = lax.fori_loop(start, start + batch, group, carry)
             sums = []
@@ -1260,8 +1298,16 @@
                 r.rd[rows, :] = by_key
                 r.zp[rows, :] = by_square
         columns = rows_of(q)
-        for part in range(3):
+        for part in range(2):
             r.est[part, :, columns] = carry[1 + part]
+
+    def query_sums(q):
+        parts = []
+        for i in range(groups):
+            rows = pl.ds(q * z.T + i * GRP, GRP)
+            parts.append(nt(r.dr[rows, :].astype(BF16), r.hist[past_rows(q, i * GRP + 1, GRP), :]))
+        blocks = jnp.where(diagonal, jnp.concatenate(parts, axis=0), 0.0).astype(BF16)
+        r.est[2, :, rows_of(q)] = nt(rep_b[: z.N], blocks)
 
     def step_back(q):
         rows = rows_of(q)
@@ -1395,9 +1441,6 @@
         if level < z.levels - 1:
             back_send(level + 1, q)
 
-    most = scatter_o.by_need()
-    scatter_o.first(into(near_o, term_o))
-    scatter_o.second(onto(sum_o, term_o), send=True, masks=most[:1])
     totals_back(0)
     back_send(0, 0)
     each(z.M, branch_to)
@@ -1417,6 +1460,8 @@
         if not mask & z.dims[0]:
             scatter_o.send(0, mask)
     scatter_1.second(onto(sum_1, term_1), send=True)
+    query_sums(0)
+    query_sums(1)
     for q in range(z.Q):
         back_take(z.levels - 1, q)
     for copy in scatter_1.sent[: len(z.masks)]:
@@ -1435,13 +1480,10 @@
         )
     step_back(1)
     project_back(1)
-    for step in range(depth - 1):
-        scatter_1.fold(step)
     sums_back(0)
     conv_back(0)
 
     last = depth - 1
-    scatter_o.fold(last)
 
     def write_to(ref):
         def write(rows, value):
@@ -1449,7 +1491,6 @@
 
         return write
 
-    scatter_o.total(write_to(r.dout))
     swap_out.wait()
     for away in range(1, z.M):
         owner = lax.rem(mp + away, z.M)
@@ -1463,10 +1504,12 @@
         r.blk[:, here] = (r.tok[:, here].astype(F32) + total).astype(BF16)
 
     each(z.Df // LANE, block_lanes)
+    sums_back(1)
+    conv_back(1)
+    for step in range(depth - 1):
+        scatter_1.fold(step)
     x_back(0)
     normed_part(0)
-    sums_back(1)
-    conv_back(1)
 
     def put_small(first, lanes, value):
         count, at = value.shape[0], 0
@@ -1540,6 +1583,8 @@
     swap_g.start(r.gvs)
     tree_s.forward(0)
     tree_s.forward(1)
+    scatter_o.fold(last)
+    scatter_o.total(write_to(r.dout))
     scatter_1.fold(last)
     scatter_1.total(write_to(r.fac))
     store_1 = pltpu.make_async_copy(r.fac.at[pl.ds(0, z.Ds)], r.din.at[1], local.at[3])
@@ -1622,7 +1667,7 @@
     o_convb[...] = sg[c + 4 : c + 5, :]
     o_dbias[...] = sg[c + 5 : c + 6, :]
     o_skip[...] = sg[c + 6 : c + 7, :]
-    for at in range(0, z.C, LANE):
+    for at in range(0, sg.shape[1], LANE):
         o_low[at : at + LANE, :] = sg[a:b, at : at + LANE].T
 
 
@@ -1633,18 +1678,18 @@
     SM = pl.BlockSpec(memory_space=pltpu.SMEM)
     row = lambda value: value.reshape(1, -1)
     operands = dict(
-        tok=(V, tokens.reshape(z.R, z.Df)),
-        cot=(V, cotangent.reshape(z.R, z.Df)),
-        gain=(V, row(norm_gain)),
+        tok_in=(A, tokens.reshape(z.R, z.Df)),
+        cot_in=(A, cotangent.reshape(z.R, z.Df)),
+        gain_in=(A, row(norm_gain)),
         win=(A, in_weight),
         wout=(A, out_weight),
-        convw=(V, conv_weight),
-        convb=(V, row(conv_bias)),
-        dbias=(V, row(delta_bias)),
-        skip=(V, row(skip_gain)),
-        loww=(V, low_weight),
-        statewt=(V, state_weight.T),
-        deltaw=(V, delta_weight),
+        convw_in=(A, conv_weight),
+        convb_in=(A, row(conv_bias)),
+        dbias_in=(A, row(delta_bias)),
+        skip_in=(A, row(skip_gain)),
+        loww_in=(A, low_weight),
+        statewt_in=(A, state_weight.T),
+        deltaw_in=(A, delta_weight),
         seqg=(SM, seq_group),
         groupw=(SM, group_weight),
     )

time: 156 us -> 150 us (0.962)
  Pallas kernels: 155 us -> 149 us
    pallas_call x1, Pallas kernels: 150 us -> 144 us  [fused(): pl.pallas_call(functools.partial(fused_kernel, z, [*operands, *outs, *scr...]
where the time goes in v5:
time: 150 us
  Pallas kernels  149 us (99%)
    pallas_call x1, Pallas kernels, fused(): pl.pallas_call(functools.partial(fused_kernel, z, [*operands, *outs, *scr...  144 us
    pallas_call x1, Pallas kernels, fused(): pl.pallas_call(functools.partial(finish_kernel, z), out_shape=[jax.ShapeD...  4.98 us

profile of v5, /device:TPU:0, one launch (start us, length us, event | category | flops | bytes accessed | tf_op | source)
XLA Modules:
  0.0 149.7 jit_solution(14454754673076287501)
XLA Ops:
  0.6 144.1 %shard_map.229 = (bf16[256,512]{1,0:T(8,128)(2,1)}, f32[256,512]{1,0:T(8,128)}, f32[16,128]{1,0:T(8,128)}, f32[2,256,1024]{2,1,0:T(8,128)}, f32[1024,256]{1,0:T(8,128)}, /*index=5*/f32[304,1024]{1,0:T(8,128)}) custom-call(bf16[256,512]{1,0:T(8,128)(2,1)} %bitcast.15, f32[256,512]{1,0:T(8,128)} %bitcast.14, f32[1,2048]{1,0:T(1,128)} %bitcast.17, ...), custom_call_target="tpu_custom_call" | custom-call | tf_op jit(solution)/shard_map/pallas_call | solution.py:1706
  144.7 5.0 %shard_map.230 = (bf16[256,512]{1,0:T(8,128)(2,1)}, f32[256,512]{1,0:T(8,128)}, f32[16,128]{1,0:T(8,128)}, f32[2,256,1024]{2,1,0:T(8,128)}, f32[4,1024]{1,0:T(4,...) custom-call(bf16[256,512]{1,0:T(8,128)(2,1)} %get-tuple-element.30.b, ...), custom_call_target="tpu_custom_call" | custom-call | tf_op jit(solution)/shard_map/pallas_call | solution.py:1731

commit v6 on v5

--- a/solution.py
+++ b/solution.py
@@ -575,6 +575,7 @@
         self.near = {mask: links.sem() for mask in z.masks}
         self.near_send = {mask: links.sem() for mask in z.masks}
         self.sent = []
+        self.late = []
         self.hops = {}
         place = 0
         for h in range(2):
@@ -623,11 +624,22 @@
                 self.sent.append(copy)
 
     def fold(self, step):
-        links = self.links
+        self.late.append(step)
+        if step < len(self.z.dims) - 1:
+            going = {(h, mask) for h, at, mask in self.hops if at == step + 1}
+            self.take(step, lambda h, into: (h, into) in going)
+            self.send(step + 1)
+
+    def rest(self):
+        for step in self.late:
+            going = {(h, mask) for h, at, mask in self.hops if at == step + 1}
+            self.take(step, lambda h, into: (h, into) not in going)
+
+    def take(self, step, wanted):
         for (h, at, mask), (dim, send, recv, place) in self.hops.items():
-            if at != step:
+            if at != step or not wanted(h, mask ^ dim):
                 continue
-            links.arrived(self.came(h, place), recv)
+            self.links.arrived(self.came(h, place), recv)
             if step < len(self.z.dims) - 1:
                 half, came = self.half(mask ^ dim, h), self.came(h, place)
 
@@ -635,10 +647,9 @@
                     half[rows, :] = (half[rows, :].astype(F32) + came[rows, :].astype(F32)).astype(BF16)
 
                 by_rows(halves(self.rows)[h][1], add)
-        if step < len(self.z.dims) - 1:
-            self.send(step + 1)
 
     def total(self, write):
+        self.rest()
         last = len(self.z.dims) - 1
         for (h, at, mask), (dim, send, recv, place) in self.hops.items():
             if at == last:
@@ -758,6 +769,12 @@
     def lane_loop(step):
         each(z.C // LANE, lambda index: step(cut(index * LANE, LANE)))
 
+    barrier = pltpu.get_barrier_semaphore()
+    ahead, behind = lax.rem(seq + 1, z.S), lax.rem(seq + z.S - 1, z.S)
+    partners = [(seq ^ other, mp) for other in range(1, z.S)] + [(ahead, mp), (behind, mp)]
+    partners += [(seq, lax.rem(mp + away, z.M)) for away in range(1, z.M)]
+    for partner in partners:
+        pl.semaphore_signal(barrier, inc=1, device_id=partner, device_id_type=MESH)
     local = r.local
     mine_in = lambda k: r.wx.at[k, cut(seq * z.Ds, z.Ds), :]
     loads = [
@@ -792,12 +809,6 @@
         ]
         r.hals[b] = jnp.concatenate(tails, axis=0).astype(BF16)
 
-    barrier = pltpu.get_barrier_semaphore()
-    ahead, behind = lax.rem(seq + 1, z.S), lax.rem(seq + z.S - 1, z.S)
-    partners = [(seq ^ other, mp) for other in range(1, z.S)] + [(ahead, mp), (behind, mp)]
-    partners += [(seq, lax.rem(mp + away, z.M)) for away in range(1, z.M)]
-    for partner in partners:
-        pl.semaphore_signal(barrier, inc=1, device_id=partner, device_id_type=MESH)
     pl.semaphore_wait(barrier, len(partners))
 
     def of_in(k):
@@ -1193,7 +1204,6 @@
     tree_o.settle(True)
     most = scatter_o.by_need()
     scatter_o.first(into(near_o, term_o))
-    scatter_o.second(onto(sum_o, term_o), send=True, masks=most[:1])
     tree_o.finish()
 
     def gated_grad(index):
@@ -1213,6 +1223,7 @@
             r.vec[6:7, lanes] += jnp.sum(d_read * r.u[rows, lanes].astype(F32), axis=0, keepdims=True)
 
     lane_loop(gate_back)
+    scatter_o.second(onto(sum_o, term_o), send=True, masks=most[:1])
 
     swap_out = Swap(z, links, lambda slot: r.orecv.at[slot])
 
@@ -1480,6 +1491,8 @@
         )
     step_back(1)
     project_back(1)
+    for step in range(depth - 1):
+        scatter_1.fold(step)
     sums_back(0)
     conv_back(0)
 
@@ -1506,10 +1519,6 @@
     each(z.Df // LANE, block_lanes)
     sums_back(1)
     conv_back(1)
-    for step in range(depth - 1):
-        scatter_1.fold(step)
-    x_back(0)
-    normed_part(0)
 
     def put_small(first, lanes, value):
         count, at = value.shape[0], 0
@@ -1535,7 +1544,7 @@
     for level in range(z.levels):
         pl.semaphore_wait(r.ready.at[level], 1)
     scatter_s.first(lambda device, mask: sgp.block(device))
-    x_back(1)
+    x_back(0)
 
     def add_small(device, mask):
         block, term = sum_s.block(mask // 2), sgp.block(device)
@@ -1546,10 +1555,14 @@
         by_rows(sg_rows, one)
 
     scatter_s.second(add_small, send=True)
+    normed_part(0)
+    for step in range(depth - 1):
+        scatter_s.fold(step)
+
+    x_back(1)
+
     scatter_0.first(into(near_i, term_0))
     scatter_0.second(onto(sum_0, term_0), send=True, masks=most[:1])
-    for step in range(depth - 1):
-        scatter_s.fold(step)
     scatter_0.second(onto(sum_0, term_0), send=True, masks=most[1:])
 
     normed_part(1)
@@ -1613,10 +1626,6 @@
 
     each(z.Df // LANE, token_lanes)
 
-    scatter_0.fold(last)
-    scatter_0.total(write_to(r.s))
-    store_0 = pltpu.make_async_copy(r.s.at[pl.ds(0, z.Ds)], r.din.at[0], local.at[4])
-    store_0.start()
     tree_s.finish()
     for block in range(z.S):
         count = min(sg_rows, r.sg.shape[0] - block * sg_rows)
@@ -1627,6 +1636,10 @@
     for slot in range(z.M - 1):
         gains = gains + r.gvm[slot]
     r.dgain[...] = gains
+    scatter_0.fold(last)
+    scatter_0.total(write_to(r.s))
+    store_0 = pltpu.make_async_copy(r.s.at[pl.ds(0, z.Ds)], r.din.at[0], local.at[4])
+    store_0.start()
 
     hal.wait_send()
     for tree in (tree_x, tree_z, tree_s):

time: 150 us -> 148 us (0.987)
  Pallas kernels: 149 us -> 147 us
    pallas_call x1, Pallas kernels: 144 us -> 142 us  [fused(): pl.pallas_call(functools.partial(fused_kernel, z, [*operands, *outs, *scr...]
where the time goes in v6:
time: 148 us
  Pallas kernels  147 us (99%)
    pallas_call x1, Pallas kernels, fused(): pl.pallas_call(functools.partial(fused_kernel, z, [*operands, *outs, *scr...  142 us
    pallas_call x1, Pallas kernels, fused(): pl.pallas_call(functools.partial(finish_kernel, z), out_shape=[jax.ShapeD...  4.98 us

profile of v6, /device:TPU:0, one launch (start us, length us, event | category | flops | bytes accessed | tf_op | source)
XLA Modules:
  0.0 147.9 jit_solution(6446454933485872339)
XLA Ops:
  0.6 142.3 %shard_map.229 = (bf16[256,512]{1,0:T(8,128)(2,1)}, f32[256,512]{1,0:T(8,128)}, f32[16,128]{1,0:T(8,128)}, f32[2,256,1024]{2,1,0:T(8,128)}, f32[1024,256]{1,0:T(8,128)}, /*index=5*/f32[304,1024]{1,0:T(8,128)}) custom-call(bf16[256,512]{1,0:T(8,128)(2,1)} %bitcast.15, f32[256,512]{1,0:T(8,128)} %bitcast.14, f32[1,2048]{1,0:T(1,128)} %bitcast.17, ...), custom_call_target="tpu_custom_call" | custom-call | tf_op jit(solution)/shard_map/pallas_call | solution.py:1719
  143.0 5.0 %shard_map.230 = (bf16[256,512]{1,0:T(8,128)(2,1)}, f32[256,512]{1,0:T(8,128)}, f32[16,128]{1,0:T(8,128)}, f32[2,256,1024]{2,1,0:T(8,128)}, f32[4,1024]{1,0:T(4,...) custom-call(bf16[256,512]{1,0:T(8,128)(2,1)} %get-tuple-element.30.b, ...), custom_call_target="tpu_custom_call" | custom-call | tf_op jit(solution)/shard_map/pallas_call | solution.py:1744

commit v7 on v6

--- a/solution.py
+++ b/solution.py
@@ -427,7 +427,7 @@
     def __init__(self, z, links, half_view, whole_view):
         self.z, self.links, self.half, self.whole = z, links, half_view, whole_view
         self.recv = {(mask, h): links.sem() for mask in z.masks[1:] for h in range(2)}
-        self.near = {mask: links.sem() for mask in z.masks}
+        self.near = {(mask, h): links.sem() for mask in z.masks for h in range(2)}
         self.sent = []
 
     def push(self, mask, h, dim):
@@ -441,9 +441,9 @@
     def take(self, mask, h):
         self.links.arrived(self.half(self.links.seq ^ mask, h), self.recv[mask, h])
 
-    def hand(self, mask):
-        view = self.whole(self.links.seq ^ mask)
-        copy = self.links.copy(view, view, self.links.sem(), self.near[mask], seq=self.links.seq ^ 1)
+    def hand(self, mask, h):
+        view = self.half(self.links.seq ^ mask, h)
+        copy = self.links.copy(view, view, self.links.sem(), self.near[mask, h], seq=self.links.seq ^ 1)
         copy.start()
         self.sent.append(copy)
 
@@ -454,14 +454,14 @@
     def second(self, h):
         for dim in self.z.order(h)[1:]:
             self.push(0, h, dim)
-        if h == 0:
-            self.hand(0)
+        self.hand(0, h)
 
     def forward(self, h):
         order = self.z.order(h)
         if len(order) > 1:
             self.take(order[0], h)
             self.push(order[0], h, order[1])
+            self.hand(order[0], h)
 
     def settle(self, far=None):
         for mask in sorted(self.z.masks[1:], key=lambda mask: bin(mask).count("1")):
@@ -471,11 +471,11 @@
                 order = self.z.order(h)
                 if len(order) == 1 or mask != order[0]:
                     self.take(mask, h)
-            self.hand(mask)
+                    self.hand(mask, h)
 
     def finish(self):
-        for mask in self.z.masks:
-            self.links.arrived(self.whole(self.links.seq ^ 1 ^ mask), self.near[mask])
+        for mask, h in self.near:
+            self.links.arrived(self.half(self.links.seq ^ 1 ^ mask, h), self.near[mask, h])
 
     def drain(self):
         for copy in self.sent:

time: 148 us -> 148 us (level)
  no operation moved by 1% of the time
where the time goes in v7:
time: 148 us
  Pallas kernels  147 us (99%)
    pallas_call x1, Pallas kernels, fused(): pl.pallas_call(functools.partial(fused_kernel, z, [*operands, *outs, *scr...  142 us
    pallas_call x1, Pallas kernels, fused(): pl.pallas_call(functools.partial(finish_kernel, z), out_shape=[jax.ShapeD...  4.98 us

profile of v7, /device:TPU:0, one launch (start us, length us, event | category | flops | bytes accessed | tf_op | source)
XLA Modules:
  0.0 148.1 jit_solution(15401376007496813933)
XLA Ops:
  0.6 142.4 %shard_map.229 = (bf16[256,512]{1,0:T(8,128)(2,1)}, f32[256,512]{1,0:T(8,128)}, f32[16,128]{1,0:T(8,128)}, f32[2,256,1024]{2,1,0:T(8,128)}, f32[1024,256]{1,0:T(8,128)}, /*index=5*/f32[304,1024]{1,0:T(8,128)}) custom-call(bf16[256,512]{1,0:T(8,128)(2,1)} %bitcast.15, f32[256,512]{1,0:T(8,128)} %bitcast.14, f32[1,2048]{1,0:T(1,128)} %bitcast.17, ...), custom_call_target="tpu_custom_call" | custom-call | tf_op jit(solution)/shard_map/pallas_call | solution.py:1719
  143.1 5.0 %shard_map.230 = (bf16[256,512]{1,0:T(8,128)(2,1)}, f32[256,512]{1,0:T(8,128)}, f32[16,128]{1,0:T(8,128)}, f32[2,256,1024]{2,1,0:T(8,128)}, f32[4,1024]{1,0:T(4,...) custom-call(bf16[256,512]{1,0:T(8,128)(2,1)} %get-tuple-element.30.b, ...), custom_call_target="tpu_custom_call" | custom-call | tf_op jit(solution)/shard_map/pallas_call | solution.py:1744
